TPU v7x, 512 devices: a whole 4x4x16 slice. The times are simulated.
512 devices in a mesh: expert: 128 (over y, z, core), dp: 4 (over x).
Axes of the slice: x: 4, y: 4, z: 16, core: 2. Of those that a mesh axis runs over, the one named last changes fastest.
Arguments:
- tokens: bfloat16 [65536, 2048], P(('expert', 'dp')), may hold values from -6 to 6
- cotangent: bfloat16 [65536, 8, 384], P(('expert', 'dp')), may hold values from -3 to 3
- routes: int32 [65536, 8], P(('expert', 'dp')), may hold values from 0 to 127, all different within a row
- route_weight: float32 [65536, 8], P(('expert', 'dp')), may hold values from 0.05 to 1
- expert_slot: int32 [128], replicated, may hold values from 0 to 127, each once
- capacity: int32 [128], replicated, may hold values from 2 to 6, as said below
- gate_up: bfloat16 [128, 2048, 768], P('expert', 'dp'), may hold values from -0.125 to 0.125
Outputs:
- token_grad: bfloat16 [65536, 2048], P(('expert', 'dp'))
- route_weight_grad: float32 [65536, 8], P(('expert', 'dp'))
- gate_up_grad: bfloat16 [128, 2048, 768], P('expert', 'dp')
Inputs may be any that keep to these rules, and one draw needn't show every extreme that they name: Every capacity is even; capacity[d] + capacity[(d + 64) mod 128] <= 8 for every slot d; some slot has exactly 6.
All inputs are finite; a program needn't handle non-finite values.
Results may differ from a plain program's by a relative error of at most 0.02.
Values may be sent and summed in bfloat16 or wider, within the bound.
No kernel may reach another device: no remote copies, remote signals or barrier semaphores. Data moves between devices by JAX's collectives and lax.ppermute only.
A program may use at most 64 MiB of HBM per device.

v0:
```python
import jax
import jax.numpy as jnp
from jax import lax
from jax.sharding import PartitionSpec as P

CAP = 6


def swapped(value, axis, apart):
    mask = 2**apart
    pairs = [(source, source ^ mask) for source in range(lax.axis_size(axis))]
    return lax.ppermute(value, axis, pairs)


def swiglu_grads(pre_act, cot_float, weight_rows, hidden_width):
    gate_part = pre_act[:, :hidden_width]
    up_part = pre_act[:, hidden_width:]
    sigmoid_gate = jax.nn.sigmoid(gate_part)
    active = gate_part * sigmoid_gate
    hidden = active * up_part
    scaled = weight_rows[:, None] * cot_float
    grad_up = scaled * active
    grad_gate = scaled * up_part * sigmoid_gate * (1.0 + gate_part * (1.0 - sigmoid_gate))
    packed = jnp.concatenate([grad_gate, grad_up], axis=1).astype(jnp.bfloat16)
    return (packed, jnp.sum(hidden * cot_float, axis=1))


def serve_column(rows_column, cot_column, weight_column, matrix, hidden_width):
    pre_act = jnp.dot(rows_column, matrix, preferred_element_type=jnp.float32)
    row_grad, router_rows = swiglu_grads(pre_act, cot_column, weight_column, hidden_width)
    input_column = jnp.einsum("rf,df->rd", row_grad, matrix, preferred_element_type=jnp.float32)
    return (row_grad, router_rows, input_column.astype(jnp.bfloat16))


def local(tokens, cotangent, routes, route_weight, expert_slot, capacity, gate_up):
    axis_count = lax.axis_size("expert")
    half_axis = axis_count // 2
    swap_bit = axis_count.bit_length() - 2
    token_rows = tokens.shape[0]
    model_width = tokens.shape[1]
    route_count = routes.shape[1]
    hidden_width = cotangent.shape[2]
    flat_routes = routes.reshape(-1)
    expert_ids = jnp.arange(axis_count, dtype=jnp.int32)
    onehot_expert = (flat_routes[:, None] == expert_ids[None, :]).astype(jnp.int32)
    route_slot = jnp.sum(onehot_expert * expert_slot[None, :], axis=1)
    earlier = jnp.cumsum(onehot_expert, axis=0) - onehot_expert
    route_rank = jnp.sum(earlier * onehot_expert, axis=1)
    onehot_slot = (route_slot[:, None] == expert_ids[None, :]).astype(jnp.int32)
    slot_capacity = jnp.sum(onehot_slot * capacity[None, :], axis=1)
    is_kept = route_rank < slot_capacity
    slot_depth = (CAP + 2) // 2
    facing_capacity = jnp.sum(onehot_slot * jnp.roll(capacity, -half_axis)[None, :], axis=1)
    is_odd = route_rank % 2 == 1
    target_dev = jnp.where(is_odd, (route_slot + half_axis) % axis_count, route_slot)
    slot_place = jnp.where(is_odd, facing_capacity // 2, 0) + route_rank // 2
    buffer_rows = axis_count * slot_depth
    target = jnp.where(is_kept, target_dev * slot_depth + slot_place, buffer_rows)
    route_inputs = jnp.repeat(tokens, route_count, axis=0)
    send_rows = (
        jnp.zeros((buffer_rows, model_width), jnp.bfloat16)
        .at[target]
        .set(route_inputs, mode="drop")
    )
    send_cot = (
        jnp.zeros((buffer_rows, hidden_width), jnp.bfloat16)
        .at[target]
        .set(cotangent.reshape(-1, hidden_width), mode="drop")
    )
    send_weight = (
        jnp.zeros((buffer_rows,), jnp.float32).at[target].set(route_weight.reshape(-1), mode="drop")
    )
    recv_rows, recv_cot, recv_weight = (
        lax.all_to_all(
            send_rows.reshape(axis_count, slot_depth, model_width),
            "expert",
            split_axis=0,
            concat_axis=0,
            tiled=True,
        ),
        lax.all_to_all(
            send_cot.reshape(axis_count, slot_depth, hidden_width),
            "expert",
            split_axis=0,
            concat_axis=0,
            tiled=True,
        ),
        lax.all_to_all(
            send_weight.reshape(axis_count, slot_depth).astype(jnp.bfloat16),
            "expert",
            split_axis=0,
            concat_axis=0,
            tiled=True,
        ).astype(jnp.float32),
    )
    weight = lax.all_gather(gate_up, "dp", axis=1, tiled=True)[0]
    my_index = lax.axis_index("expert")
    my_capacity = jnp.sum(jnp.where(expert_ids == my_index, capacity, 0))
    own_count = my_capacity // 2
    partner = swapped(weight, "expert", swap_bit)
    grad_columns = []
    input_columns = []
    router_columns = []
    for column in range(slot_depth):
        is_own = column < own_count
        rows_column = recv_rows[:, column]
        cot_column = recv_cot[:, column].astype(jnp.float32)
        weight_column = recv_weight[:, column]
        row_grad, router_rows, input_column = lax.cond(
            is_own,
            lambda: serve_column(rows_column, cot_column, weight_column, weight, hidden_width),
            lambda: serve_column(rows_column, cot_column, weight_column, partner, hidden_width),
        )
        grad_columns.append(row_grad)
        input_columns.append(input_column)
        router_columns.append(router_rows)
    input_three = jnp.stack(input_columns, axis=1)
    router_two = jnp.stack(router_columns, axis=1)
    grad_three = jnp.stack(grad_columns, axis=1)
    column_ids = jnp.arange(slot_depth, dtype=jnp.int32)
    own_mask = (column_ids < own_count)[None, :, None]
    zero_grad = jnp.zeros_like(grad_three)
    own_grad = jnp.where(own_mask, grad_three, zero_grad).reshape(-1, 2 * hidden_width)
    far_grad = jnp.where(own_mask, zero_grad, grad_three).reshape(-1, 2 * hidden_width)
    flat_rows = recv_rows.reshape(-1, model_width)
    part_own = jnp.einsum("rd,rf->df", flat_rows, own_grad, preferred_element_type=jnp.float32)
    part_far = jnp.einsum("rd,rf->df", flat_rows, far_grad, preferred_element_type=jnp.float32)
    own_rounded = part_own.astype(jnp.bfloat16)
    part_back = swapped(part_far.astype(jnp.bfloat16), "expert", swap_bit)
    local_grad = own_rounded.astype(jnp.float32) + part_back.astype(jnp.float32)
    rounded_grad = lax.optimization_barrier(local_grad.astype(jnp.bfloat16)).astype(jnp.float32)
    summed_grad = lax.psum_scatter(
        rounded_grad.astype(jnp.bfloat16), "dp", scatter_dimension=0, tiled=True
    )
    gate_up_grad = summed_grad[None]
    back_rows, back_router = (
        lax.all_to_all(input_three, "expert", split_axis=0, concat_axis=0, tiled=True),
        lax.all_to_all(
            router_two.astype(jnp.bfloat16), "expert", split_axis=0, concat_axis=0, tiled=True
        ).astype(router_two.dtype),
    )
    route_input = jnp.take(
        back_rows.reshape(buffer_rows, model_width), target, axis=0, mode="fill", fill_value=0
    )
    token_grad = jnp.sum(
        route_input.reshape(token_rows, route_count, model_width).astype(jnp.float32), axis=1
    ).astype(jnp.bfloat16)
    route_weight_grad = jnp.take(
        back_router.reshape(buffer_rows), target, axis=0, mode="fill", fill_value=0
    ).reshape(token_rows, route_count)
    return (token_grad, route_weight_grad, gate_up_grad)


def solution(mesh):
    in_specs = (
        P(("expert", "dp"), None),
        P(("expert", "dp"), None, None),
        P(("expert", "dp"), None),
        P(("expert", "dp"), None),
        P(),
        P(),
        P("expert", "dp", None),
    )
    out_specs = (P(("expert", "dp"), None), P(("expert", "dp"), None), P("expert", "dp", None))
    return jax.shard_map(local, mesh=mesh, in_specs=in_specs, out_specs=out_specs, check_vma=False)
```

profile of v0, /device:TPU:1, one launch (start us, length us, event | category | flops | bytes accessed | tf_op | source)
XLA Modules:
  0.0 488.5 jit_solution(3356568539496384129)
XLA Ops:
  7.2 0.9 copy.99
  11.6 4.3 scatter_custom_fusion.2
  16.7 20.6 %all-to-all-start.2 = ((bf16[128,1,4]{2,1,0:T(2,128)(2,1)}), bf16[128,1,4]{2,1,0:T(2,128)(2,1)S(1)}, u32[]{:S(2)}, u32[]{:S(2)}) async-start(bf16[128,1,4]{2,1,0:T(2,128)(2,1)} %convert_element_type.220), calls=%async_computation.2 | async-start | bytes 131072 | tf_op jit(solution)/shard_map/all_to_all | solution.py:88
  37.3 5.1 %scatter_custom_fusion.1 = bf16[512,384]{1,0:T(8,128)(2,1)S(1)} fusion(s32[1024]{0:T(1024)S(1)} %bitcast.167, bf16[128,8,384]{2,1,0:T(8,128)(2,1)S(1)} %copy-done, bf16[]{:T(256)} %constant.149.clone.1), kind=kCustom, calls=%fused_computation.135 | custom fusion | bytes 1179650 | tf_op jit(solution)/shard_map/scatter | solution.py:68
  43.2 9.1 %all-to-all-done.2 = bf16[128,1,4]{2,1,0:T(2,128)(2,1)S(1)} async-done(((bf16[128,1,4]{2,1,0:T(2,128)(2,1)}), bf16[128,1,4]{2,1,0:T(2,128)(2,1)S(1)}, u32[]{:S(2)}, u32[]{:S(2)}) %all-to-all-start.2) | async-done | bytes 1056 | tf_op jit(solution)/shard_map/all_to_all | solution.py:88
  52.3 7.7 %all-to-all-start.1 = ((bf16[128,4,384]{2,1,0:T(4,128)(2,1)}), bf16[128,4,384]{2,1,0:T(4,128)(2,1)S(1)}, u32[]{:S(2)}, u32[]{:S(2)}) async-start(bf16[128,4,384]{2,1,0:T(4,128)(2,1)} %reshape.447), calls=%async_computation.1 | async-start | bytes 786432 | tf_op jit(solution)/shard_map/all_to_all | solution.py:81
  60.0 7.5 %scatter_custom_fusion = bf16[512,2048]{1,0:T(8,128)(2,1)S(1)} fusion(s32[1024]{0:T(1024)S(1)} %bitcast.168, bf16[128,2048]{1,0:T(8,128)(2,1)} %param.15, bf16[]{:T(256)} %constant.149.clone.1), kind=kCustom, calls=%fused_computation.130 | custom fusion | bytes 2621442 | tf_op jit(solution)/shard_map/scatter | solution.py:63
  67.5 2.3 reshape.445
  69.7 18.0 %all-to-all-done.1 = bf16[128,4,384]{2,1,0:T(4,128)(2,1)S(1)} async-done(((bf16[128,4,384]{2,1,0:T(4,128)(2,1)}), bf16[128,4,384]{2,1,0:T(4,128)(2,1)S(1)}, u32[]{:S(2)}, u32[]{:S(2)}) %all-to-all-start.1) | async-done | bytes 393248 | tf_op jit(solution)/shard_map/all_to_all | solution.py:81
  87.7 7.2 %all-to-all-start = ((bf16[128,4,2048]{2,1,0:T(4,128)(2,1)}), bf16[128,4,2048]{2,1,0:T(4,128)(2,1)S(1)}, u32[]{:S(2)}, u32[]{:S(2)}) async-start(bf16[128,4,2048]{2,1,0:T(4,128)(2,1)} %reshape.445), calls=%async_computation | async-start | bytes 4194304 | tf_op jit(solution)/shard_map/all_to_all | solution.py:74
  95.7 50.5 %all-gather.2.cloned.1.call-done = bf16[1,2048,768]{2,1,0:T(8,128)(2,1)} async-done(((bf16[1,512,768]{2,1,0:T(8,128)(2,1)}), bf16[1,2048,768]{2,1,0:T(8,128)(2,1)}) %all-gather.2.cloned.1.call-update) | async-done | bytes 3145744 | tf_op jit(solution)/shard_map/all_gather | solution.py:96
  146.2 4.6 collective-permute-start
  156.7 37.5 %all-to-all-done = bf16[128,4,2048]{2,1,0:T(4,128)(2,1)S(1)} async-done(((bf16[128,4,2048]{2,1,0:T(4,128)(2,1)}), bf16[128,4,2048]{2,1,0:T(4,128)(2,1)S(1)}, u32[]{:S(2)}, u32[]{:S(2)}) %all-to-all-start) | async-done | bytes 2097184 | tf_op jit(solution)/shard_map/all_to_all | solution.py:74
  194.2 4.1 fusion.104
  198.3 1.6 copy_bitcast_fusion.2
  199.8 28.6 %collective-permute-done = bf16[2048,768]{1,0:T(8,128)(2,1)} collective-permute-done((bf16[2048,768]{1,0:T(8,128)(2,1)}, bf16[2048,768]{1,0:T(8,128)(2,1)}, u32[]{:S(2)}, u32[]{:S(2)}) %collective-permute-start) | collective-permute-done | bytes 3145760 | tf_op jit(solution)/shard_map/ppermute | solution.py:12
  228.4 7.9 %conditional.12 = (bf16[128,1,1]{0,2,1:T(2,128)(2,1)}, bf16[128,1,768]{2,0,1:T(8,128)(2,1)}, bf16[128,1,2048]{2,1,0:T(2,128)(2,1)S(1)}) conditional(s32[]{:T(128)} %convert_element_type.179, (bf16[128,2048]{1,0:T(8,128)(2,1)}, bf16[2048,768]{1,0:T(8,128)(2,1)}, f32[128,384]{1,0:T(8,128)}, f32[128,1]{1,0:T(8,128)}) %tuple.96, ...), branch_computations={%region_10.12_spmd, %region_12.14_spmd} | conditional | flops 807534464 | bytes 24220012
  228.6 1.4 copy.107
  230.0 2.8 fusion.108
  234.3 1.1 fusion.8
  236.3 1.8 constant_dynamic-update-slice_fusion.3
  238.1 3.1 copy_bitcast_fusion
  241.2 9.5 %conditional.13 = (bf16[128,1,1]{0,2,1:T(2,128)(2,1)}, bf16[128,1,768]{2,0,1:T(8,128)(2,1)}, bf16[128,1,2048]{2,1,0:T(2,128)(2,1)S(1)}) conditional(s32[]{:T(128)} %convert_element_type.186, (bf16[128,2048]{1,0:T(8,128)(2,1)}, bf16[2048,768]{1,0:T(8,128)(2,1)}, f32[128,384]{1,0:T(8,128)S(1)}, f32[128,1]{1,0:T(8,128)}) %tuple.98, ...), branch_computations={%region_14.16_spmd, %region_16.18_spmd} | conditional | flops 807534464 | bytes 23433552
  241.2 1.4 copy.109
  242.7 2.6 fusion.109
  246.8 3.0 fusion.16
  250.7 1.9 constant_dynamic-update-slice_fusion.2
  252.6 8.3 %conditional.14 = (bf16[128,1,1]{0,2,1:T(2,128)(2,1)}, bf16[128,1,768]{2,0,1:T(8,128)(2,1)S(1)}, bf16[128,1,2048]{2,1,0:T(2,128)(2,1)S(1)}) conditional(s32[]{:T(128)} %convert_element_type.189, (bf16[128,2048]{1,0:T(8,128)(2,1)}, bf16[2048,768]{1,0:T(8,128)(2,1)}, f32[128,384]{1,0:T(8,128)S(1)}, f32[128,1]{1,0:T(8,128)}) %tuple.100, ...), branch_computations={%region_18.20_spmd, %region_20.22_spmd} | conditional | flops 807534464 | bytes 23431476
  252.6 0.9 copy.112
  253.5 2.7 fusion.111
  257.0 3.0 fusion.32
  261.9 8.1 %conditional.15 = (bf16[128,1,1]{0,2,1:T(2,128)(2,1)S(1)}, bf16[128,1,768]{2,0,1:T(8,128)(2,1)S(1)}, bf16[128,1,2048]{2,1,0:T(2,128)(2,1)}) conditional(s32[]{:T(128)} %convert_element_type.192, (bf16[128,2048]{1,0:T(8,128)(2,1)}, bf16[2048,768]{1,0:T(8,128)(2,1)}, f32[128,384]{1,0:T(8,128)S(1)}, f32[128,1]{1,0:T(8,128)S(1)}) %tuple.102, ...), branch_computations={%region_22.24_spmd, %region_24.26_spmd} | conditional | flops 807534464 | bytes 23431476
  262.2 2.7 fusion.113
  265.2 3.0 fusion.48
  268.2 1.8 copy.131
  270.7 3.1 copy.122
  273.8 5.5 %bitcast_convert_fusion = bf16[2048,768]{1,0:T(8,128)(2,1)} fusion(bf16[128,4,2048]{0,2,1:T(8,128)(2,1)} %copy.122, bf16[128,4,768]{2,0,1:T(8,128)(2,1)} %constant_dynamic-update-slice_fusion, pred[4]{0:T(512)(128)(4,1)S(1)} %copy-done.21), kind=kOutput, calls=%fused_computation.125 | convolution fusion | flops 1612578816 | bytes 6029316 | tf_op jit(solution)/shard_map/rd,rf->df/dot_general | solution.py:127
  279.3 1.9 collective-permute-start.1
  282.6 17.2 %all-to-all-start.4 = ((bf16[128,1,4]{2,1,0:T(2,128)(2,1)}), bf16[128,1,4]{2,1,0:T(2,128)(2,1)S(1)}, u32[]{:S(2)}, u32[]{:S(2)}) async-start(bf16[128,1,4]{2,1,0:T(2,128)(2,1)} %copy.121), calls=%async_computation.4 | async-start | bytes 131072 | tf_op jit(solution)/shard_map/all_to_all | solution.py:138
  299.9 7.1 %pad_maximum_fusion = bf16[128,4,2048]{2,1,0:T(4,128)(2,1)} fusion(bf16[128,1,2048]{2,1,0:T(2,128)(2,1)} %get-tuple-element.354, bf16[128,1,2048]{2,1,0:T(2,128)(2,1)} %copy-done.11, bf16[128,1,2048]{2,1,0:T(2,128)(2,1)S(1)} %copy-done.10, bf16[128,1,2048]{2,1,0:T(2,128)(2,1)S(1)} %copy-done.8), kind=kLoop, calls=%fused_computation.132 | loop fusion | flops 8388608 | bytes 4194304 | tf_op jit(solution)/shard_map/stack | solution.py:117
  306.9 46.8 %all-to-all-done.4 = bf16[128,1,4]{2,1,0:T(2,128)(2,1)S(1)} async-done(((bf16[128,1,4]{2,1,0:T(2,128)(2,1)}), bf16[128,1,4]{2,1,0:T(2,128)(2,1)S(1)}, u32[]{:S(2)}, u32[]{:S(2)}) %all-to-all-start.4) | async-done | bytes 1056 | tf_op jit(solution)/shard_map/all_to_all | solution.py:138
  353.8 15.0 %all-to-all-start.3 = ((bf16[128,4,2048]{2,1,0:T(4,128)(2,1)}), bf16[128,4,2048]{2,1,0:T(4,128)(2,1)}, u32[]{:S(2)}, u32[]{:S(2)}) async-start(bf16[128,4,2048]{2,1,0:T(4,128)(2,1)} %pad_maximum_fusion), calls=%async_computation.3 | async-start | bytes 4194304 | tf_op jit(solution)/shard_map/all_to_all | solution.py:137
  368.9 4.9 %add_convert_fusion = bf16[2048,768]{1,0:T(8,128)(2,1)} fusion(bf16[2048,768]{1,0:T(8,128)(2,1)} %collective-permute-done.1, bf16[128,4,2048]{0,2,1:T(8,128)(2,1)S(1)} %copy-done.12, bf16[128,4,768]{2,0,1:T(8,128)(2,1)} %constant_dynamic-update-slice_fusion, pred[4]{0:T(512)(128)(4,1)S(1)} %copy-done.21), kind=kOutput, calls=%fused_computation.127 | convolution fusion | flops 1618870272 | bytes 9175044 | tf_op jit(solution)/shard_map/rd,rf->df/dot_general | solution.py:126
  374.8 6.9 %gather_fusion.1 = f32[1024]{0:T(1024)S(1)} fusion(f32[512]{0:T(512)S(1)} %reshape.463, s32[1024]{0:T(1024)S(1)} %broadcast_clamp_fusion), kind=kCustom, calls=%fused_computation.1 | custom fusion | bytes 12288 | tf_op jit(solution)/shard_map/jit(_take)/gather | solution.py:148
  382.6 85.0 %all-to-all-done.3 = bf16[128,4,2048]{2,1,0:T(4,128)(2,1)} async-done(((bf16[128,4,2048]{2,1,0:T(4,128)(2,1)}), bf16[128,4,2048]{2,1,0:T(4,128)(2,1)}, u32[]{:S(2)}, u32[]{:S(2)}) %all-to-all-start.3) | async-done | bytes 2097184 | tf_op jit(solution)/shard_map/all_to_all | solution.py:137
  467.6 2.5 reshape.449
  470.1 6.0 %gather_fusion = bf16[1024,2048]{1,0:T(8,128)(2,1)} fusion(bf16[512,2048]{1,0:T(8,128)(2,1)S(1)} %reshape.449, s32[1024]{0:T(1024)S(1)} %broadcast_clamp_fusion), kind=kCustom, calls=%fused_computation | custom fusion | bytes 8392704 | tf_op jit(solution)/shard_map/jit(_take)/gather | solution.py:142
  476.1 5.1 %fusion.64 = bf16[128,2048]{1,0:T(8,128)(2,1)} fusion(bf16[1024,2048]{1,0:T(8,128)(2,1)} %gather_fusion, pred[128,8]{1,0:T(8,128)(4,1)S(1)} %get-tuple-element.360), kind=kLoop, calls=%fused_computation.129 | loop fusion | flops 3932160 | bytes 4719616 | tf_op jit(solution)/shard_map/reduce_sum | solution.py:145
  (94 shorter events, 20.9 us)
Async XLA Ops:
  7.2 30.1 %copy-start = (bf16[128,8,384]{2,1,0:T(8,128)(2,1)S(1)}, bf16[128,8,384]{2,1,0:T(8,128)(2,1)}, u32[]{:S(2)}) copy-start(bf16[128,8,384]{2,1,0:T(8,128)(2,1)} %param.16) | copy-start | bytes 2359300
  7.2 3.9 copy-start.15
  7.2 3.3 copy-start.20
  11.6 58.1 %copy-start.13 = (s32[1024,1]{0,1:T(1,128)}, s32[1024,1]{0,1:T(1,128)S(1)}, u32[]{:S(2)}) copy-start(s32[1024,1]{0,1:T(1,128)S(1)} %compare_select_fusion.1) | copy-start | bytes 12292
  16.7 35.5 %all-to-all-start.2 = ((bf16[128,1,4]{2,1,0:T(2,128)(2,1)}), bf16[128,1,4]{2,1,0:T(2,128)(2,1)S(1)}, u32[]{:S(2)}, u32[]{:S(2)}) async-start(bf16[128,1,4]{2,1,0:T(2,128)(2,1)} %convert_element_type.220), calls=%async_computation.2 | async-start | bytes 131072 | tf_op jit(solution)/shard_map/all_to_all | solution.py:88
  52.3 35.5 %all-to-all-start.1 = ((bf16[128,4,384]{2,1,0:T(4,128)(2,1)}), bf16[128,4,384]{2,1,0:T(4,128)(2,1)S(1)}, u32[]{:S(2)}, u32[]{:S(2)}) async-start(bf16[128,4,384]{2,1,0:T(4,128)(2,1)} %reshape.447), calls=%async_computation.1 | async-start | bytes 786432 | tf_op jit(solution)/shard_map/all_to_all | solution.py:81
  87.7 106.5 %all-to-all-start = ((bf16[128,4,2048]{2,1,0:T(4,128)(2,1)}), bf16[128,4,2048]{2,1,0:T(4,128)(2,1)S(1)}, u32[]{:S(2)}, u32[]{:S(2)}) async-start(bf16[128,4,2048]{2,1,0:T(4,128)(2,1)} %reshape.445), calls=%async_computation | async-start | bytes 4194304 | tf_op jit(solution)/shard_map/all_to_all | solution.py:74
  95.0 51.2 %all-gather.2.cloned.1.call-start = ((), (), s32[]{:S(2)}) async-start(), calls=%async_computation.6 | async-start | bytes 3932160 | tf_op jit(solution)/shard_map/all_gather | solution.py:96
  146.2 82.2 %collective-permute-start = (bf16[2048,768]{1,0:T(8,128)(2,1)}, bf16[2048,768]{1,0:T(8,128)(2,1)}, u32[]{:S(2)}, u32[]{:S(2)}) collective-permute-start(bf16[2048,768]{1,0:T(8,128)(2,1)} %bitcast.148), channel_id=1, source_target_pairs={{0,256},{4,260},{8,264},{12,268},{16,272},{20,276},{24,280},{28,28... | collective-permute-start | bytes 9437192 | tf_op jit(solution)/shard_map/ppermute | solution.py:12
  230.0 2.8 copy-start.6
  230.0 2.8 copy-start.17
  230.0 4.3 copy-start.1
  236.3 4.9 %copy-start.7 = (bf16[128,1,2048]{2,1,0:T(2,128)(2,1)}, bf16[128,1,2048]{2,1,0:T(2,128)(2,1)S(1)}, u32[]{:S(2)}) copy-start(bf16[128,1,2048]{2,1,0:T(2,128)(2,1)S(1)} %get-tuple-element.351) | copy-start | bytes 1572868
  242.7 2.6 copy-start.18
  250.7 1.9 copy-start.9
  260.9 1.0 copy-start.11
  270.0 3.7 copy-start.21
  273.8 26.1 %copy-start.8 = (bf16[128,1,2048]{2,1,0:T(2,128)(2,1)S(1)}, bf16[128,1,2048]{2,1,0:T(2,128)(2,1)}, u32[]{:S(2)}) copy-start(bf16[128,1,2048]{2,1,0:T(2,128)(2,1)} %copy-done.7) | copy-start | bytes 1572868
  273.8 26.1 %copy-start.10 = (bf16[128,1,2048]{2,1,0:T(2,128)(2,1)S(1)}, bf16[128,1,2048]{2,1,0:T(2,128)(2,1)}, u32[]{:S(2)}) copy-start(bf16[128,1,2048]{2,1,0:T(2,128)(2,1)} %copy-done.9) | copy-start | bytes 1572868
  279.3 89.6 %collective-permute-start.1 = (bf16[2048,768]{1,0:T(8,128)(2,1)}, bf16[2048,768]{1,0:T(8,128)(2,1)}, u32[]{:S(2)}, u32[]{:S(2)}) collective-permute-start(bf16[2048,768]{1,0:T(8,128)(2,1)} %bitcast_convert_fusion), channel_id=1, source_target_pairs={{0,256},{4,260},{8,264},{12,268},{16,272},{20,276},{24,280},{28,28... | collective-permute-start | bytes 9437192 | tf_op jit(solution)/shard_map/ppermute | solution.py:12
  282.6 71.1 %all-to-all-start.4 = ((bf16[128,1,4]{2,1,0:T(2,128)(2,1)}), bf16[128,1,4]{2,1,0:T(2,128)(2,1)S(1)}, u32[]{:S(2)}, u32[]{:S(2)}) async-start(bf16[128,1,4]{2,1,0:T(2,128)(2,1)} %copy.121), calls=%async_computation.4 | async-start | bytes 131072 | tf_op jit(solution)/shard_map/all_to_all | solution.py:138
  306.9 61.9 %copy-start.12 = (bf16[128,4,2048]{0,2,1:T(8,128)(2,1)S(1)}, bf16[128,4,2048]{0,2,1:T(8,128)(2,1)}, u32[]{:S(2)}) copy-start(bf16[128,4,2048]{0,2,1:T(8,128)(2,1)} %copy.122) | copy-start | bytes 6291460
  353.8 113.8 %all-to-all-start.3 = ((bf16[128,4,2048]{2,1,0:T(4,128)(2,1)}), bf16[128,4,2048]{2,1,0:T(4,128)(2,1)}, u32[]{:S(2)}, u32[]{:S(2)}) async-start(bf16[128,4,2048]{2,1,0:T(4,128)(2,1)} %pad_maximum_fusion), calls=%async_computation.3 | async-start | bytes 4194304 | tf_op jit(solution)/shard_map/all_to_all | solution.py:137
  368.8 112.5 %reduce-scatter.2.cloned.1.call-start = ((), (), s32[]{:S(2)}) async-start(), calls=%async_computation.7 | async-start | bytes 3932160 | tf_op jit(solution)/shard_map/reduce_scatter | solution.py:132
  373.8 0.7 copy-start.14
Sparse Core Ops, SparseCore 0:
  97.9 48.2 all-gather.1
  374.0 46.4 reduce-scatter.1
where the time goes:
time: 496 us; the launch traced here: 489 us
  waiting for transfers between devices  276 us (56%)
  starting transfers between devices  74.3 us (15%)
  local copies, waits for them, and re-layouts  68.1 us (14%)
  matrix products  31.4 us (6%)
  other arithmetic  20.6 us (4%)
  between operations  17.5 us (4%)
    all_to_all x1, waiting for transfers between devices, local(): lax.all_to_all(input_three, 'expert', split_axis=0, concat_axis=0, tiled=...  85 us
    all_gather x1, waiting for transfers between devices, local(): weight = lax.all_gather(gate_up, 'dp', axis=1, tiled=True)[0]  50.5 us
    all_to_all x1, waiting for transfers between devices, local(): lax.all_to_all(router_two.astype(jnp.bfloat16), 'expert', split_axis=0, c...  46.8 us
    all_to_all x1, waiting for transfers between devices, local(): lax.all_to_all(send_rows.reshape(axis_count, slot_depth, model_width), 'e...  37.5 us
    ppermute x2, waiting for transfers between devices, swapped(): return lax.ppermute(value, axis, pairs)  28.6 us
    all_to_all x1, starting transfers between devices, local(): lax.all_to_all(send_weight.reshape(axis_count, slot_depth).astype(jnp.bfl...  20.6 us
    all_to_all x1, waiting for transfers between devices, local(): lax.all_to_all(send_cot.reshape(axis_count, slot_depth, hidden_width), 'e...  18 us
    all_to_all x1, starting transfers between devices, local(): lax.all_to_all(router_two.astype(jnp.bfloat16), 'expert', split_axis=0, c...  17.2 us
  transfers between devices with their start and end apart: 9, of which 7 were waited for; matrix products, arithmetic and copies ran while one was open for 12% of the time, Pallas kernels for 0%

commit v1 on v0

v1 whole, which is shorter than its diff:
```python
import jax
import jax.numpy as jnp
from jax import lax
from jax.experimental import pallas as pl
from jax.experimental.pallas import tpu as pltpu
from jax.sharding import PartitionSpec as P

BF = jnp.bfloat16
F32 = jnp.float32
VMEM_BYTES = 48 * 1024 * 1024
TAIL = 128


def params():
    return pltpu.CompilerParams(vmem_limit_bytes=VMEM_BYTES)


def whole():
    return pl.BlockSpec(memory_space=pltpu.VMEM)


def scalars():
    return pl.BlockSpec(memory_space=pltpu.SMEM)


def iota(shape, dim):
    return lax.broadcasted_iota(jnp.int32, shape, dim)


def mm(a, b, ca=1, cb=0):
    return lax.dot_general(a, b, (((ca,), (cb,)), ((), ())), preferred_element_type=F32)


def token_of_route(routes, tokens, top):
    return ((iota((routes, tokens), 0) // top) == iota((routes, tokens), 1)).astype(BF)


def gather_rows(target, weight, tokens, cot, top, out_ref):
    rows = out_ref.shape[0]
    routes = target.shape[1]
    width = tokens.shape[1]
    hit = iota((rows, routes), 0) == target
    by_token = mm(hit.astype(BF), token_of_route(routes, tokens.shape[0], top)).astype(BF)
    out_ref[:, :width] = mm(by_token, tokens[...]).astype(BF)
    out_ref[:, width:] = mm(jnp.where(hit, weight, 0.0).astype(BF), cot[...]).astype(BF)


def pack_first(routes_ref, weight_ref, slot_ref, cap_ref, tokens_ref, cot_ref, out_ref, target_ref):
    experts = slot_ref.shape[1]
    routes = routes_ref.shape[1]
    tokens = tokens_ref.shape[0]
    top = routes // tokens
    named = iota((experts, routes), 0) == routes_ref[...]
    owner = token_of_route(routes, tokens, top)
    chosen = mm(named.astype(BF), owner)
    before = (iota((tokens, tokens), 0) < iota((tokens, tokens), 1)).astype(BF)
    earlier = mm(mm(chosen.astype(BF), before).astype(BF), owner, 1, 1)
    rank = jnp.sum(jnp.where(named, earlier, 0.0), axis=0, keepdims=True).astype(jnp.int32)
    square = (experts, experts)
    slot_col = jnp.sum(
        jnp.where(iota(square, 0) == iota(square, 1), slot_ref[...], 0), axis=1, keepdims=True
    )
    cap_col = jnp.sum(
        jnp.where(iota(square, 1) == slot_col, cap_ref[...], 0), axis=1, keepdims=True
    )
    slot = jnp.sum(jnp.where(named, slot_col, 0), axis=0, keepdims=True)
    cap = jnp.sum(jnp.where(named, cap_col, 0), axis=0, keepdims=True)
    kept = rank < cap
    far = rank >= 4
    place = jnp.where(far, 7 - rank, rank)
    half = experts // 2
    dest = jnp.where(far, jnp.where(slot >= half, slot - half, slot + half), slot)
    outer = jnp.where(kept & (place >= 2), dest * 2 + place - 2, -1)
    inner = jnp.where(kept & (place < 2), dest * 2 + place, -1)
    target_ref[0:1, :] = outer
    target_ref[1:2, :] = inner
    gather_rows(outer, weight_ref[...], tokens_ref, cot_ref, top, out_ref)


def pack_second(target_ref, weight_ref, tokens_ref, cot_ref, out_ref):
    top = target_ref.shape[1] // tokens_ref.shape[0]
    gather_rows(target_ref[1:2, :], weight_ref[...], tokens_ref, cot_ref, top, out_ref)


def serve(rows_ref, valid, weights_ref):
    width = weights_ref.shape[0]
    hidden = weights_ref.shape[1] // 2
    pre = mm(rows_ref[:, :width], weights_ref[...])
    scaled = rows_ref[:, width:].astype(F32)
    if valid is not None:
        scaled = jnp.where(valid, scaled, 0.0)
    gate = pre[:, :hidden]
    up = pre[:, hidden:]
    sig = jax.nn.sigmoid(gate)
    active = gate * sig
    grad_up = scaled * active
    grad_gate = scaled * up * sig * (1.0 + gate * (1.0 - sig))
    grad = jnp.concatenate([grad_gate, grad_up], axis=1).astype(BF)
    router = jnp.sum(grad_up * up, axis=1, keepdims=True)
    back = mm(grad, weights_ref[...], 1, 1).astype(BF)
    return grad, router, back


def split_router(router, lane):
    high = router.astype(BF).astype(F32)
    low = router - high
    lanes = iota((router.shape[0], TAIL), 1)
    return jnp.where(lanes == lane, high, jnp.where(lanes == lane + 1, low, 0.0))


def serve_outer(cap_ref, own_ref, far_ref, weights_ref, own_back, far_back, own_grad, far_grad):
    width = weights_ref.shape[0]
    cap = cap_ref[0]
    grad, router, back = serve(far_ref, cap > 4, weights_ref)
    far_grad[...] = grad
    far_back[:, :width] = back
    far_back[:, width:] = split_router(router, 0).astype(BF)
    grad, router, back = serve(own_ref, cap > 2, weights_ref)
    own_grad[...] = grad
    own_back[:, :width] = back
    own_back[:, width:] = split_router(router, 0).astype(BF)


def serve_inner(rows_ref, weights_ref, own_back, swapped_back, out_ref, grad_ref):
    width = weights_ref.shape[0]
    grad, router, back = serve(rows_ref, None, weights_ref)
    grad_ref[...] = grad
    out_ref[:, :width] = own_back[:, :width] + swapped_back[:, :width]
    out_ref[:, width : 2 * width] = back
    out_ref[:, 2 * width :] = (
        own_back[:, width:].astype(F32)
        + swapped_back[:, width:].astype(F32)
        + split_router(router, 2)
    ).astype(BF)


def weight_grad(rows_a, rows_b, rows_c, grad_a, grad_b, grad_c, out_ref):
    total = mm(rows_a[...], grad_a[...], 0, 0)
    total += mm(rows_b[...], grad_b[...], 0, 0)
    total += mm(rows_c[...], grad_c[...], 0, 0)
    out_ref[...] = total.astype(BF)


def unpack(target_ref, weight_ref, back_ref, token_ref, router_ref):
    tokens, width = token_ref.shape
    routes = target_ref.shape[1]
    rows = back_ref.shape[0]
    owner = token_of_route(routes, tokens, routes // tokens)
    total = None
    router = None
    for part in range(2):
        hit = (iota((rows, routes), 0) == target_ref[part : part + 1, :]).astype(BF)
        by_token = mm(owner, hit, 0, 1).astype(BF)
        term = mm(by_token, back_ref[:, part * width : (part + 1) * width])
        total = term if total is None else total + term
        found = mm(back_ref[:, 2 * width :], hit, 0, 0)
        value = found[2 * part : 2 * part + 1, :] + found[2 * part + 1 : 2 * part + 2, :]
        router = value if router is None else router + value
    token_ref[...] = total.astype(BF)
    router_ref[...] = router / weight_ref[...].astype(BF).astype(F32)


def call(kernel, out, specs, flops, moved, *args):
    return pl.pallas_call(
        kernel,
        out_shape=[jax.ShapeDtypeStruct(s, d) for s, d in out],
        in_specs=specs,
        out_specs=[whole() for _ in out],
        compiler_params=params(),
        cost_estimate=pl.CostEstimate(flops=flops, bytes_accessed=moved, transcendentals=0),
    )(*args)


def exchange(value, count):
    one = value.reshape(count, -1, value.shape[-1])
    return lax.all_to_all(one, "expert", split_axis=0, concat_axis=0, tiled=True).reshape(
        value.shape
    )


def local(tokens, cotangent, routes, route_weight, expert_slot, capacity, gate_up):
    count = lax.axis_size("expert")
    token_rows, width = tokens.shape
    top = routes.shape[1]
    hidden = cotangent.shape[2]
    n_routes = token_rows * top
    rows = 2 * count
    route_row = routes.reshape(1, n_routes)
    weight_row = route_weight.reshape(1, n_routes)
    cot = cotangent.reshape(n_routes, hidden)
    my_cap = lax.dynamic_slice(capacity, (lax.axis_index("expert"),), (1,))
    swap = [(s, (s + count // 2) % count) for s in range(count)]

    weights = lax.all_gather(gate_up, "dp", axis=1, tiled=True)[0]
    pack_flops = 2 * rows * n_routes * (hidden + 2 * token_rows)
    row_shape = ((rows, width + hidden), BF)
    send_outer, target = call(
        pack_first,
        [row_shape, ((2, n_routes), jnp.int32)],
        [whole()] * 6,
        pack_flops,
        3 << 20,
        route_row,
        weight_row,
        expert_slot.reshape(1, count),
        capacity.reshape(1, count),
        tokens,
        cot,
    )
    recv_outer = exchange(send_outer, count)
    (send_inner,) = call(
        pack_second, [row_shape], [whole()] * 4, pack_flops, 3 << 20, target, weight_row, tokens, cot
    )
    recv_inner = exchange(send_inner, count)
    far_outer = lax.ppermute(recv_outer, "expert", swap)
    serve_flops = 2 * rows * width * 4 * hidden
    back_shape = ((rows, width + TAIL), BF)
    grad_shape = ((rows, 2 * hidden), BF)
    own_back, far_back, own_grad, far_grad = call(
        serve_outer,
        [back_shape, back_shape, grad_shape, grad_shape],
        [scalars()] + [whole()] * 3,
        2 * serve_flops,
        8 << 20,
        my_cap,
        recv_outer,
        far_outer,
        weights,
    )
    swapped_back = lax.ppermute(far_back, "expert", swap)
    send_back, inner_grad = call(
        serve_inner,
        [((rows, 2 * width + TAIL), BF), grad_shape],
        [whole()] * 4,
        serve_flops,
        8 << 20,
        recv_inner,
        weights,
        own_back,
        swapped_back,
    )
    back = exchange(send_back, count)

    block = 512
    row_spec = pl.BlockSpec((rows, block), lambda i: (0, i))
    grad_spec = pl.BlockSpec((rows, 2 * hidden), lambda i: (0, 0))
    part = pl.pallas_call(
        weight_grad,
        grid=(width // block,),
        out_shape=jax.ShapeDtypeStruct((width, 2 * hidden), BF),
        in_specs=[row_spec] * 3 + [grad_spec] * 3,
        out_specs=pl.BlockSpec((block, 2 * hidden), lambda i: (i, 0)),
        compiler_params=params(),
        cost_estimate=pl.CostEstimate(
            flops=6 * rows * width * 2 * hidden, bytes_accessed=8 << 20, transcendentals=0
        ),
    )(recv_outer, far_outer, recv_inner, own_grad, far_grad, inner_grad)
    gate_up_grad = lax.psum_scatter(part, "dp", scatter_dimension=0, tiled=True)[None]

    token_grad, router = call(
        unpack,
        [((token_rows, width), BF), ((1, n_routes), F32)],
        [whole()] * 3,
        4 * rows * n_routes * 2 * token_rows,
        4 << 20,
        target,
        weight_row,
        back,
    )
    return token_grad, router.reshape(token_rows, top), gate_up_grad


def solution(mesh):
    in_specs = (
        P(("expert", "dp"), None),
        P(("expert", "dp"), None, None),
        P(("expert", "dp"), None),
        P(("expert", "dp"), None),
        P(),
        P(),
        P("expert", "dp", None),
    )
    out_specs = (P(("expert", "dp"), None), P(("expert", "dp"), None), P("expert", "dp", None))
    return jax.shard_map(local, mesh=mesh, in_specs=in_specs, out_specs=out_specs, check_vma=False)
```

time: 496 us -> 335 us (0.68); the launches traced: 489 us -> 334 us
  waiting for transfers between devices: 276 us -> 210 us
  local copies, waits for them, and re-layouts: 68.1 us -> 29.3 us
  matrix products: 31.4 us -> 0 us
  Pallas kernels: 0 us -> 20.7 us
  other arithmetic: 20.6 us -> 0.66 us
  starting transfers between devices: 74.3 us -> 58.9 us
    all_gather x1, waiting for transfers between devices: 50.5 us -> 0.01 us  [local(): weights = lax.all_gather(gate_up, 'dp', axis=1, tiled=True)[0]]
    all_to_all x5 -> x3, waiting for transfers between devices: 196 us -> 158 us  [exchange(): lax.all_to_all(one, 'expert', split_axis=0, concat_axis=0, tiled=True)]
    dot_general x10 -> x0, matrix products: 31.4 us -> none  [the longest x4 10.7 us: serve_column(): pre_act = jnp.dot(rows_column, matrix, preferred_element_type=jnp.float32)]
    ppermute x2, waiting for transfers between devices: 28.6 us -> 51 us  [the longest x1 34.7 us: local(): far_outer = lax.ppermute(recv_outer, 'expert', swap)]
    pallas_call x0 -> x6, Pallas kernels: none -> 20.7 us  [the longest x5 15.9 us: call(): pl.pallas_call(kernel, out_shape=[jax.ShapeDtypeStruct(s, d) for s, d in...]
    all_to_all x5 -> x3, starting transfers between devices: 67.7 us -> 48.4 us  [exchange(): lax.all_to_all(one, 'expert', split_axis=0, concat_axis=0, tiled=True)]
    scatter x3 -> x0, local copies, waits for them, and re-layouts: 16.8 us -> none  [the longest x1 7.48 us: local(): send_rows = jnp.zeros((buffer_rows, model_width), jnp.bfloat16).at[target...]
    gather x3 -> x0, local copies, waits for them, and re-layouts: 13 us -> none  [the longest x2 6.95 us: local(): jnp.take(back_router.reshape(buffer_rows), target, axis=0, mode='fill', f...]
  transfers between devices with their start and end apart: 9 -> 7, of which waited for: 7 -> 5; matrix products, arithmetic and copies ran while one was open for 12% -> 4% of each run, Pallas kernels for 0% -> 4%
where the time goes in v1:
time: 335 us; the launch traced here: 334 us
  waiting for transfers between devices  210 us (63%)
  starting transfers between devices  58.9 us (18%)
  local copies, waits for them, and re-layouts  29.3 us (9%)
  Pallas kernels  20.7 us (6%)
  between operations  14.3 us (4%)
    all_to_all x3, waiting for transfers between devices, exchange(): lax.all_to_all(one, 'expert', split_axis=0, concat_axis=0, tiled=True)  158 us
    all_to_all x3, starting transfers between devices, exchange(): lax.all_to_all(one, 'expert', split_axis=0, concat_axis=0, tiled=True)  48.4 us
    ppermute x1, waiting for transfers between devices, local(): far_outer = lax.ppermute(recv_outer, 'expert', swap)  34.7 us
    ppermute x1, waiting for transfers between devices, local(): swapped_back = lax.ppermute(far_back, 'expert', swap)  16.3 us
    pallas_call x5, Pallas kernels, call(): pl.pallas_call(kernel, out_shape=[jax.ShapeDtypeStruct(s, d) for s, d in...  15.9 us
    unnamed x45, local copies, waits for them, and re-layouts  14.1 us
    reshape x3, local copies, waits for them, and re-layouts, exchange(): lax.all_to_all(one, 'expert', split_axis=0, concat_axis=0, tiled=True)  8.86 us
  transfers between devices with their start and end apart: 7, of which 5 were waited for; matrix products, arithmetic and copies ran while one was open for 4% of the time, Pallas kernels for 4%

profile of v1, /device:TPU:1, one launch (start us, length us, event | category | flops | bytes accessed | tf_op | source)
XLA Modules:
  0.0 334.0 jit_solution(1533685615926004502)
XLA Ops:
  7.2 0.8 copy.14
  8.0 0.1 reshape.43.weight_ref
  8.1 0.8 copy.13
  8.8 0.1 reshape.42.routes_ref
  8.9 1.1 copy-done
  10.1 1.0 copy-done.2
  11.1 0.7 copy-done.10
  11.8 0.7 copy-done.11
  12.4 1.5 shard_map.94
  13.9 1.3 reshape.49
  15.3 21.1 %all-to-all-start.1 = ((bf16[128,2,2432]{2,1,0:T(2,128)(2,1)}), bf16[128,2,2432]{2,1,0:T(2,128)(2,1)}, u32[]{:S(2)}, u32[]{:S(2)}) async-start(bf16[128,2,2432]{2,1,0:T(2,128)(2,1)} %reshape.49), calls=%async_computation.1 | async-start | bytes 2490368 | tf_op jit(solution)/shard_map/all_to_all | solution.py:176
  36.4 0.0 all-gather.2.cloned.1.call-start
  36.4 0.7 all-gather.2.cloned.1.call-update
  37.1 0.9 shard_map.95
  38.1 1.3 reshape.47
  39.4 59.4 %all-to-all-done.1 = bf16[128,2,2432]{2,1,0:T(2,128)(2,1)} async-done(((bf16[128,2,2432]{2,1,0:T(2,128)(2,1)}), bf16[128,2,2432]{2,1,0:T(2,128)(2,1)}, u32[]{:S(2)}, u32[]{:S(2)}) %all-to-all-start.1) | async-done | bytes 1245216 | tf_op jit(solution)/shard_map/all_to_all | solution.py:176
  98.8 8.9 %all-to-all-start = ((bf16[128,2,2432]{2,1,0:T(2,128)(2,1)}), bf16[128,2,2432]{2,1,0:T(2,128)(2,1)}, u32[]{:S(2)}, u32[]{:S(2)}) async-start(bf16[128,2,2432]{2,1,0:T(2,128)(2,1)} %reshape.47), calls=%async_computation | async-start | bytes 2490368 | tf_op jit(solution)/shard_map/all_to_all | solution.py:176
  107.8 0.0 copy-start.12
  107.8 3.0 reshape.50.own_ref.rows_a
  110.9 5.1 %collective-permute-start = (bf16[256,2432]{1,0:T(8,128)(2,1)S(1)}, bf16[256,2432]{1,0:T(8,128)(2,1)S(1)}, u32[]{:S(2)}, u32[]{:S(2)}) collective-permute-start(bf16[256,2432]{1,0:T(8,128)(2,1)S(1)} %reshape.50.own_ref.rows_a), channel_id=1, source_target_pairs={{0,256},{4,260},{8,264},{12,268},{16,272},{20,276},{24,280},{28,28... | collective-permute-start | bytes 3735560 | tf_op jit(solution)/shard_map/ppermute | solution.py:215
  116.0 0.6 dynamic_slice.3.cap_ref
  116.6 34.7 %collective-permute-done.far_ref.rows_b = bf16[256,2432]{1,0:T(8,128)(2,1)S(1)} collective-permute-done((bf16[256,2432]{1,0:T(8,128)(2,1)S(1)}, bf16[256,2432]{1,0:T(8,128)(2,1)S(1)}, u32[]{:S(2)}, u32[]{:S(2)}) %collective-permute-start) | collective-permute-done | bytes 1245216 | tf_op jit(solution)/shard_map/ppermute | solution.py:215
  151.3 7.1 %shard_map.96 = (bf16[256,2176]{1,0:T(8,128)(2,1)S(1)}, bf16[256,2176]{1,0:T(8,128)(2,1)}, bf16[256,768]{1,0:T(8,128)(2,1)S(1)}, bf16[256,768]{1,0:T(8,128)(2,1)S(1)}) custom-call(s32[1]{0:T(128)} %dynamic_slice.3.cap_ref, bf16[256,2432]{1,0:T(8,128)(2,1)S(1)} %reshape.50.own_ref.rows_a, bf16[256,2432]{1,0:T(8,128)(2,1)S(1)} %collective-permute-done.far_ref.rows_b, ...), custom_call_target="tpu_custom_call" | custom-call | flops 3221225472 | bytes 8388608 | tf_op jit(solution)/shard_map/pallas_call | solution.py:164
  158.5 1.1 copy-done.6
  159.6 0.7 copy-done.17
  160.3 5.3 %collective-permute-start.1 = (bf16[256,2176]{1,0:T(8,128)(2,1)}, bf16[256,2176]{1,0:T(8,128)(2,1)S(1)}, u32[]{:S(2)}, u32[]{:S(2)}) collective-permute-start(bf16[256,2176]{1,0:T(8,128)(2,1)} %get-tuple-element.16), channel_id=1, source_target_pairs={{0,256},{4,260},{8,264},{12,268},{16,272},{20,276},{24,280},{28,28... | collective-permute-start | bytes 3342344 | tf_op jit(solution)/shard_map/ppermute | solution.py:230
  165.7 4.6 %all-to-all-done = bf16[128,2,2432]{2,1,0:T(2,128)(2,1)} async-done(((bf16[128,2,2432]{2,1,0:T(2,128)(2,1)}), bf16[128,2,2432]{2,1,0:T(2,128)(2,1)}, u32[]{:S(2)}, u32[]{:S(2)}) %all-to-all-start) | async-done | bytes 1245216 | tf_op jit(solution)/shard_map/all_to_all | solution.py:176
  170.2 3.0 reshape.48.rows_ref.rows_c
  173.3 16.3 %collective-permute-done.1.swapped_back = bf16[256,2176]{1,0:T(8,128)(2,1)S(1)} collective-permute-done((bf16[256,2176]{1,0:T(8,128)(2,1)}, bf16[256,2176]{1,0:T(8,128)(2,1)S(1)}, u32[]{:S(2)}, u32[]{:S(2)}) %collective-permute-start.1) | collective-permute-done | bytes 1114144 | tf_op jit(solution)/shard_map/ppermute | solution.py:230
  189.5 1.0 copy-done.8
  190.6 1.2 copy-done.7
  191.8 1.2 copy-done.9
  193.1 4.3 %shard_map.97 = (bf16[256,4224]{1,0:T(8,128)(2,1)S(1)}, bf16[256,768]{1,0:T(8,128)(2,1)S(1)}) custom-call(bf16[256,2432]{1,0:T(8,128)(2,1)S(1)} %reshape.48.rows_ref.rows_c, bf16[2048,768]{1,0:T(8,128)(2,1)} %bitcast.10, bf16[256,2176]{1,0:T(8,128)(2,1)S(1)} %copy-done.7, bf16[256,2176]{1,0:T(8,128)(2,1)S(1)} %copy-done.9), custom_call_target="tpu_custom_call" | custom-call | flops 1610612736 | bytes 8388608 | tf_op jit(solution)/shard_map/pallas_call | solution.py:164
  197.4 0.7 copy-done.15
  198.2 2.2 reshape.51
  200.4 18.4 %all-to-all-start.2 = ((bf16[128,2,4224]{2,1,0:T(2,128)(2,1)}), bf16[128,2,4224]{2,1,0:T(2,128)(2,1)}, u32[]{:S(2)}, u32[]{:S(2)}) async-start(bf16[128,2,4224]{2,1,0:T(2,128)(2,1)} %reshape.51), calls=%async_computation.2 | async-start | bytes 4325376 | tf_op jit(solution)/shard_map/all_to_all | solution.py:176
  218.8 0.0 reduce-scatter.2.cloned.1.call-start
  218.9 1.3 copy-done.14
  220.2 1.0 copy-done.20
  221.2 4.8 %shard_map.99 = bf16[2048,768]{1,0:T(8,128)(2,1)} custom-call(bf16[256,2432]{1,0:T(8,128)(2,1)S(1)} %copy-done.5, bf16[256,2432]{1,0:T(8,128)(2,1)S(1)} %copy-done.14, bf16[256,2432]{1,0:T(8,128)(2,1)S(1)} %reshape.48.rows_ref.rows_c, bf16[256,768]{1,0:T(8,128)(2,1)S(1)} %copy-done.18, bf16[256,768]{1,0:T(8,128)(2,1)S(1)} %copy-done.20, ...), custom_call_target="tpu_custom_call" | custom-call | flops 2415919104 | bytes 8388608 | tf_op jit(solution)/shard_map/pallas_call | solution.py:247
  225.9 0.0 reduce-scatter.2.cloned.1.call-update
  225.9 94.5 %all-to-all-done.2 = bf16[128,2,4224]{2,1,0:T(2,128)(2,1)} async-done(((bf16[128,2,4224]{2,1,0:T(2,128)(2,1)}), bf16[128,2,4224]{2,1,0:T(2,128)(2,1)}, u32[]{:S(2)}, u32[]{:S(2)}) %all-to-all-start.2) | async-done | bytes 2162720 | tf_op jit(solution)/shard_map/all_to_all | solution.py:176
  320.4 2.8 reshape.52.back_ref
  323.2 2.0 shard_map.98
  325.2 0.5 broadcast.3
  325.7 0.7 reduce.3
  326.4 0.1 reshape.53
  326.5 0.7 copy.15
  (31 shorter events, 0.1 us)
Async XLA Ops:
  8.9 1.1 copy-start
  10.1 1.0 copy-start.2
  11.1 0.7 copy-start.10
  11.8 0.7 copy-start.11
  15.3 21.9 %copy-start.1 = (bf16[128,8,384]{2,1,0:T(8,128)(2,1)S(1)}, bf16[128,8,384]{2,1,0:T(8,128)(2,1)}, u32[]{:S(2)}) copy-start(bf16[128,8,384]{2,1,0:T(8,128)(2,1)} %param.8) | copy-start | bytes 2359300
  15.3 21.9 %copy-start.3 = (bf16[128,2048]{1,0:T(8,128)(2,1)S(1)}, bf16[128,2048]{1,0:T(8,128)(2,1)}, u32[]{:S(2)}) copy-start(bf16[128,2048]{1,0:T(8,128)(2,1)} %tokens_ref.3) | copy-start | bytes 1572868
  15.3 83.5 %all-to-all-start.1 = ((bf16[128,2,2432]{2,1,0:T(2,128)(2,1)}), bf16[128,2,2432]{2,1,0:T(2,128)(2,1)}, u32[]{:S(2)}, u32[]{:S(2)}) async-start(bf16[128,2,2432]{2,1,0:T(2,128)(2,1)} %reshape.49), calls=%async_computation.1 | async-start | bytes 2490368 | tf_op jit(solution)/shard_map/all_to_all | solution.py:176
  36.4 80.2 %all-gather.2.cloned.1.call-start = ((), (), s32[]{:S(2)}) async-start(), calls=%async_computation.4 | async-start | bytes 3932160 | tf_op jit(solution)/shard_map/all_gather | solution.py:194
  98.8 71.4 %all-to-all-start = ((bf16[128,2,2432]{2,1,0:T(2,128)(2,1)}), bf16[128,2,2432]{2,1,0:T(2,128)(2,1)}, u32[]{:S(2)}, u32[]{:S(2)}) async-start(bf16[128,2,2432]{2,1,0:T(2,128)(2,1)} %reshape.47), calls=%async_computation | async-start | bytes 2490368 | tf_op jit(solution)/shard_map/all_to_all | solution.py:176
  107.8 8.2 %copy-start.12 = (s32[128]{0:T(128)S(1)}, s32[128]{0:T(128)}, u32[]{:S(2)}) copy-start(s32[128]{0:T(128)} %param.12) | copy-start | bytes 1540
  110.8 47.6 %copy-start.4 = (bf16[256,2432]{1,0:T(8,128)(2,1)}, bf16[256,2432]{1,0:T(8,128)(2,1)S(1)}, u32[]{:S(2)}) copy-start(bf16[256,2432]{1,0:T(8,128)(2,1)S(1)} %reshape.50.own_ref.rows_a) | copy-start | bytes 3735556
  110.9 40.5 %collective-permute-start = (bf16[256,2432]{1,0:T(8,128)(2,1)S(1)}, bf16[256,2432]{1,0:T(8,128)(2,1)S(1)}, u32[]{:S(2)}, u32[]{:S(2)}) collective-permute-start(bf16[256,2432]{1,0:T(8,128)(2,1)S(1)} %reshape.50.own_ref.rows_a), channel_id=1, source_target_pairs={{0,256},{4,260},{8,264},{12,268},{16,272},{20,276},{24,280},{28,28... | collective-permute-start | bytes 3735560 | tf_op jit(solution)/shard_map/ppermute | solution.py:215
  151.3 7.2 %copy-start.13 = (bf16[256,2432]{1,0:T(8,128)(2,1)}, bf16[256,2432]{1,0:T(8,128)(2,1)S(1)}, u32[]{:S(2)}) copy-start(bf16[256,2432]{1,0:T(8,128)(2,1)S(1)} %collective-permute-done.far_ref.rows_b) | copy-start | bytes 3735556
  158.5 1.1 copy-start.6
  159.6 0.7 copy-start.17
  160.3 12.9 %copy-start.19 = (bf16[256,768]{1,0:T(8,128)(2,1)}, bf16[256,768]{1,0:T(8,128)(2,1)S(1)}, u32[]{:S(2)}) copy-start(bf16[256,768]{1,0:T(8,128)(2,1)S(1)} %get-tuple-element.21.grad_b) | copy-start | bytes 1179652
  160.3 29.2 %collective-permute-start.1 = (bf16[256,2176]{1,0:T(8,128)(2,1)}, bf16[256,2176]{1,0:T(8,128)(2,1)S(1)}, u32[]{:S(2)}, u32[]{:S(2)}) collective-permute-start(bf16[256,2176]{1,0:T(8,128)(2,1)} %get-tuple-element.16), channel_id=1, source_target_pairs={{0,256},{4,260},{8,264},{12,268},{16,272},{20,276},{24,280},{28,28... | collective-permute-start | bytes 3342344 | tf_op jit(solution)/shard_map/ppermute | solution.py:230
  189.5 1.0 copy-start.8
  190.6 1.2 copy-start.7
  191.8 1.2 copy-start.9
  197.4 0.8 copy-start.15
  200.4 18.4 %copy-start.5 = (bf16[256,2432]{1,0:T(8,128)(2,1)S(1)}, bf16[256,2432]{1,0:T(8,128)(2,1)}, u32[]{:S(2)}) copy-start(bf16[256,2432]{1,0:T(8,128)(2,1)} %copy-done.4) | copy-start | bytes 3735556
  200.4 18.4 %copy-start.16 = (bf16[256,768]{1,0:T(8,128)(2,1)S(1)}, bf16[256,768]{1,0:T(8,128)(2,1)}, u32[]{:S(2)}) copy-start(bf16[256,768]{1,0:T(8,128)(2,1)} %copy-done.15) | copy-start | bytes 1179652
  200.4 18.5 %copy-start.18 = (bf16[256,768]{1,0:T(8,128)(2,1)S(1)}, bf16[256,768]{1,0:T(8,128)(2,1)}, u32[]{:S(2)}) copy-start(bf16[256,768]{1,0:T(8,128)(2,1)} %copy-done.17) | copy-start | bytes 1179652
  200.4 120.0 %all-to-all-start.2 = ((bf16[128,2,4224]{2,1,0:T(2,128)(2,1)}), bf16[128,2,4224]{2,1,0:T(2,128)(2,1)}, u32[]{:S(2)}, u32[]{:S(2)}) async-start(bf16[128,2,4224]{2,1,0:T(2,128)(2,1)} %reshape.51), calls=%async_computation.2 | async-start | bytes 4325376 | tf_op jit(solution)/shard_map/all_to_all | solution.py:176
  218.8 108.3 %reduce-scatter.2.cloned.1.call-start = ((), (), s32[]{:S(2)}) async-start(), calls=%async_computation.5 | async-start | bytes 3932160 | tf_op jit(solution)/shard_map/reduce_scatter | solution.py:258
  218.9 1.3 copy-start.14
  220.2 1.0 copy-start.20
Sparse Core Ops, SparseCore 0:
  39.3 48.1 all-gather.1
  226.1 46.8 reduce-scatter.1

commit v2 on v1

--- a/solution.py
+++ b/solution.py
@@ -35,17 +35,20 @@
     return ((iota((routes, tokens), 0) // top) == iota((routes, tokens), 1)).astype(BF)
 
 
-def gather_rows(target, weight, tokens, cot, top, out_ref):
+def gather_rows(target, weight, tokens, cot, top, out_ref, start):
     rows = out_ref.shape[0]
     routes = target.shape[1]
     width = tokens.shape[1]
+    hidden = cot.shape[1]
     hit = iota((rows, routes), 0) == target
     by_token = mm(hit.astype(BF), token_of_route(routes, tokens.shape[0], top)).astype(BF)
-    out_ref[:, :width] = mm(by_token, tokens[...]).astype(BF)
-    out_ref[:, width:] = mm(jnp.where(hit, weight, 0.0).astype(BF), cot[...]).astype(BF)
-
-
-def pack_first(routes_ref, weight_ref, slot_ref, cap_ref, tokens_ref, cot_ref, out_ref, target_ref):
+    out_ref[:, start : start + width] = mm(by_token, tokens[...]).astype(BF)
+    out_ref[:, start + width : start + width + hidden] = mm(
+        jnp.where(hit, weight, 0.0).astype(BF), cot[...]
+    ).astype(BF)
+
+
+def pack(routes_ref, weight_ref, slot_ref, cap_ref, tokens_ref, cot_ref, out_ref, target_ref):
     experts = slot_ref.shape[1]
     routes = routes_ref.shape[1]
     tokens = tokens_ref.shape[0]
@@ -72,23 +75,18 @@
     dest = jnp.where(far, jnp.where(slot >= half, slot - half, slot + half), slot)
     outer = jnp.where(kept & (place >= 2), dest * 2 + place - 2, -1)
     inner = jnp.where(kept & (place < 2), dest * 2 + place, -1)
-    target_ref[0:1, :] = outer
-    target_ref[1:2, :] = inner
-    gather_rows(outer, weight_ref[...], tokens_ref, cot_ref, top, out_ref)
-
-
-def pack_second(target_ref, weight_ref, tokens_ref, cot_ref, out_ref):
-    top = target_ref.shape[1] // tokens_ref.shape[0]
-    gather_rows(target_ref[1:2, :], weight_ref[...], tokens_ref, cot_ref, top, out_ref)
-
-
-def serve(rows_ref, valid, weights_ref):
+    target_ref[0:1, :] = inner
+    target_ref[1:2, :] = outer
+    part = tokens_ref.shape[1] + cot_ref.shape[1]
+    gather_rows(inner, weight_ref[...], tokens_ref, cot_ref, top, out_ref, 0)
+    gather_rows(outer, weight_ref[...], tokens_ref, cot_ref, top, out_ref, part)
+
+
+def serve(rows_ref, start, weights_ref):
     width = weights_ref.shape[0]
     hidden = weights_ref.shape[1] // 2
-    pre = mm(rows_ref[:, :width], weights_ref[...])
-    scaled = rows_ref[:, width:].astype(F32)
-    if valid is not None:
-        scaled = jnp.where(valid, scaled, 0.0)
+    pre = mm(rows_ref[:, start : start + width], weights_ref[...])
+    scaled = rows_ref[:, start + width : start + width + hidden].astype(F32)
     gate = pre[:, :hidden]
     up = pre[:, hidden:]
     sig = jax.nn.sigmoid(gate)
@@ -108,37 +106,37 @@
     return jnp.where(lanes == lane, high, jnp.where(lanes == lane + 1, low, 0.0))
 
 
-def serve_outer(cap_ref, own_ref, far_ref, weights_ref, own_back, far_back, own_grad, far_grad):
-    width = weights_ref.shape[0]
-    cap = cap_ref[0]
-    grad, router, back = serve(far_ref, cap > 4, weights_ref)
-    far_grad[...] = grad
-    far_back[:, :width] = back
-    far_back[:, width:] = split_router(router, 0).astype(BF)
-    grad, router, back = serve(own_ref, cap > 2, weights_ref)
-    own_grad[...] = grad
-    own_back[:, :width] = back
-    own_back[:, width:] = split_router(router, 0).astype(BF)
-
-
-def serve_inner(rows_ref, weights_ref, own_back, swapped_back, out_ref, grad_ref):
-    width = weights_ref.shape[0]
-    grad, router, back = serve(rows_ref, None, weights_ref)
-    grad_ref[...] = grad
-    out_ref[:, :width] = own_back[:, :width] + swapped_back[:, :width]
-    out_ref[:, width : 2 * width] = back
-    out_ref[:, 2 * width :] = (
-        own_back[:, width:].astype(F32)
-        + swapped_back[:, width:].astype(F32)
-        + split_router(router, 2)
-    ).astype(BF)
-
-
-def weight_grad(rows_a, rows_b, rows_c, grad_a, grad_b, grad_c, out_ref):
-    total = mm(rows_a[...], grad_a[...], 0, 0)
-    total += mm(rows_b[...], grad_b[...], 0, 0)
-    total += mm(rows_c[...], grad_c[...], 0, 0)
-    out_ref[...] = total.astype(BF)
+def serve_all(cap_ref, rows_ref, own_ref, partner_ref, out_ref, inner_ref, outer_ref, far_ref):
+    width = own_ref.shape[0]
+    part = rows_ref.shape[1] // 2
+    grad, router, back = serve(rows_ref, 0, own_ref)
+    inner_ref[...] = grad
+    out_ref[:, :width] = back
+    tail = split_router(router, 0)
+
+    def outer_with(weights_ref, mine_ref, other_ref):
+        grad, router, back = serve(rows_ref, part, weights_ref)
+        mine_ref[...] = grad
+        other_ref[...] = jnp.zeros_like(grad)
+        out_ref[:, width : 2 * width] = back
+        out_ref[:, 2 * width :] = (tail + split_router(router, 2)).astype(BF)
+
+    is_own = cap_ref[0] > 2
+
+    @pl.when(is_own)
+    def _():
+        outer_with(own_ref, outer_ref, far_ref)
+
+    @pl.when(jnp.logical_not(is_own))
+    def _():
+        outer_with(partner_ref, far_ref, outer_ref)
+
+
+def weight_grads(inner_rows, outer_rows, inner_grad, outer_grad, far_grad, own_ref, far_ref):
+    total = mm(inner_rows[...], inner_grad[...], 0, 0)
+    total += mm(outer_rows[...], outer_grad[...], 0, 0)
+    own_ref[...] = total.astype(BF)
+    far_ref[...] = mm(outer_rows[...], far_grad[...], 0, 0).astype(BF)
 
 
 def unpack(target_ref, weight_ref, back_ref, token_ref, router_ref):
@@ -191,15 +189,16 @@
     my_cap = lax.dynamic_slice(capacity, (lax.axis_index("expert"),), (1,))
     swap = [(s, (s + count // 2) % count) for s in range(count)]
 
-    weights = lax.all_gather(gate_up, "dp", axis=1, tiled=True)[0]
-    pack_flops = 2 * rows * n_routes * (hidden + 2 * token_rows)
-    row_shape = ((rows, width + hidden), BF)
-    send_outer, target = call(
-        pack_first,
-        [row_shape, ((2, n_routes), jnp.int32)],
+    own_weights = lax.all_gather(gate_up, "dp", axis=1, tiled=True)[0]
+    partner_shard = lax.ppermute(gate_up, "expert", swap)
+    partner_weights = lax.all_gather(partner_shard, "dp", axis=1, tiled=True)[0]
+    part = width + hidden
+    send, target = call(
+        pack,
+        [((rows, 2 * part), BF), ((2, n_routes), jnp.int32)],
         [whole()] * 6,
-        pack_flops,
-        3 << 20,
+        4 * rows * n_routes * (hidden + 2 * token_rows),
+        4 << 20,
         route_row,
         weight_row,
         expert_slot.reshape(1, count),
@@ -207,55 +206,46 @@
         tokens,
         cot,
     )
-    recv_outer = exchange(send_outer, count)
-    (send_inner,) = call(
-        pack_second, [row_shape], [whole()] * 4, pack_flops, 3 << 20, target, weight_row, tokens, cot
-    )
-    recv_inner = exchange(send_inner, count)
-    far_outer = lax.ppermute(recv_outer, "expert", swap)
-    serve_flops = 2 * rows * width * 4 * hidden
-    back_shape = ((rows, width + TAIL), BF)
+    recv = exchange(send, count)
     grad_shape = ((rows, 2 * hidden), BF)
-    own_back, far_back, own_grad, far_grad = call(
-        serve_outer,
-        [back_shape, back_shape, grad_shape, grad_shape],
+    send_back, inner_grad, outer_grad, far_grad = call(
+        serve_all,
+        [((rows, 2 * width + TAIL), BF), grad_shape, grad_shape, grad_shape],
         [scalars()] + [whole()] * 3,
-        2 * serve_flops,
-        8 << 20,
+        16 * rows * width * hidden,
+        12 << 20,
         my_cap,
-        recv_outer,
-        far_outer,
-        weights,
-    )
-    swapped_back = lax.ppermute(far_back, "expert", swap)
-    send_back, inner_grad = call(
-        serve_inner,
-        [((rows, 2 * width + TAIL), BF), grad_shape],
-        [whole()] * 4,
-        serve_flops,
-        8 << 20,
-        recv_inner,
-        weights,
-        own_back,
-        swapped_back,
+        recv,
+        own_weights,
+        partner_weights,
     )
     back = exchange(send_back, count)
 
-    block = 512
-    row_spec = pl.BlockSpec((rows, block), lambda i: (0, i))
+    block = 128
     grad_spec = pl.BlockSpec((rows, 2 * hidden), lambda i: (0, 0))
-    part = pl.pallas_call(
-        weight_grad,
+    out_spec = pl.BlockSpec((block, 2 * hidden), lambda i: (i, 0))
+    out = jax.ShapeDtypeStruct((width, 2 * hidden), BF)
+    own_part, far_part = pl.pallas_call(
+        weight_grads,
         grid=(width // block,),
-        out_shape=jax.ShapeDtypeStruct((width, 2 * hidden), BF),
-        in_specs=[row_spec] * 3 + [grad_spec] * 3,
-        out_specs=pl.BlockSpec((block, 2 * hidden), lambda i: (i, 0)),
+        out_shape=[out, out],
+        in_specs=[
+            pl.BlockSpec((rows, block), lambda i: (0, i)),
+            pl.BlockSpec((rows, block), lambda i: (0, i + part // block)),
+            grad_spec,
+            grad_spec,
+            grad_spec,
+        ],
+        out_specs=[out_spec, out_spec],
         compiler_params=params(),
         cost_estimate=pl.CostEstimate(
-            flops=6 * rows * width * 2 * hidden, bytes_accessed=8 << 20, transcendentals=0
+            flops=12 * rows * width * hidden, bytes_accessed=10 << 20, transcendentals=0
         ),
-    )(recv_outer, far_outer, recv_inner, own_grad, far_grad, inner_grad)
-    gate_up_grad = lax.psum_scatter(part, "dp", scatter_dimension=0, tiled=True)[None]
+    )(recv, recv, inner_grad, outer_grad, far_grad)
+    far_shard = lax.psum_scatter(far_part, "dp", scatter_dimension=0, tiled=True)
+    own_shard = lax.psum_scatter(own_part, "dp", scatter_dimension=0, tiled=True)
+    moved_shard = lax.ppermute(far_shard, "expert", swap)
+    gate_up_grad = (own_shard.astype(F32) + moved_shard.astype(F32)).astype(BF)[None]
 
     token_grad, router = call(
         unpack,

time: 335 us -> 306 us (0.913)
  starting transfers between devices: 58.9 us -> 40.8 us
  local copies, waits for them, and re-layouts: 29.3 us -> 22.3 us
  waiting for transfers between devices: 210 us -> 203 us
    reduce_scatter x1 -> x2, waiting for transfers between devices: 0.01 us -> 69.6 us  [the longest x1 43.8 us: local(): lax.psum_scatter(own_part, 'dp', scatter_dimension=0, tiled=True)]
    all_to_all x3 -> x2, waiting for transfers between devices: 158 us -> 110 us  [exchange(): lax.all_to_all(one, 'expert', split_axis=0, concat_axis=0, tiled=True)]
    ppermute x2, waiting for transfers between devices: 51 us -> 22.3 us  [the longest x1 22.3 us: local(): partner_shard = lax.ppermute(gate_up, 'expert', swap)]
    all_to_all x3 -> x2, starting transfers between devices: 48.4 us -> 30.9 us  [exchange(): lax.all_to_all(one, 'expert', split_axis=0, concat_axis=0, tiled=True)]
    unnamed x45 -> x21, local copies, waits for them, and re-layouts: 14.1 us -> 8.19 us
    pallas_call x1, Pallas kernels: 4.76 us -> 9.74 us  [local(): pl.pallas_call(weight_grads, grid=(width // block,), out_shape=[out, out]...]
    pallas_call x5 -> x3, Pallas kernels: 15.9 us -> 12.4 us  [call(): pl.pallas_call(kernel, out_shape=[jax.ShapeDtypeStruct(s, d) for s, d in...]
    reshape x3 -> x2, local copies, waits for them, and re-layouts: 8.86 us -> 7.98 us  [exchange(): lax.all_to_all(one, 'expert', split_axis=0, concat_axis=0, tiled=True)]
  transfers between devices with their start and end apart: 7 -> 8, of which waited for: 5 -> 5; matrix products, arithmetic and copies ran while one was open for 4% -> 3% of each run, Pallas kernels for 4% -> 0%
where the time goes in v2:
time: 306 us; the launch traced here: 305 us
  waiting for transfers between devices  203 us (66%)
  starting transfers between devices  40.8 us (13%)
  local copies, waits for them, and re-layouts  22.3 us (7%)
  Pallas kernels  22.1 us (7%)
  between operations  13.9 us (5%)
    all_to_all x2, waiting for transfers between devices, exchange(): lax.all_to_all(one, 'expert', split_axis=0, concat_axis=0, tiled=True)  110 us
    reduce_scatter x1, waiting for transfers between devices, local(): lax.psum_scatter(own_part, 'dp', scatter_dimension=0, tiled=True)  43.8 us
    all_to_all x2, starting transfers between devices, exchange(): lax.all_to_all(one, 'expert', split_axis=0, concat_axis=0, tiled=True)  30.9 us
    reduce_scatter x1, waiting for transfers between devices, local(): lax.psum_scatter(far_part, 'dp', scatter_dimension=0, tiled=True)  25.8 us
    ppermute x1, waiting for transfers between devices, local(): partner_shard = lax.ppermute(gate_up, 'expert', swap)  22.3 us
    pallas_call x3, Pallas kernels, call(): pl.pallas_call(kernel, out_shape=[jax.ShapeDtypeStruct(s, d) for s, d in...  12.4 us
    pallas_call x1, Pallas kernels, local(): pl.pallas_call(weight_grads, grid=(width // block,), out_shape=[out, out]...  9.74 us
    unnamed x21, local copies, waits for them, and re-layouts  8.19 us
  transfers between devices with their start and end apart: 8, of which 5 were waited for; matrix products, arithmetic and copies ran while one was open for 3% of the time, Pallas kernels for 0%

profile of v2, /device:TPU:1, one launch (start us, length us, event | category | flops | bytes accessed | tf_op | source)
XLA Modules:
  0.0 305.2 jit_solution(8360262158511501749)
XLA Ops:
  7.2 0.8 copy.13
  8.0 0.1 reshape.36.routes_ref
  8.1 0.8 copy.14
  8.8 0.1 reshape.37.weight_ref
  8.9 1.1 copy-done.2
  10.1 1.0 copy-done.3
  11.1 0.7 copy-done.4
  11.8 0.7 copy-done.5
  12.4 2.2 shard_map.94
  14.7 2.4 reshape.41
  17.1 21.1 %all-to-all-start = ((bf16[128,2,4864]{2,1,0:T(2,128)(2,1)}), bf16[128,2,4864]{2,1,0:T(2,128)(2,1)}, u32[]{:S(2)}, u32[]{:S(2)}) async-start(bf16[128,2,4864]{2,1,0:T(2,128)(2,1)} %reshape.41), calls=%async_computation | async-start | bytes 4980736 | tf_op jit(solution)/shard_map/all_to_all | solution.py:174
  38.2 0.0 all-gather.3.cloned.1.call-start
  38.3 0.7 all-gather.3.cloned.1.call-update
  39.0 0.0 all-gather.5.cloned.1.call-start
  39.0 0.0 copy-done.7
  39.0 5.1 %collective-permute-start = (bf16[1,512,768]{2,1,0:T(8,128)(2,1)S(1)}, bf16[1,512,768]{2,1,0:T(8,128)(2,1)S(1)}, u32[]{:S(2)}, u32[]{:S(2)}) collective-permute-start(bf16[1,512,768]{2,1,0:T(8,128)(2,1)S(1)} %copy-done.7), channel_id=1, source_target_pairs={{0,256},{4,260},{8,264},{12,268},{16,272},{20,276},{24,280},{28,28... | collective-permute-start | bytes 2359304 | tf_op jit(solution)/shard_map/ppermute | solution.py:193
  44.1 22.3 %collective-permute-done = bf16[1,512,768]{2,1,0:T(8,128)(2,1)S(1)} collective-permute-done((bf16[1,512,768]{2,1,0:T(8,128)(2,1)S(1)}, bf16[1,512,768]{2,1,0:T(8,128)(2,1)S(1)}, u32[]{:S(2)}, u32[]{:S(2)}) %collective-permute-start) | collective-permute-done | bytes 786464 | tf_op jit(solution)/shard_map/ppermute | solution.py:193
  66.4 0.9 copy-done.8
  67.3 0.0 all-gather.5.cloned.1.call-update
  67.3 0.0 reduce-scatter.5.cloned.1.call-start
  67.4 0.0 copy-done.6
  67.4 0.6 dynamic_slice.3.cap_ref
  68.0 85.5 %all-to-all-done = bf16[128,2,4864]{2,1,0:T(2,128)(2,1)} async-done(((bf16[128,2,4864]{2,1,0:T(2,128)(2,1)}), bf16[128,2,4864]{2,1,0:T(2,128)(2,1)}, u32[]{:S(2)}, u32[]{:S(2)}) %all-to-all-start) | async-done | bytes 2490400 | tf_op jit(solution)/shard_map/all_to_all | solution.py:174
  153.5 5.2 %reshape.42.rows_ref.inner_rows.outer_rows = bf16[256,4864]{1,0:T(8,128)(2,1)S(1)} reshape(bf16[128,2,4864]{2,1,0:T(2,128)(2,1)} %all-to-all-done) | data formatting | bytes 4980736 | tf_op jit(solution)/shard_map/reshape | solution.py:174
  158.7 0.0 all-gather.3.cloned.1.call-done
  158.7 0.0 all-gather.5.cloned.1.call-done
  158.7 8.2 %shard_map.95 = (bf16[256,4224]{1,0:T(8,128)(2,1)S(1)}, bf16[256,768]{1,0:T(8,128)(2,1)S(1)}, bf16[256,768]{1,0:T(8,128)(2,1)S(1)}, bf16[256,768]{1,0:T(8,128)(2,1)S(1)}) custom-call(s32[1]{0:T(128)} %dynamic_slice.3.cap_ref, bf16[256,4864]{1,0:T(8,128)(2,1)S(1)} %reshape.42.rows_ref.inner_rows.outer_rows, bf16[2048,768]{1,0:T(8,128)(2,1)} %bitcast.10, ...), custom_call_target="tpu_custom_call" | custom-call | flops 3221225472 | bytes 12582912 | tf_op jit(solution)/shard_map/pallas_call | solution.py:162
  166.9 0.0 copy-start
  166.9 9.7 %shard_map.97 = (bf16[2048,768]{1,0:T(8,128)(2,1)}, bf16[2048,768]{1,0:T(8,128)(2,1)}) custom-call(bf16[256,4864]{1,0:T(8,128)(2,1)S(1)} %reshape.42.rows_ref.inner_rows.outer_rows, bf16[256,4864]{1,0:T(8,128)(2,1)S(1)} %reshape.42.rows_ref.inner_rows.outer_rows, bf16[256,768]{1,0:T(8,128)(2,1)S(1)} %get-tuple-element.18.inner_grad, ...), custom_call_target="tpu_custom_call" | custom-call | flops 2415919104 | bytes 10485760 | tf_op jit(solution)/shard_map/pallas_call | solution.py:228
  176.7 0.0 copy-done
  176.7 0.0 reduce-scatter.5.cloned.1.call-update
  176.7 1.6 copy-done.1
  178.3 2.3 reshape.43
  180.6 9.8 %all-to-all-start.1 = ((bf16[128,2,4224]{2,1,0:T(2,128)(2,1)}), bf16[128,2,4224]{2,1,0:T(2,128)(2,1)}, u32[]{:S(2)}, u32[]{:S(2)}) async-start(bf16[128,2,4224]{2,1,0:T(2,128)(2,1)} %reshape.43), calls=%async_computation.1 | async-start | bytes 4325376 | tf_op jit(solution)/shard_map/all_to_all | solution.py:174
  190.4 0.0 reduce-scatter.3.cloned.1.call-start
  190.4 0.5 reduce-scatter.3.cloned.1.call-update
  190.9 25.8 %reduce-scatter.5.cloned.1.call-done = bf16[512,768]{1,0:T(8,128)(2,1)} async-done(((bf16[2048,768]{1,0:T(8,128)(2,1)}), bf16[512,768]{1,0:T(8,128)(2,1)}) %reduce-scatter.5.cloned.1.call-update) | async-done | bytes 786448 | tf_op jit(solution)/shard_map/reduce_scatter | solution.py:245
  216.7 4.6 %collective-permute-start.1 = (bf16[512,768]{1,0:T(8,128)(2,1)}, bf16[512,768]{1,0:T(8,128)(2,1)S(1)}, u32[]{:S(2)}, u32[]{:S(2)}) collective-permute-start(bf16[512,768]{1,0:T(8,128)(2,1)} %reduce-scatter.5.cloned.1.call-done), channel_id=1, source_target_pairs={{0,256},{4,260},{8,264},{12,268},{16,272},{20,276},{24,280},{28,28... | collective-permute-start | bytes 2359304 | tf_op jit(solution)/shard_map/ppermute | solution.py:247
  221.4 43.8 %reduce-scatter.3.cloned.1.call-done = bf16[512,768]{1,0:T(8,128)(2,1)} async-done(((bf16[2048,768]{1,0:T(8,128)(2,1)}), bf16[512,768]{1,0:T(8,128)(2,1)}) %reduce-scatter.3.cloned.1.call-update) | async-done | bytes 786448 | tf_op jit(solution)/shard_map/reduce_scatter | solution.py:246
  265.2 0.0 collective-permute-done.1
  265.2 2.2 fusion
  267.4 24.6 %all-to-all-done.1 = bf16[128,2,4224]{2,1,0:T(2,128)(2,1)} async-done(((bf16[128,2,4224]{2,1,0:T(2,128)(2,1)}), bf16[128,2,4224]{2,1,0:T(2,128)(2,1)}, u32[]{:S(2)}, u32[]{:S(2)}) %all-to-all-start.1) | async-done | bytes 2162720 | tf_op jit(solution)/shard_map/all_to_all | solution.py:174
  292.0 2.8 reshape.44.back_ref
  294.8 2.0 shard_map.96
  296.8 0.5 broadcast.3
  297.3 0.7 reduce.3
  297.9 0.1 reshape.45
  298.0 0.7 copy.15
  (8 shorter events, 0.0 us)
Async XLA Ops:
  8.9 1.1 copy-start.2
  10.1 1.0 copy-start.3
  11.1 0.7 copy-start.4
  11.8 0.7 copy-start.5
  17.1 21.9 %copy-start.7 = (bf16[1,512,768]{2,1,0:T(8,128)(2,1)S(1)}, bf16[1,512,768]{2,1,0:T(8,128)(2,1)}, u32[]{:S(2)}) copy-start(bf16[1,512,768]{2,1,0:T(8,128)(2,1)} %param.13) | copy-start | bytes 2359300
  17.1 50.2 %copy-start.6 = (s32[128]{0:T(128)S(1)}, s32[128]{0:T(128)}, u32[]{:S(2)}) copy-start(s32[128]{0:T(128)} %param.12) | copy-start | bytes 1540
  17.1 136.3 %all-to-all-start = ((bf16[128,2,4864]{2,1,0:T(2,128)(2,1)}), bf16[128,2,4864]{2,1,0:T(2,128)(2,1)}, u32[]{:S(2)}, u32[]{:S(2)}) async-start(bf16[128,2,4864]{2,1,0:T(2,128)(2,1)} %reshape.41), calls=%async_computation | async-start | bytes 4980736 | tf_op jit(solution)/shard_map/all_to_all | solution.py:174
  38.2 120.5 %all-gather.3.cloned.1.call-start = ((), (), s32[]{:S(2)}) async-start(), calls=%async_computation.4 | async-start | bytes 3932160 | tf_op jit(solution)/shard_map/all_gather | solution.py:192
  39.0 119.8 %all-gather.5.cloned.1.call-start = ((), (), s32[]{:S(2)}) async-start(), calls=%async_computation.5 | async-start | bytes 3932160 | tf_op jit(solution)/shard_map/all_gather | solution.py:194
  39.0 27.4 %collective-permute-start = (bf16[1,512,768]{2,1,0:T(8,128)(2,1)S(1)}, bf16[1,512,768]{2,1,0:T(8,128)(2,1)S(1)}, u32[]{:S(2)}, u32[]{:S(2)}) collective-permute-start(bf16[1,512,768]{2,1,0:T(8,128)(2,1)S(1)} %copy-done.7), channel_id=1, source_target_pairs={{0,256},{4,260},{8,264},{12,268},{16,272},{20,276},{24,280},{28,28... | collective-permute-start | bytes 2359304 | tf_op jit(solution)/shard_map/ppermute | solution.py:193
  66.4 0.9 copy-start.8
  67.3 149.4 %reduce-scatter.5.cloned.1.call-start = ((), (), s32[]{:S(2)}) async-start(), calls=%async_computation.7 | async-start | bytes 3932160 | tf_op jit(solution)/shard_map/reduce_scatter | solution.py:245
  166.9 9.8 %copy-start = (bf16[256,4224]{1,0:T(8,128)(2,1)}, bf16[256,4224]{1,0:T(8,128)(2,1)S(1)}, u32[]{:S(2)}) copy-start(bf16[256,4224]{1,0:T(8,128)(2,1)S(1)} %get-tuple-element.15) | copy-start | bytes 6488068
  176.7 1.6 copy-start.1
  180.6 111.4 %all-to-all-start.1 = ((bf16[128,2,4224]{2,1,0:T(2,128)(2,1)}), bf16[128,2,4224]{2,1,0:T(2,128)(2,1)}, u32[]{:S(2)}, u32[]{:S(2)}) async-start(bf16[128,2,4224]{2,1,0:T(2,128)(2,1)} %reshape.43), calls=%async_computation.1 | async-start | bytes 4325376 | tf_op jit(solution)/shard_map/all_to_all | solution.py:174
  190.4 74.8 %reduce-scatter.3.cloned.1.call-start = ((), (), s32[]{:S(2)}) async-start(), calls=%async_computation.6 | async-start | bytes 3932160 | tf_op jit(solution)/shard_map/reduce_scatter | solution.py:246
  216.7 48.5 %collective-permute-start.1 = (bf16[512,768]{1,0:T(8,128)(2,1)}, bf16[512,768]{1,0:T(8,128)(2,1)S(1)}, u32[]{:S(2)}, u32[]{:S(2)}) collective-permute-start(bf16[512,768]{1,0:T(8,128)(2,1)} %reduce-scatter.5.cloned.1.call-done), channel_id=1, source_target_pairs={{0,256},{4,260},{8,264},{12,268},{16,272},{20,276},{24,280},{28,28... | collective-permute-start | bytes 2359304 | tf_op jit(solution)/shard_map/ppermute | solution.py:247
Sparse Core Ops, SparseCore 0:
  41.2 48.1 all-gather.2
  92.0 47.4 all-gather.4
  176.8 39.8 reduce-scatter.4
  219.4 45.7 reduce-scatter.2

commit v3 on v2

v3 whole, which is shorter than its diff:
```python
import jax
import jax.numpy as jnp
from jax import lax
from jax.experimental import pallas as pl
from jax.experimental.pallas import tpu as pltpu
from jax.sharding import PartitionSpec as P

BF = jnp.bfloat16
F32 = jnp.float32
VMEM_BYTES = 40 * 1024 * 1024
VMEM_MOST = 56 * 1024 * 1024
TAIL = 128


def params(limit=VMEM_BYTES):
    return pltpu.CompilerParams(vmem_limit_bytes=limit)


def whole():
    return pl.BlockSpec(memory_space=pltpu.VMEM)


def in_hbm():
    return pl.BlockSpec(memory_space=pltpu.HBM)


def scalars():
    return pl.BlockSpec(memory_space=pltpu.SMEM)


def iota(shape, dim):
    return lax.broadcasted_iota(jnp.int32, shape, dim)


def mm(a, b, ca=1, cb=0):
    return lax.dot_general(a, b, (((ca,), (cb,)), ((), ())), preferred_element_type=F32)


def by_token_and_route(tokens, routes, top):
    shape = (tokens, routes)
    return (iota(shape, 0) == (iota(shape, 1) // top)).astype(BF)


def to_row(per_rank, owner, top):
    routes = owner.shape[1]
    spread = mm(per_rank.astype(F32).astype(BF), owner)
    mine = iota((top, routes), 0) == (iota((top, routes), 1) % top)
    return jnp.sum(jnp.where(mine, spread, 0.0), axis=0, keepdims=True)


def from_row(row, owner, top):
    routes = owner.shape[1]
    mine = iota((top, routes), 0) == (iota((top, routes), 1) % top)
    rest = jnp.where(mine, row, 0.0)
    total = None
    for _ in range(3):
        piece = rest.astype(BF)
        rest = rest - piece.astype(F32)
        term = mm(piece, owner, 1, 1)
        total = term if total is None else total + term
    return total


def copies(sems, *pairs):
    made = [pltpu.make_async_copy(src, dst, sems.at[i]) for i, (src, dst) in enumerate(pairs)]
    for one in made:
        one.start()
    return made


def route_targets(routes_row, owner, slot_row, cap_row):
    experts = slot_row.shape[1]
    tokens, routes = owner.shape
    named = iota((experts, routes), 0) == routes_row
    chosen = mm(named.astype(BF), owner, 1, 1)
    before = (iota((tokens, tokens), 0) < iota((tokens, tokens), 1)).astype(BF)
    earlier = mm(mm(chosen.astype(BF), before).astype(BF), owner)
    rank = jnp.sum(jnp.where(named, earlier, 0.0), axis=0, keepdims=True).astype(jnp.int32)
    square = (experts, experts)
    slot_col = jnp.sum(
        jnp.where(iota(square, 0) == iota(square, 1), slot_row, 0), axis=1, keepdims=True
    )
    cap_col = jnp.sum(jnp.where(iota(square, 1) == slot_col, cap_row, 0), axis=1, keepdims=True)
    slot = jnp.sum(jnp.where(named, slot_col, 0), axis=0, keepdims=True)
    cap = jnp.sum(jnp.where(named, cap_col, 0), axis=0, keepdims=True)
    kept = rank < cap
    far = rank >= 4
    place = jnp.where(far, 7 - rank, rank)
    half = experts // 2
    dest = jnp.where(far, jnp.where(slot >= half, slot - half, slot + half), slot)
    inner = jnp.where(kept & (place < 2), dest * 2 + place, -1)
    outer = jnp.where(kept & (place >= 2), dest * 2 + place - 2, -1)
    return inner, outer


def pack(
    routes_hbm, weight_hbm, slot_hbm, cap_hbm, tokens_hbm, cot_hbm, out_hbm, target_ref, scaled_ref,
    routes, weight, slot, cap, tokens, cot, out, sems, out_sems,
):
    top, n_tokens = routes.shape
    n_routes = top * n_tokens
    width = tokens.shape[1]
    hidden = cot.shape[1]
    part = width + hidden
    loads = copies(
        sems, (routes_hbm, routes), (slot_hbm, slot), (cap_hbm, cap), (weight_hbm, weight),
        (tokens_hbm, tokens), (cot_hbm, cot),
    )
    owner = by_token_and_route(n_tokens, n_routes, top)
    for one in loads[:4]:
        one.wait()
    routes_row = to_row(routes[...], owner, top).astype(jnp.int32)
    weight_row = to_row(weight[...], owner, top)
    scaled_ref[...] = weight_row
    targets = route_targets(routes_row, owner, slot[...], cap[...])
    target_ref[0:1, :] = targets[0]
    target_ref[1:2, :] = targets[1]
    rows = out.shape[0] * out.shape[1]
    loads[4].wait()
    stores = []
    for i, target in enumerate(targets):
        hit = iota((rows, n_routes), 0) == target
        pick = mm(hit.astype(BF), owner, 1, 1).astype(BF)
        start = i * part
        moved = mm(pick, tokens[...]).astype(BF)
        out[:, :, start : start + width] = moved.reshape(rows // 2, 2, width)
        if i == 0:
            loads[5].wait()
        moved = mm(jnp.where(hit, weight_row, 0.0).astype(BF), cot[...]).astype(BF)
        out[:, :, start + width : start + part] = moved.reshape(rows // 2, 2, hidden)
        span = pl.ds(start, part)
        store = pltpu.make_async_copy(out.at[:, :, span], out_hbm.at[:, :, span], out_sems.at[i])
        store.start()
        stores.append(store)
    for one in stores:
        one.wait()


def split_router(router, lane):
    high = router.astype(BF).astype(F32)
    low = router - high
    lanes = iota((router.shape[0], TAIL), 1)
    return jnp.where(lanes == lane, high, jnp.where(lanes == lane + 1, low, 0.0))


def serve(rows, scaled, weights):
    hidden = weights.shape[1] // 2
    pre = mm(rows, weights[...])
    scaled = scaled.astype(F32)
    gate = pre[:, :hidden]
    up = pre[:, hidden:]
    sig = jax.nn.sigmoid(gate)
    active = gate * sig
    grad_up = scaled * active
    grad_gate = scaled * up * sig * (1.0 + gate * (1.0 - sig))
    grad = jnp.concatenate([grad_gate, grad_up], axis=1).astype(BF)
    router = jnp.sum(grad_up * up, axis=1, keepdims=True)
    back = mm(grad, weights[...], 1, 1).astype(BF)
    return grad, router, back


def serve_all(
    cap_ref, recv_hbm, own_hbm, partner_hbm, back_hbm, rows_hbm, grad_hbm,
    recv, own, other, back, all_rows, all_grads, sems, out_sems,
):
    width = own.shape[0]
    hidden = own.shape[1] // 2
    part = width + hidden
    sources = recv.shape[0]
    rows = 2 * sources
    chunks, _, chunk = all_rows.shape
    is_own = cap_ref[0] > 2
    spans = [pl.ds(0, part), pl.ds(part, part)]
    views = [(recv_hbm.at[:, :, s], recv.at[:, :, s]) for s in spans]
    loads = copies(sems, views[0], (own_hbm, own), views[1])

    @pl.when(is_own)
    def _():
        pltpu.make_async_copy(own_hbm, other, sems.at[3]).start()

    @pl.when(jnp.logical_not(is_own))
    def _():
        pltpu.make_async_copy(partner_hbm, other, sems.at[3]).start()

    stores = []

    def store(src, dst):
        one = pltpu.make_async_copy(src, dst, out_sems.at[len(stores)])
        one.start()
        stores.append(one)

    tail = None
    for i, weights in enumerate((own, other)):
        start = i * part
        span = pl.ds(i * rows, rows)
        loads[2 * i].wait()
        tokens = recv[:, :, start : start + width].reshape(rows, width)
        for c in range(chunks):
            all_rows[c, i * rows : (i + 1) * rows, :] = tokens[:, c * chunk : (c + 1) * chunk]
        store(all_rows.at[:, span, :], rows_hbm.at[:, span, :])
        scaled = recv[:, :, start + width : start + part].reshape(rows, hidden)
        if i == 0:
            loads[1].wait()
        else:
            pltpu.make_async_copy(own_hbm, other, sems.at[3]).wait()
        grad, router, result = serve(tokens, scaled, weights)
        all_grads[i * rows : (i + 1) * rows, :] = grad
        store(all_grads.at[span, :], grad_hbm.at[span, :])
        back[:, :, i * width : (i + 1) * width] = result.reshape(sources, 2, width)
        wide = width
        lanes = split_router(router, 2 * i)
        tail = lanes if tail is None else tail + lanes
        if i == 1:
            wide = width + TAIL
            back[:, :, 2 * width :] = tail.astype(BF).reshape(sources, 2, TAIL)
        out_span = pl.ds(i * width, wide)
        store(back.at[:, :, out_span], back_hbm.at[:, :, out_span])
    for one in stores:
        one.wait()


def weight_grads(cap_ref, me_ref, rows_0, rows_1, rows_2, rows_3, grads, own_ref, far_ref):
    received = (rows_0, rows_1, rows_2, rows_3)
    sources = len(received)
    half = rows_0.shape[0] // 2
    is_own = cap_ref[0] > 2
    inner = None
    outer = None
    for k, rows in enumerate(received):
        source = lax.rem(me_ref[0] + sources - k, sources)
        term = mm(rows[:half, :], grads[source, :half, :], 0, 0)
        inner = term if inner is None else inner + term
        term = mm(rows[half:, :], grads[source, half:, :], 0, 0)
        outer = term if outer is None else outer + term
    own_ref[...] = inner + jnp.where(is_own, outer, 0.0)
    far_ref[...] = jnp.where(is_own, 0.0, outer).astype(BF)


def unpack(target_ref, scaled_ref, back, token_ref, router_ref):
    n_tokens, width = token_ref.shape
    top = router_ref.shape[0]
    n_routes = top * n_tokens
    rows = 2 * back.shape[0]
    owner = by_token_and_route(n_tokens, n_routes, top)
    hits = [
        (iota((rows, n_routes), 0) == target_ref[i : i + 1, :]).astype(BF) for i in range(2)
    ]
    picks = [mm(owner, hit, 1, 1).astype(BF) for hit in hits]
    tail = back[:, :, 2 * width :].reshape(rows, TAIL)
    router = None
    for i, hit in enumerate(hits):
        found = mm(tail, hit, 0, 0)
        value = found[2 * i : 2 * i + 1, :] + found[2 * i + 1 : 2 * i + 2, :]
        router = value if router is None else router + value
    router_ref[...] = from_row(router / scaled_ref[...], owner, top)
    total = None
    for i, pick in enumerate(picks):
        term = mm(pick, back[:, :, i * width : (i + 1) * width].reshape(rows, width))
        total = term if total is None else total + term
    token_ref[...] = total.astype(BF)


def call(kernel, out, in_specs, out_specs, scratch, flops, moved, *args, limit=VMEM_BYTES):
    return pl.pallas_call(
        kernel,
        out_shape=[jax.ShapeDtypeStruct(s, d) for s, d in out],
        in_specs=in_specs,
        out_specs=out_specs,
        scratch_shapes=scratch,
        compiler_params=params(limit),
        cost_estimate=pl.CostEstimate(flops=flops, bytes_accessed=moved, transcendentals=0),
    )(*args)


def exchange(value):
    return lax.all_to_all(value, "expert", split_axis=0, concat_axis=0, tiled=True)


def local(tokens, cotangent, routes, route_weight, expert_slot, capacity, gate_up):
    count = lax.axis_size("expert")
    n_tokens, width = tokens.shape
    top = routes.shape[1]
    hidden = cotangent.shape[2]
    n_routes = n_tokens * top
    rows = 2 * count
    part = width + hidden
    my_cap = lax.dynamic_slice(capacity, (lax.axis_index("expert"),), (1,))
    swap = [(s, (s + count // 2) % count) for s in range(count)]
    dma = pltpu.SemaphoreType.DMA

    own_weights = lax.all_gather(gate_up, "dp", axis=1, tiled=True)[0]
    partner_shard = lax.ppermute(gate_up, "expert", swap)
    partner_weights = lax.all_gather(partner_shard, "dp", axis=1, tiled=True)[0]
    send, target, scaled = call(
        pack,
        [((count, 2, 2 * part), BF), ((2, n_routes), jnp.int32), ((1, n_routes), F32)],
        [in_hbm()] * 6,
        [in_hbm(), whole(), whole()],
        [
            pltpu.VMEM((top, n_tokens), jnp.int32),
            pltpu.VMEM((top, n_tokens), F32),
            pltpu.VMEM((1, count), jnp.int32),
            pltpu.VMEM((1, count), jnp.int32),
            pltpu.VMEM((n_tokens, width), BF),
            pltpu.VMEM((n_routes, hidden), BF),
            pltpu.VMEM((count, 2, 2 * part), BF),
            dma((6,)),
            dma((2,)),
        ],
        4 * rows * n_routes * (hidden + 2 * n_tokens),
        4 << 20,
        routes.T,
        route_weight.T,
        expert_slot.reshape(1, count),
        capacity.reshape(1, count),
        tokens,
        cotangent.reshape(n_routes, hidden),
        limit=VMEM_MOST,
    )
    recv = exchange(send)
    replicas = lax.axis_size("dp")
    chunk = width // replicas
    send_back, sent_rows, grads = call(
        serve_all,
        [
            ((count, 2, 2 * width + TAIL), BF),
            ((replicas, 2 * rows, chunk), BF),
            ((2 * rows, 2 * hidden), BF),
        ],
        [scalars()] + [in_hbm()] * 3,
        [in_hbm()] * 3,
        [
            pltpu.VMEM((count, 2, 2 * part), BF),
            pltpu.VMEM((width, 2 * hidden), BF),
            pltpu.VMEM((width, 2 * hidden), BF),
            pltpu.VMEM((count, 2, 2 * width + TAIL), BF),
            pltpu.VMEM((replicas, 2 * rows, chunk), BF),
            pltpu.VMEM((2 * rows, 2 * hidden), BF),
            dma((4,)),
            dma((6,)),
        ],
        16 * rows * width * hidden,
        12 << 20,
        my_cap,
        recv,
        own_weights,
        partner_weights,
        limit=VMEM_MOST,
    )
    back = exchange(send_back)
    all_grads = lax.all_gather(grads, "dp", axis=0, tiled=False)
    me = lax.axis_index("dp")
    received = []
    for k in range(replicas):
        piece = lax.dynamic_index_in_dim(
            sent_rows, lax.rem(me + k, replicas), axis=0, keepdims=False
        )
        if k:
            piece = lax.ppermute(piece, "dp", [(q, (q + k) % replicas) for q in range(replicas)])
        received.append(piece)
    shard = (chunk, 2 * hidden)
    own_shard, far_shard = call(
        weight_grads,
        [(shard, F32), (shard, BF)],
        [scalars(), scalars()] + [whole()] * 5,
        [whole()] * 2,
        [],
        8 * replicas * rows * chunk * hidden,
        8 << 20,
        my_cap,
        me.reshape(1),
        *received,
        all_grads,
    )
    moved_shard = lax.ppermute(far_shard, "expert", swap)
    gate_up_grad = (own_shard + moved_shard.astype(F32)).astype(BF)[None]

    token_grad, router = call(
        unpack,
        [((n_tokens, width), BF), ((top, n_tokens), F32)],
        [whole()] * 3,
        [whole()] * 2,
        [],
        4 * rows * n_routes * 2 * n_tokens,
        4 << 20,
        target,
        scaled,
        back,
    )
    return token_grad, router.T, gate_up_grad


def solution(mesh):
    in_specs = (
        P(("expert", "dp"), None),
        P(("expert", "dp"), None, None),
        P(("expert", "dp"), None),
        P(("expert", "dp"), None),
        P(),
        P(),
        P("expert", "dp", None),
    )
    out_specs = (P(("expert", "dp"), None), P(("expert", "dp"), None), P("expert", "dp", None))
    return jax.shard_map(local, mesh=mesh, in_specs=in_specs, out_specs=out_specs, check_vma=False)
```

time: 306 us -> 281 us (0.918)
  waiting for transfers between devices: 203 us -> 185 us
  local copies, waits for them, and re-layouts: 22.3 us -> 9.35 us
  starting transfers between devices: 40.8 us -> 51 us
    all_to_all x2, waiting for transfers between devices: 110 us -> 22.6 us  [exchange(): lax.all_to_all(value, 'expert', split_axis=0, concat_axis=0, tiled=True)]
    reduce_scatter x2 -> x0, waiting for transfers between devices: 69.6 us -> none  [the longest x1 43.8 us: local(): lax.psum_scatter(own_part, 'dp', scatter_dimension=0, tiled=True)]
    all_gather x1, waiting for transfers between devices: 0.02 us -> 49.6 us  [local(): partner_weights = lax.all_gather(partner_shard, 'dp', axis=1, tiled=True)[0]]
    ppermute x0 -> x3, waiting for transfers between devices: none -> 26.6 us  [local(): lax.ppermute(piece, 'dp', [(q, (q + k) % replicas) for q in range(replica...]
    ppermute x1, waiting for transfers between devices: 0.01 us -> 22.5 us  [local(): moved_shard = lax.ppermute(far_shard, 'expert', swap)]
    all_gather x1, waiting for transfers between devices: 0.02 us -> 22.4 us  [local(): own_weights = lax.all_gather(gate_up, 'dp', axis=1, tiled=True)[0]]
    all_gather x0 -> x1, waiting for transfers between devices: none -> 17.7 us  [local(): all_grads = lax.all_gather(grads, 'dp', axis=0, tiled=False)]
    reshape x7 -> x0, local copies, waits for them, and re-layouts: 13 us -> none  [the longest x2 7.98 us: exchange(): lax.all_to_all(one, 'expert', split_axis=0, concat_axis=0, tiled=True)]
  transfers between devices with their start and end apart: 8 -> 10, of which waited for: 5 -> 10; matrix products, arithmetic and copies ran while one was open for 3% -> 1% of each run, Pallas kernels for 0% -> 1%
where the time goes in v3:
time: 281 us; the launch traced here: 280 us
  waiting for transfers between devices  185 us (66%)
  starting transfers between devices  51 us (18%)
  Pallas kernels  20 us (7%)
  between operations  13.9 us (5%)
  local copies, waits for them, and re-layouts  9.35 us (3%)
    all_gather x1, waiting for transfers between devices, local(): partner_weights = lax.all_gather(partner_shard, 'dp', axis=1, tiled=True)[0]  49.6 us
    all_to_all x2, starting transfers between devices, exchange(): lax.all_to_all(value, 'expert', split_axis=0, concat_axis=0, tiled=True)  29.9 us
    ppermute x3, waiting for transfers between devices, local(): lax.ppermute(piece, 'dp', [(q, (q + k) % replicas) for q in range(replica...  26.6 us
    all_to_all x2, waiting for transfers between devices, exchange(): lax.all_to_all(value, 'expert', split_axis=0, concat_axis=0, tiled=True)  22.6 us
    ppermute x1, waiting for transfers between devices, local(): moved_shard = lax.ppermute(far_shard, 'expert', swap)  22.5 us
    all_gather x1, waiting for transfers between devices, local(): own_weights = lax.all_gather(gate_up, 'dp', axis=1, tiled=True)[0]  22.4 us
    ppermute x1, waiting for transfers between devices, local(): partner_shard = lax.ppermute(gate_up, 'expert', swap)  22.1 us
    pallas_call x4, Pallas kernels, call(): pl.pallas_call(kernel, out_shape=[jax.ShapeDtypeStruct(s, d) for s, d in...  20 us
  transfers between devices with their start and end apart: 10, of which 10 were waited for; matrix products, arithmetic and copies ran while one was open for 1% of the time, Pallas kernels for 1%

profile of v3, /device:TPU:1, one launch (start us, length us, event | category | flops | bytes accessed | tf_op | source)
XLA Modules:
  0.0 280.2 jit_solution(2587990004060821299)
XLA Ops:
  7.2 5.7 %shard_map.94 = (bf16[128,2,4864]{2,1,0:T(2,128)(2,1)}, s32[2,1024]{1,0:T(2,128)}, f32[1,1024]{1,0:T(1,128)}) custom-call(s32[8,128]{1,0:T(8,128)} %bitcast.24, f32[8,128]{1,0:T(8,128)} %bitcast.25, s32[1,128]{1,0:T(1,128)} %bitcast.27, s32[1,128]{1,0:T(1,128)} %bitcast.28, bf16[128,2048]{1,0:T(8,128)(2,1)} %tokens_hbm.1, bf16[1024,384]{1,0:T(8,128)(2,1)} %bitcast.23), custom_call_target="tpu_custom_call" | custom-call | flops 671088640 | bytes 4194304 | tf_op jit(solution)/shard_map/pallas_call | solution.py:264
  12.9 0.0 copy-start.8
  12.9 0.0 copy-start.9
  12.9 20.7 %all-to-all-start = ((bf16[128,2,4864]{2,1,0:T(2,128)(2,1)}), bf16[128,2,4864]{2,1,0:T(2,128)(2,1)S(1)}, u32[]{:S(2)}, u32[]{:S(2)}) async-start(bf16[128,2,4864]{2,1,0:T(2,128)(2,1)} %get-tuple-element.15), calls=%async_computation | async-start | bytes 4980736 | tf_op jit(solution)/shard_map/all_to_all | solution.py:276
  33.6 0.0 all-gather.5.cloned.1.call-start
  33.6 0.7 all-gather.5.cloned.1.call-update
  34.3 0.0 all-gather.7.cloned.1.call-start
  34.4 0.0 copy-done.8
  34.4 5.1 %collective-permute-start = (bf16[1,512,768]{2,1,0:T(8,128)(2,1)S(1)}, bf16[1,512,768]{2,1,0:T(8,128)(2,1)}, u32[]{:S(2)}, u32[]{:S(2)}) collective-permute-start(bf16[1,512,768]{2,1,0:T(8,128)(2,1)S(1)} %copy-done.8), channel_id=1, source_target_pairs={{0,256},{4,260},{8,264},{12,268},{16,272},{20,276},{24,280},{28,28... | collective-permute-start | bytes 2359304 | tf_op jit(solution)/shard_map/ppermute | solution.py:292
  39.5 22.1 %collective-permute-done = bf16[1,512,768]{2,1,0:T(8,128)(2,1)} collective-permute-done((bf16[1,512,768]{2,1,0:T(8,128)(2,1)S(1)}, bf16[1,512,768]{2,1,0:T(8,128)(2,1)}, u32[]{:S(2)}, u32[]{:S(2)}) %collective-permute-start) | collective-permute-done | bytes 786464 | tf_op jit(solution)/shard_map/ppermute | solution.py:292
  61.7 0.0 all-gather.7.cloned.1.call-update
  61.7 0.0 copy-done.9
  61.7 0.6 dynamic_slice.16.cap_ref
  62.3 22.4 %all-gather.5.cloned.1.call-done = bf16[1,2048,768]{2,1,0:T(8,128)(2,1)} async-done(((bf16[1,512,768]{2,1,0:T(8,128)(2,1)}), bf16[1,2048,768]{2,1,0:T(8,128)(2,1)}) %all-gather.5.cloned.1.call-update) | async-done | bytes 3145744 | tf_op jit(solution)/shard_map/all_gather | solution.py:291
  84.7 49.6 %all-gather.7.cloned.1.call-done = bf16[1,2048,768]{2,1,0:T(8,128)(2,1)} async-done(((bf16[1,512,768]{2,1,0:T(8,128)(2,1)}), bf16[1,2048,768]{2,1,0:T(8,128)(2,1)}) %all-gather.7.cloned.1.call-update) | async-done | bytes 3145744 | tf_op jit(solution)/shard_map/all_gather | solution.py:293
  134.3 14.8 %all-to-all-done.recv_hbm = bf16[128,2,4864]{2,1,0:T(2,128)(2,1)S(1)} async-done(((bf16[128,2,4864]{2,1,0:T(2,128)(2,1)}), bf16[128,2,4864]{2,1,0:T(2,128)(2,1)S(1)}, u32[]{:S(2)}, u32[]{:S(2)}) %all-to-all-start) | async-done | bytes 2490400 | tf_op jit(solution)/shard_map/all_to_all | solution.py:276
  149.1 0.0 copy-start.7
  149.1 1.5 copy-done.7
  150.6 9.7 %shard_map.95 = (bf16[128,2,4224]{2,1,0:T(2,128)(2,1)}, bf16[4,512,512]{2,1,0:T(8,128)(2,1)}, bf16[512,768]{1,0:T(8,128)(2,1)}) custom-call(s32[1]{0:T(128)} %dynamic_slice.16.cap_ref, bf16[128,2,4864]{2,1,0:T(2,128)(2,1)} %copy-done.7, bf16[2048,768]{1,0:T(8,128)(2,1)} %bitcast.21, bf16[2048,768]{1,0:T(8,128)(2,1)} %bitcast.22), custom_call_target="tpu_custom_call" | custom-call | flops 3221225472 | bytes 12582912 | tf_op jit(solution)/shard_map/pallas_call | solution.py:264
  160.3 9.2 %all-to-all-start.1 = ((bf16[128,2,4224]{2,1,0:T(2,128)(2,1)}), bf16[128,2,4224]{2,1,0:T(2,128)(2,1)S(1)}, u32[]{:S(2)}, u32[]{:S(2)}) async-start(bf16[128,2,4224]{2,1,0:T(2,128)(2,1)} %get-tuple-element.16), calls=%async_computation.1 | async-start | bytes 4325376 | tf_op jit(solution)/shard_map/all_to_all | solution.py:276
  169.5 0.0 all-gather.9.cloned.1.call-start
  169.6 0.7 all-gather.9.cloned.1.call-update
  170.3 1.7 dynamic-slice_bitcast_fusion
  172.0 3.3 %collective-permute-start.1 = (bf16[512,512]{1,0:T(8,128)(2,1)S(1)}, bf16[512,512]{1,0:T(8,128)(2,1)S(1)}, u32[]{:S(2)}, u32[]{:S(2)}) collective-permute-start(bf16[512,512]{1,0:T(8,128)(2,1)S(1)} %get-tuple-element.25), channel_id=1, source_target_pairs={{0,1},{1,2},{2,3},{3,0},{4,5},{5,6},{6,7},{7,4},{8,9},{9,10},{10,1... | collective-permute-start | bytes 1572872 | tf_op jit(solution)/shard_map/ppermute | solution.py:359
  175.3 4.4 %collective-permute-start.2 = (bf16[512,512]{1,0:T(8,128)(2,1)S(1)}, bf16[512,512]{1,0:T(8,128)(2,1)S(1)}, u32[]{:S(2)}, u32[]{:S(2)}) collective-permute-start(bf16[512,512]{1,0:T(8,128)(2,1)S(1)} %get-tuple-element.24), channel_id=1, source_target_pairs={{0,2},{1,3},{2,0},{3,1},{4,6},{5,7},{6,4},{7,5},{8,10},{9,11},{10,... | collective-permute-start | bytes 1572872 | tf_op jit(solution)/shard_map/ppermute | solution.py:359
  179.7 3.1 %collective-permute-start.3 = (bf16[512,512]{1,0:T(8,128)(2,1)S(1)}, bf16[512,512]{1,0:T(8,128)(2,1)S(1)}, u32[]{:S(2)}, u32[]{:S(2)}) collective-permute-start(bf16[512,512]{1,0:T(8,128)(2,1)S(1)} %get-tuple-element.23), channel_id=1, source_target_pairs={{0,3},{1,0},{2,1},{3,2},{4,7},{5,4},{6,5},{7,6},{8,11},{9,8},{10,9... | collective-permute-start | bytes 1572872 | tf_op jit(solution)/shard_map/ppermute | solution.py:359
  182.7 4.9 %collective-permute-done.1.rows_1 = bf16[512,512]{1,0:T(8,128)(2,1)S(1)} collective-permute-done((bf16[512,512]{1,0:T(8,128)(2,1)S(1)}, bf16[512,512]{1,0:T(8,128)(2,1)S(1)}, u32[]{:S(2)}, u32[]{:S(2)}) %collective-permute-start.1) | collective-permute-done | bytes 524320 | tf_op jit(solution)/shard_map/ppermute | solution.py:359
  187.6 15.8 %collective-permute-done.2.rows_2 = bf16[512,512]{1,0:T(8,128)(2,1)S(1)} collective-permute-done((bf16[512,512]{1,0:T(8,128)(2,1)S(1)}, bf16[512,512]{1,0:T(8,128)(2,1)S(1)}, u32[]{:S(2)}, u32[]{:S(2)}) %collective-permute-start.2) | collective-permute-done | bytes 524320 | tf_op jit(solution)/shard_map/ppermute | solution.py:359
  203.5 0.0 copy-start.3
  203.5 0.8 copy-done.3
  204.3 5.8 %collective-permute-done.3.rows_3 = bf16[512,512]{1,0:T(8,128)(2,1)S(1)} collective-permute-done((bf16[512,512]{1,0:T(8,128)(2,1)S(1)}, bf16[512,512]{1,0:T(8,128)(2,1)S(1)}, u32[]{:S(2)}, u32[]{:S(2)}) %collective-permute-start.3) | collective-permute-done | bytes 524320 | tf_op jit(solution)/shard_map/ppermute | solution.py:359
  210.1 0.0 copy-start.5
  210.1 0.8 copy-done.5
  210.9 17.7 %all-gather.9.cloned.1.call-done = bf16[2048,768]{1,0:T(8,128)(2,1)} async-done(((bf16[512,768]{1,0:T(8,128)(2,1)}), bf16[2048,768]{1,0:T(8,128)(2,1)}) %all-gather.9.cloned.1.call-update) | async-done | bytes 3145744 | tf_op jit(solution)/shard_map/all_gather | solution.py:351
  228.6 0.0 copy-start.2
  228.6 1.9 copy-done.2
  230.5 1.0 copy-done.4
  231.5 1.0 copy-done.6
  232.5 2.5 shard_map.97
  235.0 0.0 copy-start
  235.0 0.0 copy-start.1
  235.1 5.1 %collective-permute-start.4 = (bf16[512,768]{1,0:T(8,128)(2,1)S(1)}, bf16[512,768]{1,0:T(8,128)(2,1)S(1)}, u32[]{:S(2)}, u32[]{:S(2)}) collective-permute-start(bf16[512,768]{1,0:T(8,128)(2,1)S(1)} %get-tuple-element.22), channel_id=1, source_target_pairs={{0,256},{4,260},{8,264},{12,268},{16,272},{20,276},{24,280},{28,28... | collective-permute-start | bytes 2359304 | tf_op jit(solution)/shard_map/ppermute | solution.py:375
  240.2 22.5 %collective-permute-done.4 = bf16[512,768]{1,0:T(8,128)(2,1)S(1)} collective-permute-done((bf16[512,768]{1,0:T(8,128)(2,1)S(1)}, bf16[512,768]{1,0:T(8,128)(2,1)S(1)}, u32[]{:S(2)}, u32[]{:S(2)}) %collective-permute-start.4) | collective-permute-done | bytes 786464 | tf_op jit(solution)/shard_map/ppermute | solution.py:375
  262.6 1.0 fusion
  263.7 7.8 %all-to-all-done.1.back = bf16[128,2,4224]{2,1,0:T(2,128)(2,1)S(1)} async-done(((bf16[128,2,4224]{2,1,0:T(2,128)(2,1)}), bf16[128,2,4224]{2,1,0:T(2,128)(2,1)S(1)}, u32[]{:S(2)}, u32[]{:S(2)}) %all-to-all-start.1) | async-done | bytes 2162720 | tf_op jit(solution)/shard_map/all_to_all | solution.py:276
  271.5 0.0 copy-done
  271.5 0.0 copy-done.1
  271.5 2.2 shard_map.96
  (2 shorter events, 0.0 us)
Async XLA Ops:
  12.9 21.5 %copy-start.8 = (bf16[1,512,768]{2,1,0:T(8,128)(2,1)S(1)}, bf16[1,512,768]{2,1,0:T(8,128)(2,1)}, u32[]{:S(2)}) copy-start(bf16[1,512,768]{2,1,0:T(8,128)(2,1)} %param.13) | copy-start | bytes 2359300
  12.9 48.8 %copy-start.9 = (s32[128]{0:T(128)S(1)}, s32[128]{0:T(128)}, u32[]{:S(2)}) copy-start(s32[128]{0:T(128)} %param.12) | copy-start | bytes 1540
  12.9 136.2 %all-to-all-start = ((bf16[128,2,4864]{2,1,0:T(2,128)(2,1)}), bf16[128,2,4864]{2,1,0:T(2,128)(2,1)S(1)}, u32[]{:S(2)}, u32[]{:S(2)}) async-start(bf16[128,2,4864]{2,1,0:T(2,128)(2,1)} %get-tuple-element.15), calls=%async_computation | async-start | bytes 4980736 | tf_op jit(solution)/shard_map/all_to_all | solution.py:276
  33.6 51.1 %all-gather.5.cloned.1.call-start = ((), (), s32[]{:S(2)}) async-start(), calls=%async_computation.2 | async-start | bytes 3932160 | tf_op jit(solution)/shard_map/all_gather | solution.py:291
  34.3 100.0 %all-gather.7.cloned.1.call-start = ((), (), s32[]{:S(2)}) async-start(), calls=%async_computation.3 | async-start | bytes 3932160 | tf_op jit(solution)/shard_map/all_gather | solution.py:293
  34.4 27.3 %collective-permute-start = (bf16[1,512,768]{2,1,0:T(8,128)(2,1)S(1)}, bf16[1,512,768]{2,1,0:T(8,128)(2,1)}, u32[]{:S(2)}, u32[]{:S(2)}) collective-permute-start(bf16[1,512,768]{2,1,0:T(8,128)(2,1)S(1)} %copy-done.8), channel_id=1, source_target_pairs={{0,256},{4,260},{8,264},{12,268},{16,272},{20,276},{24,280},{28,28... | collective-permute-start | bytes 2359304 | tf_op jit(solution)/shard_map/ppermute | solution.py:292
  149.1 1.5 copy-start.7
  160.3 111.1 %all-to-all-start.1 = ((bf16[128,2,4224]{2,1,0:T(2,128)(2,1)}), bf16[128,2,4224]{2,1,0:T(2,128)(2,1)S(1)}, u32[]{:S(2)}, u32[]{:S(2)}) async-start(bf16[128,2,4224]{2,1,0:T(2,128)(2,1)} %get-tuple-element.16), calls=%async_computation.1 | async-start | bytes 4325376 | tf_op jit(solution)/shard_map/all_to_all | solution.py:276
  169.5 59.0 %all-gather.9.cloned.1.call-start = ((), (), s32[]{:S(2)}) async-start(), calls=%async_computation.4 | async-start | bytes 3932160 | tf_op jit(solution)/shard_map/all_gather | solution.py:351
  172.0 15.6 %collective-permute-start.1 = (bf16[512,512]{1,0:T(8,128)(2,1)S(1)}, bf16[512,512]{1,0:T(8,128)(2,1)S(1)}, u32[]{:S(2)}, u32[]{:S(2)}) collective-permute-start(bf16[512,512]{1,0:T(8,128)(2,1)S(1)} %get-tuple-element.25), channel_id=1, source_target_pairs={{0,1},{1,2},{2,3},{3,0},{4,5},{5,6},{6,7},{7,4},{8,9},{9,10},{10,1... | collective-permute-start | bytes 1572872 | tf_op jit(solution)/shard_map/ppermute | solution.py:359
  175.3 28.2 %collective-permute-start.2 = (bf16[512,512]{1,0:T(8,128)(2,1)S(1)}, bf16[512,512]{1,0:T(8,128)(2,1)S(1)}, u32[]{:S(2)}, u32[]{:S(2)}) collective-permute-start(bf16[512,512]{1,0:T(8,128)(2,1)S(1)} %get-tuple-element.24), channel_id=1, source_target_pairs={{0,2},{1,3},{2,0},{3,1},{4,6},{5,7},{6,4},{7,5},{8,10},{9,11},{10,... | collective-permute-start | bytes 1572872 | tf_op jit(solution)/shard_map/ppermute | solution.py:359
  179.7 30.4 %collective-permute-start.3 = (bf16[512,512]{1,0:T(8,128)(2,1)S(1)}, bf16[512,512]{1,0:T(8,128)(2,1)S(1)}, u32[]{:S(2)}, u32[]{:S(2)}) collective-permute-start(bf16[512,512]{1,0:T(8,128)(2,1)S(1)} %get-tuple-element.23), channel_id=1, source_target_pairs={{0,3},{1,0},{2,1},{3,2},{4,7},{5,4},{6,5},{7,6},{8,11},{9,8},{10,9... | collective-permute-start | bytes 1572872 | tf_op jit(solution)/shard_map/ppermute | solution.py:359
  203.5 0.8 copy-start.3
  210.1 0.8 copy-start.5
  228.6 1.9 copy-start.2
  230.5 1.0 copy-start.4
  231.5 1.0 copy-start.6
  235.0 36.4 %copy-start = (s32[2,1024]{1,0:T(2,128)S(1)}, s32[2,1024]{1,0:T(2,128)}, u32[]{:S(2)}) copy-start(s32[2,1024]{1,0:T(2,128)} %get-tuple-element.13.target_ref) | copy-start | bytes 24580
  235.0 36.4 %copy-start.1 = (f32[1,1024]{1,0:T(1,128)S(1)}, f32[1,1024]{1,0:T(1,128)}, u32[]{:S(2)}) copy-start(f32[1,1024]{1,0:T(1,128)} %get-tuple-element.14.scaled_ref) | copy-start | bytes 12292
  235.1 27.6 %collective-permute-start.4 = (bf16[512,768]{1,0:T(8,128)(2,1)S(1)}, bf16[512,768]{1,0:T(8,128)(2,1)S(1)}, u32[]{:S(2)}, u32[]{:S(2)}) collective-permute-start(bf16[512,768]{1,0:T(8,128)(2,1)S(1)} %get-tuple-element.22), channel_id=1, source_target_pairs={{0,256},{4,260},{8,264},{12,268},{16,272},{20,276},{24,280},{28,28... | collective-permute-start | bytes 2359304 | tf_op jit(solution)/shard_map/ppermute | solution.py:375
Sparse Core Ops, SparseCore 0:
  36.5 48.1 all-gather.4
  86.8 47.4 all-gather.6
  173.1 55.4 all-gather.8

commit v4 on v3

--- a/solution.py
+++ b/solution.py
@@ -10,6 +10,8 @@
 VMEM_BYTES = 40 * 1024 * 1024
 VMEM_MOST = 56 * 1024 * 1024
 TAIL = 128
+PIECES = 4
+VMEM_SERVE = 47 * 1024 * 1024
 
 
 def params(limit=VMEM_BYTES):
@@ -143,9 +145,15 @@
     return jnp.where(lanes == lane, high, jnp.where(lanes == lane + 1, low, 0.0))
 
 
-def serve(rows, scaled, weights):
-    hidden = weights.shape[1] // 2
-    pre = mm(rows, weights[...])
+def serve(rows, scaled, weights, loads):
+    width, hidden = weights.shape[0], weights.shape[1] // 2
+    pre = None
+    deep = width // len(loads)
+    for k, load in enumerate(loads):
+        load.wait()
+        span = slice(k * deep, (k + 1) * deep)
+        term = mm(rows[:, span], weights[span, :])
+        pre = term if pre is None else pre + term
     scaled = scaled.astype(F32)
     gate = pre[:, :hidden]
     up = pre[:, hidden:]
@@ -160,63 +168,59 @@
 
 
 def serve_all(
-    cap_ref, recv_hbm, own_hbm, partner_hbm, back_hbm, rows_hbm, grad_hbm,
-    recv, own, other, back, all_rows, all_grads, sems, out_sems,
+    cap_ref, recv, own_hbm, partner_hbm, back, grad_hbm, own, other, all_grads, sems, out_sems
 ):
     width = own.shape[0]
     hidden = own.shape[1] // 2
     part = width + hidden
     sources = recv.shape[0]
     rows = 2 * sources
-    chunks, _, chunk = all_rows.shape
     is_own = cap_ref[0] > 2
-    spans = [pl.ds(0, part), pl.ds(part, part)]
-    views = [(recv_hbm.at[:, :, s], recv.at[:, :, s]) for s in spans]
-    loads = copies(sems, views[0], (own_hbm, own), views[1])
+    deep = width // PIECES
+    pieces = [pl.ds(k * deep, deep) for k in range(PIECES)]
+    loads = copies(sems, *[(own_hbm.at[p], own.at[p]) for p in pieces])
+    last = sems.at[PIECES]
 
     @pl.when(is_own)
     def _():
-        pltpu.make_async_copy(own_hbm, other, sems.at[3]).start()
+        pltpu.make_async_copy(own_hbm, other, last).start()
 
     @pl.when(jnp.logical_not(is_own))
     def _():
-        pltpu.make_async_copy(partner_hbm, other, sems.at[3]).start()
-
+        pltpu.make_async_copy(partner_hbm, other, last).start()
+
+    ready = (loads, [pltpu.make_async_copy(own_hbm, other, last)])
     stores = []
-
-    def store(src, dst):
-        one = pltpu.make_async_copy(src, dst, out_sems.at[len(stores)])
-        one.start()
-        stores.append(one)
-
     tail = None
     for i, weights in enumerate((own, other)):
         start = i * part
+        tokens = recv[:, :, start : start + width].reshape(rows, width)
+        scaled = recv[:, :, start + width : start + part].reshape(rows, hidden)
+        grad, router, result = serve(tokens, scaled, weights, ready[i])
         span = pl.ds(i * rows, rows)
-        loads[2 * i].wait()
-        tokens = recv[:, :, start : start + width].reshape(rows, width)
-        for c in range(chunks):
-            all_rows[c, i * rows : (i + 1) * rows, :] = tokens[:, c * chunk : (c + 1) * chunk]
-        store(all_rows.at[:, span, :], rows_hbm.at[:, span, :])
-        scaled = recv[:, :, start + width : start + part].reshape(rows, hidden)
-        if i == 0:
-            loads[1].wait()
-        else:
-            pltpu.make_async_copy(own_hbm, other, sems.at[3]).wait()
-        grad, router, result = serve(tokens, scaled, weights)
         all_grads[i * rows : (i + 1) * rows, :] = grad
-        store(all_grads.at[span, :], grad_hbm.at[span, :])
+        store = pltpu.make_async_copy(all_grads.at[span], grad_hbm.at[span], out_sems.at[i])
+        store.start()
+        stores.append(store)
         back[:, :, i * width : (i + 1) * width] = result.reshape(sources, 2, width)
-        wide = width
         lanes = split_router(router, 2 * i)
         tail = lanes if tail is None else tail + lanes
-        if i == 1:
-            wide = width + TAIL
-            back[:, :, 2 * width :] = tail.astype(BF).reshape(sources, 2, TAIL)
-        out_span = pl.ds(i * width, wide)
-        store(back.at[:, :, out_span], back_hbm.at[:, :, out_span])
+    back[:, :, 2 * width :] = tail.astype(BF).reshape(sources, 2, TAIL)
     for one in stores:
         one.wait()
+
+
+def slice_rows(me_ref, recv, grads_hbm, *out_refs):
+    del grads_hbm
+    slices = len(out_refs)
+    rows = 2 * recv.shape[0]
+    part = recv.shape[2] // 2
+    chunk = out_refs[0].shape[1]
+    for k, out_ref in enumerate(out_refs):
+        column = lax.rem(me_ref[0] + k, slices) * chunk
+        for i in range(2):
+            span = pl.ds(pl.multiple_of(i * part + column, 128), chunk)
+            out_ref[i * rows : (i + 1) * rows, :] = recv[:, :, span].reshape(rows, chunk)
 
 
 def weight_grads(cap_ref, me_ref, rows_0, rows_1, rows_2, rows_3, grads, own_ref, far_ref):
@@ -276,22 +280,14 @@
     return lax.all_to_all(value, "expert", split_axis=0, concat_axis=0, tiled=True)
 
 
-def local(tokens, cotangent, routes, route_weight, expert_slot, capacity, gate_up):
-    count = lax.axis_size("expert")
-    n_tokens, width = tokens.shape
-    top = routes.shape[1]
-    hidden = cotangent.shape[2]
-    n_routes = n_tokens * top
+def pack_call(routes, weight, slot, cap, tokens, cot, count):
+    top, n_tokens = routes.shape
+    width = tokens.shape[1]
+    n_routes, hidden = cot.shape
+    part = width + hidden
     rows = 2 * count
-    part = width + hidden
-    my_cap = lax.dynamic_slice(capacity, (lax.axis_index("expert"),), (1,))
-    swap = [(s, (s + count // 2) % count) for s in range(count)]
     dma = pltpu.SemaphoreType.DMA
-
-    own_weights = lax.all_gather(gate_up, "dp", axis=1, tiled=True)[0]
-    partner_shard = lax.ppermute(gate_up, "expert", swap)
-    partner_weights = lax.all_gather(partner_shard, "dp", axis=1, tiled=True)[0]
-    send, target, scaled = call(
+    return call(
         pack,
         [((count, 2, 2 * part), BF), ((2, n_routes), jnp.int32), ((1, n_routes), F32)],
         [in_hbm()] * 6,
@@ -309,35 +305,33 @@
         ],
         4 * rows * n_routes * (hidden + 2 * n_tokens),
         4 << 20,
-        routes.T,
-        route_weight.T,
-        expert_slot.reshape(1, count),
-        capacity.reshape(1, count),
+        routes,
+        weight,
+        slot,
+        cap,
         tokens,
-        cotangent.reshape(n_routes, hidden),
+        cot,
         limit=VMEM_MOST,
     )
-    recv = exchange(send)
-    replicas = lax.axis_size("dp")
-    chunk = width // replicas
-    send_back, sent_rows, grads = call(
+
+
+def serve_call(my_cap, recv, own_weights, partner_weights):
+    count = recv.shape[0]
+    width = own_weights.shape[0]
+    hidden = own_weights.shape[1] // 2
+    rows = 2 * count
+    dma = pltpu.SemaphoreType.DMA
+    return call(
         serve_all,
+        [((count, 2, 2 * width + TAIL), BF), ((2 * rows, 2 * hidden), BF)],
+        [scalars(), whole(), in_hbm(), in_hbm()],
+        [whole(), in_hbm()],
         [
-            ((count, 2, 2 * width + TAIL), BF),
-            ((replicas, 2 * rows, chunk), BF),
-            ((2 * rows, 2 * hidden), BF),
-        ],
-        [scalars()] + [in_hbm()] * 3,
-        [in_hbm()] * 3,
-        [
-            pltpu.VMEM((count, 2, 2 * part), BF),
             pltpu.VMEM((width, 2 * hidden), BF),
             pltpu.VMEM((width, 2 * hidden), BF),
-            pltpu.VMEM((count, 2, 2 * width + TAIL), BF),
-            pltpu.VMEM((replicas, 2 * rows, chunk), BF),
             pltpu.VMEM((2 * rows, 2 * hidden), BF),
-            dma((4,)),
-            dma((6,)),
+            dma((PIECES + 1,)),
+            dma((2,)),
         ],
         16 * rows * width * hidden,
         12 << 20,
@@ -345,19 +339,51 @@
         recv,
         own_weights,
         partner_weights,
-        limit=VMEM_MOST,
-    )
+        limit=VMEM_SERVE,
+    )
+
+
+def local(tokens, cotangent, routes, route_weight, expert_slot, capacity, gate_up):
+    count = lax.axis_size("expert")
+    n_tokens, width = tokens.shape
+    top = routes.shape[1]
+    hidden = cotangent.shape[2]
+    n_routes = n_tokens * top
+    rows = 2 * count
+    my_cap = lax.dynamic_slice(capacity, (lax.axis_index("expert"),), (1,))
+    swap = [(s, (s + count // 2) % count) for s in range(count)]
+
+    own_weights = lax.all_gather(gate_up, "dp", axis=1, tiled=True)[0]
+    partner_shard = lax.ppermute(gate_up, "expert", swap)
+    partner_weights = lax.all_gather(partner_shard, "dp", axis=1, tiled=True)[0]
+    send, target, scaled = pack_call(
+        routes.T, route_weight.T, expert_slot.reshape(1, count), capacity.reshape(1, count),
+        tokens, cotangent.reshape(n_routes, hidden), count,
+    )
+    recv = exchange(send)
+    replicas = lax.axis_size("dp")
+    chunk = width // replicas
+    send_back, grads = serve_call(my_cap, recv, own_weights, partner_weights)
     back = exchange(send_back)
     all_grads = lax.all_gather(grads, "dp", axis=0, tiled=False)
-    me = lax.axis_index("dp")
-    received = []
-    for k in range(replicas):
-        piece = lax.dynamic_index_in_dim(
-            sent_rows, lax.rem(me + k, replicas), axis=0, keepdims=False
+    me = lax.axis_index("dp").reshape(1)
+    received = list(
+        call(
+            slice_rows,
+            [((2 * rows, chunk), BF)] * replicas,
+            [scalars(), whole(), in_hbm()],
+            [whole()] * replicas,
+            [],
+            0,
+            5 << 20,
+            me,
+            recv,
+            grads,
         )
-        if k:
-            piece = lax.ppermute(piece, "dp", [(q, (q + k) % replicas) for q in range(replicas)])
-        received.append(piece)
+    )
+    for k in range(1, replicas):
+        shift = [(q, (q + k) % replicas) for q in range(replicas)]
+        received[k] = lax.ppermute(received[k], "dp", shift)
     shard = (chunk, 2 * hidden)
     own_shard, far_shard = call(
         weight_grads,
@@ -368,7 +394,7 @@
         8 * replicas * rows * chunk * hidden,
         8 << 20,
         my_cap,
-        me.reshape(1),
+        me,
         *received,
         all_grads,
     )

time: 281 us -> 280 us (level)
  local copies, waits for them, and re-layouts: 9.35 us -> 5.63 us
  waiting for transfers between devices: 185 us -> 188 us
    unnamed x20 -> x16, local copies, waits for them, and re-layouts: 7.09 us -> 5.07 us
    pallas_call x4 -> x5, Pallas kernels: 20 us -> 19.7 us  [call(): pl.pallas_call(kernel, out_shape=[jax.ShapeDtypeStruct(s, d) for s, d in...]
where the time goes in v4:
time: 280 us
  waiting for transfers between devices  188 us (67%)
  starting transfers between devices  51.4 us (18%)
  Pallas kernels  19.7 us (7%)
  between operations  13.9 us (5%)
  local copies, waits for them, and re-layouts  5.63 us (2%)
    all_gather x1, waiting for transfers between devices, local(): partner_weights = lax.all_gather(partner_shard, 'dp', axis=1, tiled=True)[0]  49.6 us
    all_to_all x2, starting transfers between devices, exchange(): lax.all_to_all(value, 'expert', split_axis=0, concat_axis=0, tiled=True)  30.3 us
    ppermute x3, waiting for transfers between devices, local(): received[k] = lax.ppermute(received[k], 'dp', shift)  26 us
    all_to_all x2, waiting for transfers between devices, exchange(): lax.all_to_all(value, 'expert', split_axis=0, concat_axis=0, tiled=True)  24.4 us
    ppermute x1, waiting for transfers between devices, local(): moved_shard = lax.ppermute(far_shard, 'expert', swap)  22.9 us
    all_gather x1, waiting for transfers between devices, local(): own_weights = lax.all_gather(gate_up, 'dp', axis=1, tiled=True)[0]  22.4 us
    ppermute x1, waiting for transfers between devices, local(): partner_shard = lax.ppermute(gate_up, 'expert', swap)  22.1 us
    pallas_call x5, Pallas kernels, call(): pl.pallas_call(kernel, out_shape=[jax.ShapeDtypeStruct(s, d) for s, d in...  19.7 us
  transfers between devices with their start and end apart: 10, of which 10 were waited for; matrix products, arithmetic and copies ran while one was open for 1% of the time, Pallas kernels for 1%

profile of v4, /device:TPU:1, one launch (start us, length us, event | category | flops | bytes accessed | tf_op | source)
XLA Modules:
  0.0 279.6 jit_solution(14007008953455881508)
XLA Ops:
  7.2 5.7 %shard_map.94 = (bf16[128,2,4864]{2,1,0:T(2,128)(2,1)}, s32[2,1024]{1,0:T(2,128)}, f32[1,1024]{1,0:T(1,128)}) custom-call(s32[8,128]{1,0:T(8,128)} %bitcast.16, f32[8,128]{1,0:T(8,128)} %bitcast.17, s32[1,128]{1,0:T(1,128)} %bitcast.19, s32[1,128]{1,0:T(1,128)} %bitcast.20, bf16[128,2048]{1,0:T(8,128)(2,1)} %tokens_hbm.1, bf16[1024,384]{1,0:T(8,128)(2,1)} %bitcast.15), custom_call_target="tpu_custom_call" | custom-call | flops 671088640 | bytes 4194304 | tf_op jit(solution)/shard_map/pallas_call | solution.py:268
  12.9 0.0 copy-start.6
  12.9 0.0 copy-start.7
  12.9 20.7 %all-to-all-start = ((bf16[128,2,4864]{2,1,0:T(2,128)(2,1)}), bf16[128,2,4864]{2,1,0:T(2,128)(2,1)S(1)}, u32[]{:S(2)}, u32[]{:S(2)}) async-start(bf16[128,2,4864]{2,1,0:T(2,128)(2,1)} %get-tuple-element.18), calls=%async_computation | async-start | bytes 4980736 | tf_op jit(solution)/shard_map/all_to_all | solution.py:280
  33.6 0.0 all-gather.5.cloned.1.call-start
  33.7 0.7 all-gather.5.cloned.1.call-update
  34.4 0.0 all-gather.7.cloned.1.call-start
  34.4 0.0 copy-done.6
  34.4 5.1 %collective-permute-start = (bf16[1,512,768]{2,1,0:T(8,128)(2,1)S(1)}, bf16[1,512,768]{2,1,0:T(8,128)(2,1)}, u32[]{:S(2)}, u32[]{:S(2)}) collective-permute-start(bf16[1,512,768]{2,1,0:T(8,128)(2,1)S(1)} %copy-done.6), channel_id=1, source_target_pairs={{0,256},{4,260},{8,264},{12,268},{16,272},{20,276},{24,280},{28,28... | collective-permute-start | bytes 2359304 | tf_op jit(solution)/shard_map/ppermute | solution.py:357
  39.5 22.1 %collective-permute-done = bf16[1,512,768]{2,1,0:T(8,128)(2,1)} collective-permute-done((bf16[1,512,768]{2,1,0:T(8,128)(2,1)S(1)}, bf16[1,512,768]{2,1,0:T(8,128)(2,1)}, u32[]{:S(2)}, u32[]{:S(2)}) %collective-permute-start) | collective-permute-done | bytes 786464 | tf_op jit(solution)/shard_map/ppermute | solution.py:357
  61.7 0.0 all-gather.7.cloned.1.call-update
  61.7 0.0 copy-done.7
  61.7 0.6 dynamic_slice.3.cap_ref
  62.3 22.4 %all-gather.5.cloned.1.call-done = bf16[1,2048,768]{2,1,0:T(8,128)(2,1)} async-done(((bf16[1,512,768]{2,1,0:T(8,128)(2,1)}), bf16[1,2048,768]{2,1,0:T(8,128)(2,1)}) %all-gather.5.cloned.1.call-update) | async-done | bytes 3145744 | tf_op jit(solution)/shard_map/all_gather | solution.py:356
  84.7 49.6 %all-gather.7.cloned.1.call-done = bf16[1,2048,768]{2,1,0:T(8,128)(2,1)} async-done(((bf16[1,512,768]{2,1,0:T(8,128)(2,1)}), bf16[1,2048,768]{2,1,0:T(8,128)(2,1)}) %all-gather.7.cloned.1.call-update) | async-done | bytes 3145744 | tf_op jit(solution)/shard_map/all_gather | solution.py:358
  134.3 14.8 %all-to-all-done.recv = bf16[128,2,4864]{2,1,0:T(2,128)(2,1)S(1)} async-done(((bf16[128,2,4864]{2,1,0:T(2,128)(2,1)}), bf16[128,2,4864]{2,1,0:T(2,128)(2,1)S(1)}, u32[]{:S(2)}, u32[]{:S(2)}) %all-to-all-start) | async-done | bytes 2490400 | tf_op jit(solution)/shard_map/all_to_all | solution.py:280
  149.1 7.6 %shard_map.95 = (bf16[128,2,4224]{2,1,0:T(2,128)(2,1)S(1)}, bf16[512,768]{1,0:T(8,128)(2,1)}) custom-call(s32[1]{0:T(128)} %dynamic_slice.3.cap_ref, bf16[128,2,4864]{2,1,0:T(2,128)(2,1)S(1)} %all-to-all-done.recv, bf16[2048,768]{1,0:T(8,128)(2,1)} %bitcast.13, bf16[2048,768]{1,0:T(8,128)(2,1)} %bitcast.14), custom_call_target="tpu_custom_call" | custom-call | flops 3221225472 | bytes 12582912 | tf_op jit(solution)/shard_map/pallas_call | solution.py:268
  156.7 0.0 copy-start
  156.8 1.3 copy-done
  158.1 9.6 %all-to-all-start.1 = ((bf16[128,2,4224]{2,1,0:T(2,128)(2,1)}), bf16[128,2,4224]{2,1,0:T(2,128)(2,1)}, u32[]{:S(2)}, u32[]{:S(2)}) async-start(bf16[128,2,4224]{2,1,0:T(2,128)(2,1)} %copy-done), calls=%async_computation.1 | async-start | bytes 4325376 | tf_op jit(solution)/shard_map/all_to_all | solution.py:280
  167.7 0.0 all-gather.9.cloned.1.call-start
  167.7 0.7 all-gather.9.cloned.1.call-update
  168.4 0.3 shard_map.97
  168.7 3.3 %collective-permute-start.1 = (bf16[512,512]{1,0:T(8,128)(2,1)S(1)}, bf16[512,512]{1,0:T(8,128)(2,1)S(1)}, u32[]{:S(2)}, u32[]{:S(2)}) collective-permute-start(bf16[512,512]{1,0:T(8,128)(2,1)S(1)} %get-tuple-element.24), channel_id=1, source_target_pairs={{0,1},{1,2},{2,3},{3,0},{4,5},{5,6},{6,7},{7,4},{8,9},{9,10},{10,1... | collective-permute-start | bytes 1572872 | tf_op jit(solution)/shard_map/ppermute | solution.py:386
  172.0 4.4 %collective-permute-start.2 = (bf16[512,512]{1,0:T(8,128)(2,1)S(1)}, bf16[512,512]{1,0:T(8,128)(2,1)S(1)}, u32[]{:S(2)}, u32[]{:S(2)}) collective-permute-start(bf16[512,512]{1,0:T(8,128)(2,1)S(1)} %get-tuple-element.25), channel_id=1, source_target_pairs={{0,2},{1,3},{2,0},{3,1},{4,6},{5,7},{6,4},{7,5},{8,10},{9,11},{10,... | collective-permute-start | bytes 1572872 | tf_op jit(solution)/shard_map/ppermute | solution.py:386
  176.4 3.1 %collective-permute-start.3 = (bf16[512,512]{1,0:T(8,128)(2,1)S(1)}, bf16[512,512]{1,0:T(8,128)(2,1)S(1)}, u32[]{:S(2)}, u32[]{:S(2)}) collective-permute-start(bf16[512,512]{1,0:T(8,128)(2,1)S(1)} %get-tuple-element.26), channel_id=1, source_target_pairs={{0,3},{1,0},{2,1},{3,2},{4,7},{5,4},{6,5},{7,6},{8,11},{9,8},{10,9... | collective-permute-start | bytes 1572872 | tf_op jit(solution)/shard_map/ppermute | solution.py:386
  179.5 4.9 %collective-permute-done.1.rows_1 = bf16[512,512]{1,0:T(8,128)(2,1)S(1)} collective-permute-done((bf16[512,512]{1,0:T(8,128)(2,1)S(1)}, bf16[512,512]{1,0:T(8,128)(2,1)S(1)}, u32[]{:S(2)}, u32[]{:S(2)}) %collective-permute-start.1) | collective-permute-done | bytes 524320 | tf_op jit(solution)/shard_map/ppermute | solution.py:386
  184.4 14.2 %collective-permute-done.2.rows_2 = bf16[512,512]{1,0:T(8,128)(2,1)S(1)} collective-permute-done((bf16[512,512]{1,0:T(8,128)(2,1)S(1)}, bf16[512,512]{1,0:T(8,128)(2,1)S(1)}, u32[]{:S(2)}, u32[]{:S(2)}) %collective-permute-start.2) | collective-permute-done | bytes 524320 | tf_op jit(solution)/shard_map/ppermute | solution.py:386
  198.6 6.8 %collective-permute-done.3.rows_3 = bf16[512,512]{1,0:T(8,128)(2,1)S(1)} collective-permute-done((bf16[512,512]{1,0:T(8,128)(2,1)S(1)}, bf16[512,512]{1,0:T(8,128)(2,1)S(1)}, u32[]{:S(2)}, u32[]{:S(2)}) %collective-permute-start.3) | collective-permute-done | bytes 524320 | tf_op jit(solution)/shard_map/ppermute | solution.py:386
  205.4 0.0 copy-start.4
  205.4 0.8 copy-done.4
  206.2 19.1 %all-gather.9.cloned.1.call-done = bf16[2048,768]{1,0:T(8,128)(2,1)} async-done(((bf16[512,768]{1,0:T(8,128)(2,1)}), bf16[2048,768]{1,0:T(8,128)(2,1)}) %all-gather.9.cloned.1.call-update) | async-done | bytes 3145744 | tf_op jit(solution)/shard_map/all_gather | solution.py:368
  225.3 0.0 copy-start.3
  225.3 1.9 copy-done.3
  227.2 0.0 copy-start.5
  227.2 1.0 copy-done.5
  228.2 2.4 shard_map.98
  230.6 0.0 copy-start.1
  230.7 0.0 copy-start.2
  230.7 5.1 %collective-permute-start.4 = (bf16[512,768]{1,0:T(8,128)(2,1)S(1)}, bf16[512,768]{1,0:T(8,128)(2,1)S(1)}, u32[]{:S(2)}, u32[]{:S(2)}) collective-permute-start(bf16[512,768]{1,0:T(8,128)(2,1)S(1)} %get-tuple-element.28), channel_id=1, source_target_pairs={{0,256},{4,260},{8,264},{12,268},{16,272},{20,276},{24,280},{28,28... | collective-permute-start | bytes 2359304 | tf_op jit(solution)/shard_map/ppermute | solution.py:401
  235.8 22.9 %collective-permute-done.4 = bf16[512,768]{1,0:T(8,128)(2,1)S(1)} collective-permute-done((bf16[512,768]{1,0:T(8,128)(2,1)S(1)}, bf16[512,768]{1,0:T(8,128)(2,1)S(1)}, u32[]{:S(2)}, u32[]{:S(2)}) %collective-permute-start.4) | collective-permute-done | bytes 786464 | tf_op jit(solution)/shard_map/ppermute | solution.py:401
  258.7 1.1 fusion
  259.7 9.6 %all-to-all-done.1.back = bf16[128,2,4224]{2,1,0:T(2,128)(2,1)} async-done(((bf16[128,2,4224]{2,1,0:T(2,128)(2,1)}), bf16[128,2,4224]{2,1,0:T(2,128)(2,1)}, u32[]{:S(2)}, u32[]{:S(2)}) %all-to-all-start.1) | async-done | bytes 2162720 | tf_op jit(solution)/shard_map/all_to_all | solution.py:280
  269.3 0.0 copy-done.1
  269.3 0.0 copy-done.2
  269.3 3.7 %shard_map.96 = (bf16[128,2048]{1,0:T(8,128)(2,1)}, f32[8,128]{1,0:T(8,128)}) custom-call(s32[2,1024]{1,0:T(2,128)S(1)} %copy-done.1, f32[1,1024]{1,0:T(1,128)S(1)} %copy-done.2, bf16[128,2,4224]{2,1,0:T(2,128)(2,1)} %all-to-all-done.1.back), custom_call_target="tpu_custom_call" | custom-call | flops 268435456 | bytes 4194304 | tf_op jit(solution)/shard_map/pallas_call | solution.py:268
Async XLA Ops:
  12.9 21.5 %copy-start.6 = (bf16[1,512,768]{2,1,0:T(8,128)(2,1)S(1)}, bf16[1,512,768]{2,1,0:T(8,128)(2,1)}, u32[]{:S(2)}) copy-start(bf16[1,512,768]{2,1,0:T(8,128)(2,1)} %param.13) | copy-start | bytes 2359300
  12.9 48.8 %copy-start.7 = (s32[128]{0:T(128)S(1)}, s32[128]{0:T(128)}, u32[]{:S(2)}) copy-start(s32[128]{0:T(128)} %param.12) | copy-start | bytes 1540
  12.9 136.2 %all-to-all-start = ((bf16[128,2,4864]{2,1,0:T(2,128)(2,1)}), bf16[128,2,4864]{2,1,0:T(2,128)(2,1)S(1)}, u32[]{:S(2)}, u32[]{:S(2)}) async-start(bf16[128,2,4864]{2,1,0:T(2,128)(2,1)} %get-tuple-element.18), calls=%async_computation | async-start | bytes 4980736 | tf_op jit(solution)/shard_map/all_to_all | solution.py:280
  33.6 51.1 %all-gather.5.cloned.1.call-start = ((), (), s32[]{:S(2)}) async-start(), calls=%async_computation.2 | async-start | bytes 3932160 | tf_op jit(solution)/shard_map/all_gather | solution.py:356
  34.4 100.0 %all-gather.7.cloned.1.call-start = ((), (), s32[]{:S(2)}) async-start(), calls=%async_computation.3 | async-start | bytes 3932160 | tf_op jit(solution)/shard_map/all_gather | solution.py:358
  34.4 27.3 %collective-permute-start = (bf16[1,512,768]{2,1,0:T(8,128)(2,1)S(1)}, bf16[1,512,768]{2,1,0:T(8,128)(2,1)}, u32[]{:S(2)}, u32[]{:S(2)}) collective-permute-start(bf16[1,512,768]{2,1,0:T(8,128)(2,1)S(1)} %copy-done.6), channel_id=1, source_target_pairs={{0,256},{4,260},{8,264},{12,268},{16,272},{20,276},{24,280},{28,28... | collective-permute-start | bytes 2359304 | tf_op jit(solution)/shard_map/ppermute | solution.py:357
  156.7 1.3 copy-start
  158.1 111.2 %all-to-all-start.1 = ((bf16[128,2,4224]{2,1,0:T(2,128)(2,1)}), bf16[128,2,4224]{2,1,0:T(2,128)(2,1)}, u32[]{:S(2)}, u32[]{:S(2)}) async-start(bf16[128,2,4224]{2,1,0:T(2,128)(2,1)} %copy-done), calls=%async_computation.1 | async-start | bytes 4325376 | tf_op jit(solution)/shard_map/all_to_all | solution.py:280
  167.7 57.6 %all-gather.9.cloned.1.call-start = ((), (), s32[]{:S(2)}) async-start(), calls=%async_computation.4 | async-start | bytes 3932160 | tf_op jit(solution)/shard_map/all_gather | solution.py:368
  168.7 15.7 %collective-permute-start.1 = (bf16[512,512]{1,0:T(8,128)(2,1)S(1)}, bf16[512,512]{1,0:T(8,128)(2,1)S(1)}, u32[]{:S(2)}, u32[]{:S(2)}) collective-permute-start(bf16[512,512]{1,0:T(8,128)(2,1)S(1)} %get-tuple-element.24), channel_id=1, source_target_pairs={{0,1},{1,2},{2,3},{3,0},{4,5},{5,6},{6,7},{7,4},{8,9},{9,10},{10,1... | collective-permute-start | bytes 1572872 | tf_op jit(solution)/shard_map/ppermute | solution.py:386
  172.0 26.6 %collective-permute-start.2 = (bf16[512,512]{1,0:T(8,128)(2,1)S(1)}, bf16[512,512]{1,0:T(8,128)(2,1)S(1)}, u32[]{:S(2)}, u32[]{:S(2)}) collective-permute-start(bf16[512,512]{1,0:T(8,128)(2,1)S(1)} %get-tuple-element.25), channel_id=1, source_target_pairs={{0,2},{1,3},{2,0},{3,1},{4,6},{5,7},{6,4},{7,5},{8,10},{9,11},{10,... | collective-permute-start | bytes 1572872 | tf_op jit(solution)/shard_map/ppermute | solution.py:386
  176.4 29.1 %collective-permute-start.3 = (bf16[512,512]{1,0:T(8,128)(2,1)S(1)}, bf16[512,512]{1,0:T(8,128)(2,1)S(1)}, u32[]{:S(2)}, u32[]{:S(2)}) collective-permute-start(bf16[512,512]{1,0:T(8,128)(2,1)S(1)} %get-tuple-element.26), channel_id=1, source_target_pairs={{0,3},{1,0},{2,1},{3,2},{4,7},{5,4},{6,5},{7,6},{8,11},{9,8},{10,9... | collective-permute-start | bytes 1572872 | tf_op jit(solution)/shard_map/ppermute | solution.py:386
  205.4 0.8 copy-start.4
  225.3 1.9 copy-start.3
  227.2 1.0 copy-start.5
  230.6 38.7 %copy-start.1 = (s32[2,1024]{1,0:T(2,128)S(1)}, s32[2,1024]{1,0:T(2,128)}, u32[]{:S(2)}) copy-start(s32[2,1024]{1,0:T(2,128)} %get-tuple-element.16.target_ref) | copy-start | bytes 24580
  230.7 38.7 %copy-start.2 = (f32[1,1024]{1,0:T(1,128)S(1)}, f32[1,1024]{1,0:T(1,128)}, u32[]{:S(2)}) copy-start(f32[1,1024]{1,0:T(1,128)} %get-tuple-element.17.scaled_ref) | copy-start | bytes 12292
  230.7 28.0 %collective-permute-start.4 = (bf16[512,768]{1,0:T(8,128)(2,1)S(1)}, bf16[512,768]{1,0:T(8,128)(2,1)S(1)}, u32[]{:S(2)}, u32[]{:S(2)}) collective-permute-start(bf16[512,768]{1,0:T(8,128)(2,1)S(1)} %get-tuple-element.28), channel_id=1, source_target_pairs={{0,256},{4,260},{8,264},{12,268},{16,272},{20,276},{24,280},{28,28... | collective-permute-start | bytes 2359304 | tf_op jit(solution)/shard_map/ppermute | solution.py:401
Sparse Core Ops, SparseCore 0:
  36.6 48.1 all-gather.4
  86.8 47.4 all-gather.6
  171.2 54.0 all-gather.8

commit v5 on v4

--- a/solution.py
+++ b/solution.py
@@ -118,22 +118,27 @@
     target_ref[0:1, :] = targets[0]
     target_ref[1:2, :] = targets[1]
     rows = out.shape[0] * out.shape[1]
+    stores = []
+
+    def send(span):
+        sem = out_sems.at[len(stores)]
+        store = pltpu.make_async_copy(out.at[:, :, span], out_hbm.at[:, :, span], sem)
+        store.start()
+        stores.append(store)
+
     loads[4].wait()
-    stores = []
     for i, target in enumerate(targets):
         hit = iota((rows, n_routes), 0) == target
         pick = mm(hit.astype(BF), owner, 1, 1).astype(BF)
         start = i * part
         moved = mm(pick, tokens[...]).astype(BF)
         out[:, :, start : start + width] = moved.reshape(rows // 2, 2, width)
+        send(pl.ds(start, width))
         if i == 0:
             loads[5].wait()
         moved = mm(jnp.where(hit, weight_row, 0.0).astype(BF), cot[...]).astype(BF)
         out[:, :, start + width : start + part] = moved.reshape(rows // 2, 2, hidden)
-        span = pl.ds(start, part)
-        store = pltpu.make_async_copy(out.at[:, :, span], out_hbm.at[:, :, span], out_sems.at[i])
-        store.start()
-        stores.append(store)
+        send(pl.ds(start + width, hidden))
     for one in stores:
         one.wait()
 
@@ -168,13 +173,15 @@
 
 
 def serve_all(
-    cap_ref, recv, own_hbm, partner_hbm, back, grad_hbm, own, other, all_grads, sems, out_sems
+    cap_ref, recv, own_hbm, partner_hbm, back, rows_hbm, grad_hbm,
+    own, other, all_rows, all_grads, sems, out_sems,
 ):
     width = own.shape[0]
     hidden = own.shape[1] // 2
     part = width + hidden
     sources = recv.shape[0]
     rows = 2 * sources
+    chunks, _, chunk = all_rows.shape
     is_own = cap_ref[0] > 2
     deep = width // PIECES
     pieces = [pl.ds(k * deep, deep) for k in range(PIECES)]
@@ -191,36 +198,30 @@
 
     ready = (loads, [pltpu.make_async_copy(own_hbm, other, last)])
     stores = []
+
+    def store(src, dst):
+        one = pltpu.make_async_copy(src, dst, out_sems.at[len(stores)])
+        one.start()
+        stores.append(one)
+
     tail = None
     for i, weights in enumerate((own, other)):
         start = i * part
+        span = pl.ds(i * rows, rows)
         tokens = recv[:, :, start : start + width].reshape(rows, width)
+        for c in range(chunks):
+            all_rows[c, i * rows : (i + 1) * rows, :] = tokens[:, c * chunk : (c + 1) * chunk]
+        store(all_rows.at[:, span, :], rows_hbm.at[pl.ds(0, chunks), span, :])
         scaled = recv[:, :, start + width : start + part].reshape(rows, hidden)
         grad, router, result = serve(tokens, scaled, weights, ready[i])
-        span = pl.ds(i * rows, rows)
         all_grads[i * rows : (i + 1) * rows, :] = grad
-        store = pltpu.make_async_copy(all_grads.at[span], grad_hbm.at[span], out_sems.at[i])
-        store.start()
-        stores.append(store)
+        store(all_grads.at[span], grad_hbm.at[span])
         back[:, :, i * width : (i + 1) * width] = result.reshape(sources, 2, width)
         lanes = split_router(router, 2 * i)
         tail = lanes if tail is None else tail + lanes
     back[:, :, 2 * width :] = tail.astype(BF).reshape(sources, 2, TAIL)
     for one in stores:
         one.wait()
-
-
-def slice_rows(me_ref, recv, grads_hbm, *out_refs):
-    del grads_hbm
-    slices = len(out_refs)
-    rows = 2 * recv.shape[0]
-    part = recv.shape[2] // 2
-    chunk = out_refs[0].shape[1]
-    for k, out_ref in enumerate(out_refs):
-        column = lax.rem(me_ref[0] + k, slices) * chunk
-        for i in range(2):
-            span = pl.ds(pl.multiple_of(i * part + column, 128), chunk)
-            out_ref[i * rows : (i + 1) * rows, :] = recv[:, :, span].reshape(rows, chunk)
 
 
 def weight_grads(cap_ref, me_ref, rows_0, rows_1, rows_2, rows_3, grads, own_ref, far_ref):
@@ -301,7 +302,7 @@
             pltpu.VMEM((n_routes, hidden), BF),
             pltpu.VMEM((count, 2, 2 * part), BF),
             dma((6,)),
-            dma((2,)),
+            dma((4,)),
         ],
         4 * rows * n_routes * (hidden + 2 * n_tokens),
         4 << 20,
@@ -315,23 +316,29 @@
     )
 
 
-def serve_call(my_cap, recv, own_weights, partner_weights):
+def serve_call(my_cap, recv, own_weights, partner_weights, replicas):
     count = recv.shape[0]
     width = own_weights.shape[0]
     hidden = own_weights.shape[1] // 2
     rows = 2 * count
+    chunk = width // replicas
     dma = pltpu.SemaphoreType.DMA
     return call(
         serve_all,
-        [((count, 2, 2 * width + TAIL), BF), ((2 * rows, 2 * hidden), BF)],
+        [
+            ((count, 2, 2 * width + TAIL), BF),
+            ((2 * replicas, 2 * rows, chunk), BF),
+            ((2 * rows, 2 * hidden), BF),
+        ],
         [scalars(), whole(), in_hbm(), in_hbm()],
-        [whole(), in_hbm()],
+        [whole(), in_hbm(), in_hbm()],
         [
             pltpu.VMEM((width, 2 * hidden), BF),
             pltpu.VMEM((width, 2 * hidden), BF),
+            pltpu.VMEM((replicas, 2 * rows, chunk), BF),
             pltpu.VMEM((2 * rows, 2 * hidden), BF),
             dma((PIECES + 1,)),
-            dma((2,)),
+            dma((4,)),
         ],
         16 * rows * width * hidden,
         12 << 20,
@@ -363,27 +370,20 @@
     recv = exchange(send)
     replicas = lax.axis_size("dp")
     chunk = width // replicas
-    send_back, grads = serve_call(my_cap, recv, own_weights, partner_weights)
+    send_back, sent_rows, grads = serve_call(
+        my_cap, recv, own_weights, partner_weights, replicas
+    )
     back = exchange(send_back)
     all_grads = lax.all_gather(grads, "dp", axis=0, tiled=False)
-    me = lax.axis_index("dp").reshape(1)
-    received = list(
-        call(
-            slice_rows,
-            [((2 * rows, chunk), BF)] * replicas,
-            [scalars(), whole(), in_hbm()],
-            [whole()] * replicas,
-            [],
-            0,
-            5 << 20,
-            me,
-            recv,
-            grads,
+    me = lax.axis_index("dp")
+    received = []
+    for k in range(replicas):
+        piece = lax.dynamic_index_in_dim(
+            sent_rows, lax.rem(me + k, replicas), axis=0, keepdims=False
         )
-    )
-    for k in range(1, replicas):
-        shift = [(q, (q + k) % replicas) for q in range(replicas)]
-        received[k] = lax.ppermute(received[k], "dp", shift)
+        if k:
+            piece = lax.ppermute(piece, "dp", [(q, (q + k) % replicas) for q in range(replicas)])
+        received.append(piece)
     shard = (chunk, 2 * hidden)
     own_shard, far_shard = call(
         weight_grads,
@@ -394,7 +394,7 @@
         8 * replicas * rows * chunk * hidden,
         8 << 20,
         my_cap,
-        me,
+        me.reshape(1),
         *received,
         all_grads,
     )

time: 280 us -> 279 us (level)
  local copies, waits for them, and re-layouts: 5.63 us -> 9.33 us
  waiting for transfers between devices: 188 us -> 185 us
    unnamed x16 -> x20, local copies, waits for them, and re-layouts: 5.07 us -> 7.01 us
    pallas_call x5 -> x4, Pallas kernels: 19.7 us -> 18.4 us  [call(): pl.pallas_call(kernel, out_shape=[jax.ShapeDtypeStruct(s, d) for s, d in...]
where the time goes in v5:
time: 279 us; the launch traced here: 278 us
  waiting for transfers between devices  185 us (66%)
  starting transfers between devices  51 us (18%)
  Pallas kernels  18.4 us (7%)
  between operations  13.9 us (5%)
  local copies, waits for them, and re-layouts  9.33 us (3%)
    all_gather x1, waiting for transfers between devices, local(): partner_weights = lax.all_gather(partner_shard, 'dp', axis=1, tiled=True)[0]  49.6 us
    all_to_all x2, starting transfers between devices, exchange(): lax.all_to_all(value, 'expert', split_axis=0, concat_axis=0, tiled=True)  29.9 us
    ppermute x3, waiting for transfers between devices, local(): lax.ppermute(piece, 'dp', [(q, (q + k) % replicas) for q in range(replica...  26.4 us
    all_to_all x2, waiting for transfers between devices, exchange(): lax.all_to_all(value, 'expert', split_axis=0, concat_axis=0, tiled=True)  22.8 us
    ppermute x1, waiting for transfers between devices, local(): moved_shard = lax.ppermute(far_shard, 'expert', swap)  22.4 us
    all_gather x1, waiting for transfers between devices, local(): own_weights = lax.all_gather(gate_up, 'dp', axis=1, tiled=True)[0]  22.3 us
    ppermute x1, waiting for transfers between devices, local(): partner_shard = lax.ppermute(gate_up, 'expert', swap)  22.1 us
    pallas_call x4, Pallas kernels, call(): pl.pallas_call(kernel, out_shape=[jax.ShapeDtypeStruct(s, d) for s, d in...  18.4 us
  transfers between devices with their start and end apart: 10, of which 10 were waited for; matrix products, arithmetic and copies ran while one was open for 1% of the time, Pallas kernels for 1%

profile of v5, /device:TPU:1, one launch (start us, length us, event | category | flops | bytes accessed | tf_op | source)
XLA Modules:
  0.0 278.4 jit_solution(13350161904281137634)
XLA Ops:
  7.2 5.4 %shard_map.94 = (bf16[128,2,4864]{2,1,0:T(2,128)(2,1)}, s32[2,1024]{1,0:T(2,128)}, f32[1,1024]{1,0:T(1,128)}) custom-call(s32[8,128]{1,0:T(8,128)} %bitcast.24, f32[8,128]{1,0:T(8,128)} %bitcast.25, s32[1,128]{1,0:T(1,128)} %bitcast.27, s32[1,128]{1,0:T(1,128)} %bitcast.28, bf16[128,2048]{1,0:T(8,128)(2,1)} %tokens_hbm.1, bf16[1024,384]{1,0:T(8,128)(2,1)} %bitcast.23), custom_call_target="tpu_custom_call" | custom-call | flops 671088640 | bytes 4194304 | tf_op jit(solution)/shard_map/pallas_call | solution.py:269
  12.6 0.0 copy-start.8
  12.6 0.0 copy-start.9
  12.6 20.7 %all-to-all-start = ((bf16[128,2,4864]{2,1,0:T(2,128)(2,1)}), bf16[128,2,4864]{2,1,0:T(2,128)(2,1)S(1)}, u32[]{:S(2)}, u32[]{:S(2)}) async-start(bf16[128,2,4864]{2,1,0:T(2,128)(2,1)} %get-tuple-element.15), calls=%async_computation | async-start | bytes 4980736 | tf_op jit(solution)/shard_map/all_to_all | solution.py:281
  33.3 0.0 all-gather.5.cloned.1.call-start
  33.4 0.7 all-gather.5.cloned.1.call-update
  34.1 0.0 all-gather.7.cloned.1.call-start
  34.1 0.0 copy-done.8
  34.1 5.1 %collective-permute-start = (bf16[1,512,768]{2,1,0:T(8,128)(2,1)S(1)}, bf16[1,512,768]{2,1,0:T(8,128)(2,1)}, u32[]{:S(2)}, u32[]{:S(2)}) collective-permute-start(bf16[1,512,768]{2,1,0:T(8,128)(2,1)S(1)} %copy-done.8), channel_id=1, source_target_pairs={{0,256},{4,260},{8,264},{12,268},{16,272},{20,276},{24,280},{28,28... | collective-permute-start | bytes 2359304 | tf_op jit(solution)/shard_map/ppermute | solution.py:364
  39.3 22.1 %collective-permute-done = bf16[1,512,768]{2,1,0:T(8,128)(2,1)} collective-permute-done((bf16[1,512,768]{2,1,0:T(8,128)(2,1)S(1)}, bf16[1,512,768]{2,1,0:T(8,128)(2,1)}, u32[]{:S(2)}, u32[]{:S(2)}) %collective-permute-start) | collective-permute-done | bytes 786464 | tf_op jit(solution)/shard_map/ppermute | solution.py:364
  61.4 0.0 all-gather.7.cloned.1.call-update
  61.4 0.0 copy-done.9
  61.4 0.7 dynamic_slice.16.cap_ref
  62.1 22.3 %all-gather.5.cloned.1.call-done = bf16[1,2048,768]{2,1,0:T(8,128)(2,1)} async-done(((bf16[1,512,768]{2,1,0:T(8,128)(2,1)}), bf16[1,2048,768]{2,1,0:T(8,128)(2,1)}) %all-gather.5.cloned.1.call-update) | async-done | bytes 3145744 | tf_op jit(solution)/shard_map/all_gather | solution.py:363
  84.4 49.6 %all-gather.7.cloned.1.call-done = bf16[1,2048,768]{2,1,0:T(8,128)(2,1)} async-done(((bf16[1,512,768]{2,1,0:T(8,128)(2,1)}), bf16[1,2048,768]{2,1,0:T(8,128)(2,1)}) %all-gather.7.cloned.1.call-update) | async-done | bytes 3145744 | tf_op jit(solution)/shard_map/all_gather | solution.py:365
  134.0 14.8 %all-to-all-done.recv = bf16[128,2,4864]{2,1,0:T(2,128)(2,1)S(1)} async-done(((bf16[128,2,4864]{2,1,0:T(2,128)(2,1)}), bf16[128,2,4864]{2,1,0:T(2,128)(2,1)S(1)}, u32[]{:S(2)}, u32[]{:S(2)}) %all-to-all-start) | async-done | bytes 2490400 | tf_op jit(solution)/shard_map/all_to_all | solution.py:281
  148.9 8.2 %shard_map.95 = (bf16[128,2,4224]{2,1,0:T(2,128)(2,1)S(1)}, bf16[8,512,512]{2,1,0:T(8,128)(2,1)}, bf16[512,768]{1,0:T(8,128)(2,1)}) custom-call(s32[1]{0:T(128)} %dynamic_slice.16.cap_ref, bf16[128,2,4864]{2,1,0:T(2,128)(2,1)S(1)} %all-to-all-done.recv, bf16[2048,768]{1,0:T(8,128)(2,1)} %bitcast.21, bf16[2048,768]{1,0:T(8,128)(2,1)} %bitcast.22), custom_call_target="tpu_custom_call" | custom-call | flops 3221225472 | bytes 12582912 | tf_op jit(solution)/shard_map/pallas_call | solution.py:269
  157.1 0.0 copy-start
  157.1 1.4 copy-done
  158.6 9.2 %all-to-all-start.1 = ((bf16[128,2,4224]{2,1,0:T(2,128)(2,1)}), bf16[128,2,4224]{2,1,0:T(2,128)(2,1)S(1)}, u32[]{:S(2)}, u32[]{:S(2)}) async-start(bf16[128,2,4224]{2,1,0:T(2,128)(2,1)} %copy-done), calls=%async_computation.1 | async-start | bytes 4325376 | tf_op jit(solution)/shard_map/all_to_all | solution.py:281
  167.7 0.2 all-gather.9.cloned.1.call-start
  168.0 0.5 all-gather.9.cloned.1.call-update
  168.5 1.7 dynamic-slice_bitcast_fusion
  170.2 3.1 %collective-permute-start.1 = (bf16[512,512]{1,0:T(8,128)(2,1)S(1)}, bf16[512,512]{1,0:T(8,128)(2,1)S(1)}, u32[]{:S(2)}, u32[]{:S(2)}) collective-permute-start(bf16[512,512]{1,0:T(8,128)(2,1)S(1)} %get-tuple-element.25), channel_id=1, source_target_pairs={{0,1},{1,2},{2,3},{3,0},{4,5},{5,6},{6,7},{7,4},{8,9},{9,10},{10,1... | collective-permute-start | bytes 1572872 | tf_op jit(solution)/shard_map/ppermute | solution.py:385
  173.3 4.4 %collective-permute-start.2 = (bf16[512,512]{1,0:T(8,128)(2,1)S(1)}, bf16[512,512]{1,0:T(8,128)(2,1)S(1)}, u32[]{:S(2)}, u32[]{:S(2)}) collective-permute-start(bf16[512,512]{1,0:T(8,128)(2,1)S(1)} %get-tuple-element.24), channel_id=1, source_target_pairs={{0,2},{1,3},{2,0},{3,1},{4,6},{5,7},{6,4},{7,5},{8,10},{9,11},{10,... | collective-permute-start | bytes 1572872 | tf_op jit(solution)/shard_map/ppermute | solution.py:385
  177.7 3.1 %collective-permute-start.3 = (bf16[512,512]{1,0:T(8,128)(2,1)S(1)}, bf16[512,512]{1,0:T(8,128)(2,1)S(1)}, u32[]{:S(2)}, u32[]{:S(2)}) collective-permute-start(bf16[512,512]{1,0:T(8,128)(2,1)S(1)} %get-tuple-element.23), channel_id=1, source_target_pairs={{0,3},{1,0},{2,1},{3,2},{4,7},{5,4},{6,5},{7,6},{8,11},{9,8},{10,9... | collective-permute-start | bytes 1572872 | tf_op jit(solution)/shard_map/ppermute | solution.py:385
  180.7 5.1 %collective-permute-done.1.rows_1 = bf16[512,512]{1,0:T(8,128)(2,1)S(1)} collective-permute-done((bf16[512,512]{1,0:T(8,128)(2,1)S(1)}, bf16[512,512]{1,0:T(8,128)(2,1)S(1)}, u32[]{:S(2)}, u32[]{:S(2)}) %collective-permute-start.1) | collective-permute-done | bytes 524320 | tf_op jit(solution)/shard_map/ppermute | solution.py:385
  185.8 15.8 %collective-permute-done.2.rows_2 = bf16[512,512]{1,0:T(8,128)(2,1)S(1)} collective-permute-done((bf16[512,512]{1,0:T(8,128)(2,1)S(1)}, bf16[512,512]{1,0:T(8,128)(2,1)S(1)}, u32[]{:S(2)}, u32[]{:S(2)}) %collective-permute-start.2) | collective-permute-done | bytes 524320 | tf_op jit(solution)/shard_map/ppermute | solution.py:385
  201.6 0.0 copy-start.4
  201.6 0.8 copy-done.4
  202.4 5.5 %collective-permute-done.3.rows_3 = bf16[512,512]{1,0:T(8,128)(2,1)S(1)} collective-permute-done((bf16[512,512]{1,0:T(8,128)(2,1)S(1)}, bf16[512,512]{1,0:T(8,128)(2,1)S(1)}, u32[]{:S(2)}, u32[]{:S(2)}) %collective-permute-start.3) | collective-permute-done | bytes 524320 | tf_op jit(solution)/shard_map/ppermute | solution.py:385
  207.9 0.0 copy-start.6
  207.9 0.8 copy-done.6
  208.7 17.9 %all-gather.9.cloned.1.call-done = bf16[2048,768]{1,0:T(8,128)(2,1)} async-done(((bf16[512,768]{1,0:T(8,128)(2,1)}), bf16[2048,768]{1,0:T(8,128)(2,1)}) %all-gather.9.cloned.1.call-update) | async-done | bytes 3145744 | tf_op jit(solution)/shard_map/all_gather | solution.py:377
  226.6 0.0 copy-start.3
  226.6 1.9 copy-done.3
  228.5 1.0 copy-done.5
  229.5 1.0 copy-done.7
  230.6 2.5 shard_map.97
  233.1 0.0 copy-start.1
  233.1 0.0 copy-start.2
  233.1 5.1 %collective-permute-start.4 = (bf16[512,768]{1,0:T(8,128)(2,1)S(1)}, bf16[512,768]{1,0:T(8,128)(2,1)S(1)}, u32[]{:S(2)}, u32[]{:S(2)}) collective-permute-start(bf16[512,768]{1,0:T(8,128)(2,1)S(1)} %get-tuple-element.22), channel_id=1, source_target_pairs={{0,256},{4,260},{8,264},{12,268},{16,272},{20,276},{24,280},{28,28... | collective-permute-start | bytes 2359304 | tf_op jit(solution)/shard_map/ppermute | solution.py:401
  238.3 22.4 %collective-permute-done.4 = bf16[512,768]{1,0:T(8,128)(2,1)S(1)} collective-permute-done((bf16[512,768]{1,0:T(8,128)(2,1)S(1)}, bf16[512,768]{1,0:T(8,128)(2,1)S(1)}, u32[]{:S(2)}, u32[]{:S(2)}) %collective-permute-start.4) | collective-permute-done | bytes 786464 | tf_op jit(solution)/shard_map/ppermute | solution.py:401
  260.7 1.0 fusion
  261.7 8.0 %all-to-all-done.1.back = bf16[128,2,4224]{2,1,0:T(2,128)(2,1)S(1)} async-done(((bf16[128,2,4224]{2,1,0:T(2,128)(2,1)}), bf16[128,2,4224]{2,1,0:T(2,128)(2,1)S(1)}, u32[]{:S(2)}, u32[]{:S(2)}) %all-to-all-start.1) | async-done | bytes 2162720 | tf_op jit(solution)/shard_map/all_to_all | solution.py:281
  269.7 0.0 copy-done.1
  269.7 0.0 copy-done.2
  269.7 2.2 shard_map.96
  (2 shorter events, 0.0 us)
Async XLA Ops:
  12.6 21.5 %copy-start.8 = (bf16[1,512,768]{2,1,0:T(8,128)(2,1)S(1)}, bf16[1,512,768]{2,1,0:T(8,128)(2,1)}, u32[]{:S(2)}) copy-start(bf16[1,512,768]{2,1,0:T(8,128)(2,1)} %param.13) | copy-start | bytes 2359300
  12.6 48.8 %copy-start.9 = (s32[128]{0:T(128)S(1)}, s32[128]{0:T(128)}, u32[]{:S(2)}) copy-start(s32[128]{0:T(128)} %param.12) | copy-start | bytes 1540
  12.6 136.2 %all-to-all-start = ((bf16[128,2,4864]{2,1,0:T(2,128)(2,1)}), bf16[128,2,4864]{2,1,0:T(2,128)(2,1)S(1)}, u32[]{:S(2)}, u32[]{:S(2)}) async-start(bf16[128,2,4864]{2,1,0:T(2,128)(2,1)} %get-tuple-element.15), calls=%async_computation | async-start | bytes 4980736 | tf_op jit(solution)/shard_map/all_to_all | solution.py:281
  33.3 51.1 %all-gather.5.cloned.1.call-start = ((), (), s32[]{:S(2)}) async-start(), calls=%async_computation.2 | async-start | bytes 3932160 | tf_op jit(solution)/shard_map/all_gather | solution.py:363
  34.1 100.0 %all-gather.7.cloned.1.call-start = ((), (), s32[]{:S(2)}) async-start(), calls=%async_computation.3 | async-start | bytes 3932160 | tf_op jit(solution)/shard_map/all_gather | solution.py:365
  34.1 27.3 %collective-permute-start = (bf16[1,512,768]{2,1,0:T(8,128)(2,1)S(1)}, bf16[1,512,768]{2,1,0:T(8,128)(2,1)}, u32[]{:S(2)}, u32[]{:S(2)}) collective-permute-start(bf16[1,512,768]{2,1,0:T(8,128)(2,1)S(1)} %copy-done.8), channel_id=1, source_target_pairs={{0,256},{4,260},{8,264},{12,268},{16,272},{20,276},{24,280},{28,28... | collective-permute-start | bytes 2359304 | tf_op jit(solution)/shard_map/ppermute | solution.py:364
  157.1 1.4 copy-start
  158.6 111.1 %all-to-all-start.1 = ((bf16[128,2,4224]{2,1,0:T(2,128)(2,1)}), bf16[128,2,4224]{2,1,0:T(2,128)(2,1)S(1)}, u32[]{:S(2)}, u32[]{:S(2)}) async-start(bf16[128,2,4224]{2,1,0:T(2,128)(2,1)} %copy-done), calls=%async_computation.1 | async-start | bytes 4325376 | tf_op jit(solution)/shard_map/all_to_all | solution.py:281
  167.7 58.8 %all-gather.9.cloned.1.call-start = ((), (), s32[]{:S(2)}) async-start(), calls=%async_computation.4 | async-start | bytes 3932160 | tf_op jit(solution)/shard_map/all_gather | solution.py:377
  170.2 15.6 %collective-permute-start.1 = (bf16[512,512]{1,0:T(8,128)(2,1)S(1)}, bf16[512,512]{1,0:T(8,128)(2,1)S(1)}, u32[]{:S(2)}, u32[]{:S(2)}) collective-permute-start(bf16[512,512]{1,0:T(8,128)(2,1)S(1)} %get-tuple-element.25), channel_id=1, source_target_pairs={{0,1},{1,2},{2,3},{3,0},{4,5},{5,6},{6,7},{7,4},{8,9},{9,10},{10,1... | collective-permute-start | bytes 1572872 | tf_op jit(solution)/shard_map/ppermute | solution.py:385
  173.3 28.3 %collective-permute-start.2 = (bf16[512,512]{1,0:T(8,128)(2,1)S(1)}, bf16[512,512]{1,0:T(8,128)(2,1)S(1)}, u32[]{:S(2)}, u32[]{:S(2)}) collective-permute-start(bf16[512,512]{1,0:T(8,128)(2,1)S(1)} %get-tuple-element.24), channel_id=1, source_target_pairs={{0,2},{1,3},{2,0},{3,1},{4,6},{5,7},{6,4},{7,5},{8,10},{9,11},{10,... | collective-permute-start | bytes 1572872 | tf_op jit(solution)/shard_map/ppermute | solution.py:385
  177.7 30.3 %collective-permute-start.3 = (bf16[512,512]{1,0:T(8,128)(2,1)S(1)}, bf16[512,512]{1,0:T(8,128)(2,1)S(1)}, u32[]{:S(2)}, u32[]{:S(2)}) collective-permute-start(bf16[512,512]{1,0:T(8,128)(2,1)S(1)} %get-tuple-element.23), channel_id=1, source_target_pairs={{0,3},{1,0},{2,1},{3,2},{4,7},{5,4},{6,5},{7,6},{8,11},{9,8},{10,9... | collective-permute-start | bytes 1572872 | tf_op jit(solution)/shard_map/ppermute | solution.py:385
  201.6 0.8 copy-start.4
  207.9 0.8 copy-start.6
  226.6 1.9 copy-start.3
  228.5 1.0 copy-start.5
  229.5 1.0 copy-start.7
  233.1 36.6 %copy-start.1 = (s32[2,1024]{1,0:T(2,128)S(1)}, s32[2,1024]{1,0:T(2,128)}, u32[]{:S(2)}) copy-start(s32[2,1024]{1,0:T(2,128)} %get-tuple-element.13.target_ref) | copy-start | bytes 24580
  233.1 36.6 %copy-start.2 = (f32[1,1024]{1,0:T(1,128)S(1)}, f32[1,1024]{1,0:T(1,128)}, u32[]{:S(2)}) copy-start(f32[1,1024]{1,0:T(1,128)} %get-tuple-element.14.scaled_ref) | copy-start | bytes 12292
  233.1 27.5 %collective-permute-start.4 = (bf16[512,768]{1,0:T(8,128)(2,1)S(1)}, bf16[512,768]{1,0:T(8,128)(2,1)S(1)}, u32[]{:S(2)}, u32[]{:S(2)}) collective-permute-start(bf16[512,768]{1,0:T(8,128)(2,1)S(1)} %get-tuple-element.22), channel_id=1, source_target_pairs={{0,256},{4,260},{8,264},{12,268},{16,272},{20,276},{24,280},{28,28... | collective-permute-start | bytes 2359304 | tf_op jit(solution)/shard_map/ppermute | solution.py:401
Sparse Core Ops, SparseCore 0:
  36.3 48.1 all-gather.4
  86.5 47.4 all-gather.6
  171.3 55.2 all-gather.8

commit v6 on v5

--- a/solution.py
+++ b/solution.py
@@ -10,7 +10,7 @@
 VMEM_BYTES = 40 * 1024 * 1024
 VMEM_MOST = 56 * 1024 * 1024
 TAIL = 128
-PIECES = 4
+PIECES = 2
 VMEM_SERVE = 47 * 1024 * 1024
 
 
@@ -126,10 +126,11 @@
         store.start()
         stores.append(store)
 
-    loads[4].wait()
     for i, target in enumerate(targets):
         hit = iota((rows, n_routes), 0) == target
         pick = mm(hit.astype(BF), owner, 1, 1).astype(BF)
+        if i == 0:
+            loads[4].wait()
         start = i * part
         moved = mm(pick, tokens[...]).astype(BF)
         out[:, :, start : start + width] = moved.reshape(rows // 2, 2, width)
@@ -204,8 +205,8 @@
         one.start()
         stores.append(one)
 
-    tail = None
-    for i, weights in enumerate((own, other)):
+    parts = []
+    for i in range(2):
         start = i * part
         span = pl.ds(i * rows, rows)
         tokens = recv[:, :, start : start + width].reshape(rows, width)
@@ -213,6 +214,11 @@
             all_rows[c, i * rows : (i + 1) * rows, :] = tokens[:, c * chunk : (c + 1) * chunk]
         store(all_rows.at[:, span, :], rows_hbm.at[pl.ds(0, chunks), span, :])
         scaled = recv[:, :, start + width : start + part].reshape(rows, hidden)
+        parts.append((tokens, scaled))
+    tail = None
+    for i, weights in enumerate((own, other)):
+        span = pl.ds(i * rows, rows)
+        tokens, scaled = parts[i]
         grad, router, result = serve(tokens, scaled, weights, ready[i])
         all_grads[i * rows : (i + 1) * rows, :] = grad
         store(all_grads.at[span], grad_hbm.at[span])

time: 279 us -> 279 us (level)
  no operation moved by 1% of the time
where the time goes in v6:
time: 279 us
  waiting for transfers between devices  185 us (66%)
  starting transfers between devices  51 us (18%)
  Pallas kernels  18.7 us (7%)
  between operations  13.9 us (5%)
  local copies, waits for them, and re-layouts  9.33 us (3%)
    all_gather x1, waiting for transfers between devices, local(): partner_weights = lax.all_gather(partner_shard, 'dp', axis=1, tiled=True)[0]  49.6 us
    all_to_all x2, starting transfers between devices, exchange(): lax.all_to_all(value, 'expert', split_axis=0, concat_axis=0, tiled=True)  29.9 us
    ppermute x3, waiting for transfers between devices, local(): lax.ppermute(piece, 'dp', [(q, (q + k) % replicas) for q in range(replica...  26.4 us
    all_to_all x2, waiting for transfers between devices, exchange(): lax.all_to_all(value, 'expert', split_axis=0, concat_axis=0, tiled=True)  22.8 us
    ppermute x1, waiting for transfers between devices, local(): moved_shard = lax.ppermute(far_shard, 'expert', swap)  22.4 us
    all_gather x1, waiting for transfers between devices, local(): own_weights = lax.all_gather(gate_up, 'dp', axis=1, tiled=True)[0]  22.3 us
    ppermute x1, waiting for transfers between devices, local(): partner_shard = lax.ppermute(gate_up, 'expert', swap)  22.1 us
    pallas_call x4, Pallas kernels, call(): pl.pallas_call(kernel, out_shape=[jax.ShapeDtypeStruct(s, d) for s, d in...  18.7 us
  transfers between devices with their start and end apart: 10, of which 10 were waited for; matrix products, arithmetic and copies ran while one was open for 1% of the time, Pallas kernels for 1%

profile of v6, /device:TPU:1, one launch (start us, length us, event | category | flops | bytes accessed | tf_op | source)
XLA Modules:
  0.0 278.7 jit_solution(3494913759461028988)
XLA Ops:
  7.2 5.4 %shard_map.94 = (bf16[128,2,4864]{2,1,0:T(2,128)(2,1)}, s32[2,1024]{1,0:T(2,128)}, f32[1,1024]{1,0:T(1,128)}) custom-call(s32[8,128]{1,0:T(8,128)} %bitcast.24, f32[8,128]{1,0:T(8,128)} %bitcast.25, s32[1,128]{1,0:T(1,128)} %bitcast.27, s32[1,128]{1,0:T(1,128)} %bitcast.28, bf16[128,2048]{1,0:T(8,128)(2,1)} %tokens_hbm.1, bf16[1024,384]{1,0:T(8,128)(2,1)} %bitcast.23), custom_call_target="tpu_custom_call" | custom-call | flops 671088640 | bytes 4194304 | tf_op jit(solution)/shard_map/pallas_call | solution.py:275
  12.6 0.0 copy-start.8
  12.6 0.0 copy-start.9
  12.6 20.7 %all-to-all-start = ((bf16[128,2,4864]{2,1,0:T(2,128)(2,1)}), bf16[128,2,4864]{2,1,0:T(2,128)(2,1)S(1)}, u32[]{:S(2)}, u32[]{:S(2)}) async-start(bf16[128,2,4864]{2,1,0:T(2,128)(2,1)} %get-tuple-element.15), calls=%async_computation | async-start | bytes 4980736 | tf_op jit(solution)/shard_map/all_to_all | solution.py:287
  33.3 0.0 all-gather.5.cloned.1.call-start
  33.3 0.7 all-gather.5.cloned.1.call-update
  34.0 0.0 all-gather.7.cloned.1.call-start
  34.1 0.0 copy-done.8
  34.1 5.1 %collective-permute-start = (bf16[1,512,768]{2,1,0:T(8,128)(2,1)S(1)}, bf16[1,512,768]{2,1,0:T(8,128)(2,1)}, u32[]{:S(2)}, u32[]{:S(2)}) collective-permute-start(bf16[1,512,768]{2,1,0:T(8,128)(2,1)S(1)} %copy-done.8), channel_id=1, source_target_pairs={{0,256},{4,260},{8,264},{12,268},{16,272},{20,276},{24,280},{28,28... | collective-permute-start | bytes 2359304 | tf_op jit(solution)/shard_map/ppermute | solution.py:370
  39.2 22.1 %collective-permute-done = bf16[1,512,768]{2,1,0:T(8,128)(2,1)} collective-permute-done((bf16[1,512,768]{2,1,0:T(8,128)(2,1)S(1)}, bf16[1,512,768]{2,1,0:T(8,128)(2,1)}, u32[]{:S(2)}, u32[]{:S(2)}) %collective-permute-start) | collective-permute-done | bytes 786464 | tf_op jit(solution)/shard_map/ppermute | solution.py:370
  61.4 0.0 all-gather.7.cloned.1.call-update
  61.4 0.0 copy-done.9
  61.4 0.7 dynamic_slice.16.cap_ref
  62.1 22.3 %all-gather.5.cloned.1.call-done = bf16[1,2048,768]{2,1,0:T(8,128)(2,1)} async-done(((bf16[1,512,768]{2,1,0:T(8,128)(2,1)}), bf16[1,2048,768]{2,1,0:T(8,128)(2,1)}) %all-gather.5.cloned.1.call-update) | async-done | bytes 3145744 | tf_op jit(solution)/shard_map/all_gather | solution.py:369
  84.4 49.6 %all-gather.7.cloned.1.call-done = bf16[1,2048,768]{2,1,0:T(8,128)(2,1)} async-done(((bf16[1,512,768]{2,1,0:T(8,128)(2,1)}), bf16[1,2048,768]{2,1,0:T(8,128)(2,1)}) %all-gather.7.cloned.1.call-update) | async-done | bytes 3145744 | tf_op jit(solution)/shard_map/all_gather | solution.py:371
  134.0 14.8 %all-to-all-done.recv = bf16[128,2,4864]{2,1,0:T(2,128)(2,1)S(1)} async-done(((bf16[128,2,4864]{2,1,0:T(2,128)(2,1)}), bf16[128,2,4864]{2,1,0:T(2,128)(2,1)S(1)}, u32[]{:S(2)}, u32[]{:S(2)}) %all-to-all-start) | async-done | bytes 2490400 | tf_op jit(solution)/shard_map/all_to_all | solution.py:287
  148.8 8.7 %shard_map.95 = (bf16[128,2,4224]{2,1,0:T(2,128)(2,1)S(1)}, bf16[8,512,512]{2,1,0:T(8,128)(2,1)}, bf16[512,768]{1,0:T(8,128)(2,1)}) custom-call(s32[1]{0:T(128)} %dynamic_slice.16.cap_ref, bf16[128,2,4864]{2,1,0:T(2,128)(2,1)S(1)} %all-to-all-done.recv, bf16[2048,768]{1,0:T(8,128)(2,1)} %bitcast.21, bf16[2048,768]{1,0:T(8,128)(2,1)} %bitcast.22), custom_call_target="tpu_custom_call" | custom-call | flops 3221225472 | bytes 12582912 | tf_op jit(solution)/shard_map/pallas_call | solution.py:275
  157.5 0.0 copy-start
  157.5 1.4 copy-done
  158.9 9.2 %all-to-all-start.1 = ((bf16[128,2,4224]{2,1,0:T(2,128)(2,1)}), bf16[128,2,4224]{2,1,0:T(2,128)(2,1)S(1)}, u32[]{:S(2)}, u32[]{:S(2)}) async-start(bf16[128,2,4224]{2,1,0:T(2,128)(2,1)} %copy-done), calls=%async_computation.1 | async-start | bytes 4325376 | tf_op jit(solution)/shard_map/all_to_all | solution.py:287
  168.1 0.2 all-gather.9.cloned.1.call-start
  168.3 0.5 all-gather.9.cloned.1.call-update
  168.9 1.7 dynamic-slice_bitcast_fusion
  170.5 3.1 %collective-permute-start.1 = (bf16[512,512]{1,0:T(8,128)(2,1)S(1)}, bf16[512,512]{1,0:T(8,128)(2,1)S(1)}, u32[]{:S(2)}, u32[]{:S(2)}) collective-permute-start(bf16[512,512]{1,0:T(8,128)(2,1)S(1)} %get-tuple-element.25), channel_id=1, source_target_pairs={{0,1},{1,2},{2,3},{3,0},{4,5},{5,6},{6,7},{7,4},{8,9},{9,10},{10,1... | collective-permute-start | bytes 1572872 | tf_op jit(solution)/shard_map/ppermute | solution.py:391
  173.7 4.4 %collective-permute-start.2 = (bf16[512,512]{1,0:T(8,128)(2,1)S(1)}, bf16[512,512]{1,0:T(8,128)(2,1)S(1)}, u32[]{:S(2)}, u32[]{:S(2)}) collective-permute-start(bf16[512,512]{1,0:T(8,128)(2,1)S(1)} %get-tuple-element.24), channel_id=1, source_target_pairs={{0,2},{1,3},{2,0},{3,1},{4,6},{5,7},{6,4},{7,5},{8,10},{9,11},{10,... | collective-permute-start | bytes 1572872 | tf_op jit(solution)/shard_map/ppermute | solution.py:391
  178.0 3.1 %collective-permute-start.3 = (bf16[512,512]{1,0:T(8,128)(2,1)S(1)}, bf16[512,512]{1,0:T(8,128)(2,1)S(1)}, u32[]{:S(2)}, u32[]{:S(2)}) collective-permute-start(bf16[512,512]{1,0:T(8,128)(2,1)S(1)} %get-tuple-element.23), channel_id=1, source_target_pairs={{0,3},{1,0},{2,1},{3,2},{4,7},{5,4},{6,5},{7,6},{8,11},{9,8},{10,9... | collective-permute-start | bytes 1572872 | tf_op jit(solution)/shard_map/ppermute | solution.py:391
  181.1 5.1 %collective-permute-done.1.rows_1 = bf16[512,512]{1,0:T(8,128)(2,1)S(1)} collective-permute-done((bf16[512,512]{1,0:T(8,128)(2,1)S(1)}, bf16[512,512]{1,0:T(8,128)(2,1)S(1)}, u32[]{:S(2)}, u32[]{:S(2)}) %collective-permute-start.1) | collective-permute-done | bytes 524320 | tf_op jit(solution)/shard_map/ppermute | solution.py:391
  186.2 15.8 %collective-permute-done.2.rows_2 = bf16[512,512]{1,0:T(8,128)(2,1)S(1)} collective-permute-done((bf16[512,512]{1,0:T(8,128)(2,1)S(1)}, bf16[512,512]{1,0:T(8,128)(2,1)S(1)}, u32[]{:S(2)}, u32[]{:S(2)}) %collective-permute-start.2) | collective-permute-done | bytes 524320 | tf_op jit(solution)/shard_map/ppermute | solution.py:391
  202.0 0.0 copy-start.4
  202.0 0.8 copy-done.4
  202.8 5.5 %collective-permute-done.3.rows_3 = bf16[512,512]{1,0:T(8,128)(2,1)S(1)} collective-permute-done((bf16[512,512]{1,0:T(8,128)(2,1)S(1)}, bf16[512,512]{1,0:T(8,128)(2,1)S(1)}, u32[]{:S(2)}, u32[]{:S(2)}) %collective-permute-start.3) | collective-permute-done | bytes 524320 | tf_op jit(solution)/shard_map/ppermute | solution.py:391
  208.3 0.0 copy-start.6
  208.3 0.8 copy-done.6
  209.1 17.8 %all-gather.9.cloned.1.call-done = bf16[2048,768]{1,0:T(8,128)(2,1)} async-done(((bf16[512,768]{1,0:T(8,128)(2,1)}), bf16[2048,768]{1,0:T(8,128)(2,1)}) %all-gather.9.cloned.1.call-update) | async-done | bytes 3145744 | tf_op jit(solution)/shard_map/all_gather | solution.py:383
  227.0 0.0 copy-start.3
  227.0 1.9 copy-done.3
  228.8 1.0 copy-done.5
  229.9 1.0 copy-done.7
  230.9 2.5 shard_map.97
  233.5 0.0 copy-start.1
  233.5 0.0 copy-start.2
  233.5 5.1 %collective-permute-start.4 = (bf16[512,768]{1,0:T(8,128)(2,1)S(1)}, bf16[512,768]{1,0:T(8,128)(2,1)S(1)}, u32[]{:S(2)}, u32[]{:S(2)}) collective-permute-start(bf16[512,768]{1,0:T(8,128)(2,1)S(1)} %get-tuple-element.22), channel_id=1, source_target_pairs={{0,256},{4,260},{8,264},{12,268},{16,272},{20,276},{24,280},{28,28... | collective-permute-start | bytes 2359304 | tf_op jit(solution)/shard_map/ppermute | solution.py:407
  238.6 22.4 %collective-permute-done.4 = bf16[512,768]{1,0:T(8,128)(2,1)S(1)} collective-permute-done((bf16[512,768]{1,0:T(8,128)(2,1)S(1)}, bf16[512,768]{1,0:T(8,128)(2,1)S(1)}, u32[]{:S(2)}, u32[]{:S(2)}) %collective-permute-start.4) | collective-permute-done | bytes 786464 | tf_op jit(solution)/shard_map/ppermute | solution.py:407
  261.1 1.0 fusion
  262.1 7.9 %all-to-all-done.1.back = bf16[128,2,4224]{2,1,0:T(2,128)(2,1)S(1)} async-done(((bf16[128,2,4224]{2,1,0:T(2,128)(2,1)}), bf16[128,2,4224]{2,1,0:T(2,128)(2,1)S(1)}, u32[]{:S(2)}, u32[]{:S(2)}) %all-to-all-start.1) | async-done | bytes 2162720 | tf_op jit(solution)/shard_map/all_to_all | solution.py:287
  270.1 0.0 copy-done.1
  270.1 0.0 copy-done.2
  270.1 2.2 shard_map.96
  (2 shorter events, 0.0 us)
Async XLA Ops:
  12.6 21.5 %copy-start.8 = (bf16[1,512,768]{2,1,0:T(8,128)(2,1)S(1)}, bf16[1,512,768]{2,1,0:T(8,128)(2,1)}, u32[]{:S(2)}) copy-start(bf16[1,512,768]{2,1,0:T(8,128)(2,1)} %param.13) | copy-start | bytes 2359300
  12.6 48.8 %copy-start.9 = (s32[128]{0:T(128)S(1)}, s32[128]{0:T(128)}, u32[]{:S(2)}) copy-start(s32[128]{0:T(128)} %param.12) | copy-start | bytes 1540
  12.6 136.2 %all-to-all-start = ((bf16[128,2,4864]{2,1,0:T(2,128)(2,1)}), bf16[128,2,4864]{2,1,0:T(2,128)(2,1)S(1)}, u32[]{:S(2)}, u32[]{:S(2)}) async-start(bf16[128,2,4864]{2,1,0:T(2,128)(2,1)} %get-tuple-element.15), calls=%async_computation | async-start | bytes 4980736 | tf_op jit(solution)/shard_map/all_to_all | solution.py:287
  33.3 51.1 %all-gather.5.cloned.1.call-start = ((), (), s32[]{:S(2)}) async-start(), calls=%async_computation.2 | async-start | bytes 3932160 | tf_op jit(solution)/shard_map/all_gather | solution.py:369
  34.0 100.0 %all-gather.7.cloned.1.call-start = ((), (), s32[]{:S(2)}) async-start(), calls=%async_computation.3 | async-start | bytes 3932160 | tf_op jit(solution)/shard_map/all_gather | solution.py:371
  34.1 27.3 %collective-permute-start = (bf16[1,512,768]{2,1,0:T(8,128)(2,1)S(1)}, bf16[1,512,768]{2,1,0:T(8,128)(2,1)}, u32[]{:S(2)}, u32[]{:S(2)}) collective-permute-start(bf16[1,512,768]{2,1,0:T(8,128)(2,1)S(1)} %copy-done.8), channel_id=1, source_target_pairs={{0,256},{4,260},{8,264},{12,268},{16,272},{20,276},{24,280},{28,28... | collective-permute-start | bytes 2359304 | tf_op jit(solution)/shard_map/ppermute | solution.py:370
  157.5 1.4 copy-start
  158.9 111.1 %all-to-all-start.1 = ((bf16[128,2,4224]{2,1,0:T(2,128)(2,1)}), bf16[128,2,4224]{2,1,0:T(2,128)(2,1)S(1)}, u32[]{:S(2)}, u32[]{:S(2)}) async-start(bf16[128,2,4224]{2,1,0:T(2,128)(2,1)} %copy-done), calls=%async_computation.1 | async-start | bytes 4325376 | tf_op jit(solution)/shard_map/all_to_all | solution.py:287
  168.1 58.8 %all-gather.9.cloned.1.call-start = ((), (), s32[]{:S(2)}) async-start(), calls=%async_computation.4 | async-start | bytes 3932160 | tf_op jit(solution)/shard_map/all_gather | solution.py:383
  170.5 15.6 %collective-permute-start.1 = (bf16[512,512]{1,0:T(8,128)(2,1)S(1)}, bf16[512,512]{1,0:T(8,128)(2,1)S(1)}, u32[]{:S(2)}, u32[]{:S(2)}) collective-permute-start(bf16[512,512]{1,0:T(8,128)(2,1)S(1)} %get-tuple-element.25), channel_id=1, source_target_pairs={{0,1},{1,2},{2,3},{3,0},{4,5},{5,6},{6,7},{7,4},{8,9},{9,10},{10,1... | collective-permute-start | bytes 1572872 | tf_op jit(solution)/shard_map/ppermute | solution.py:391
  173.7 28.3 %collective-permute-start.2 = (bf16[512,512]{1,0:T(8,128)(2,1)S(1)}, bf16[512,512]{1,0:T(8,128)(2,1)S(1)}, u32[]{:S(2)}, u32[]{:S(2)}) collective-permute-start(bf16[512,512]{1,0:T(8,128)(2,1)S(1)} %get-tuple-element.24), channel_id=1, source_target_pairs={{0,2},{1,3},{2,0},{3,1},{4,6},{5,7},{6,4},{7,5},{8,10},{9,11},{10,... | collective-permute-start | bytes 1572872 | tf_op jit(solution)/shard_map/ppermute | solution.py:391
  178.0 30.3 %collective-permute-start.3 = (bf16[512,512]{1,0:T(8,128)(2,1)S(1)}, bf16[512,512]{1,0:T(8,128)(2,1)S(1)}, u32[]{:S(2)}, u32[]{:S(2)}) collective-permute-start(bf16[512,512]{1,0:T(8,128)(2,1)S(1)} %get-tuple-element.23), channel_id=1, source_target_pairs={{0,3},{1,0},{2,1},{3,2},{4,7},{5,4},{6,5},{7,6},{8,11},{9,8},{10,9... | collective-permute-start | bytes 1572872 | tf_op jit(solution)/shard_map/ppermute | solution.py:391
  202.0 0.8 copy-start.4
  208.3 0.8 copy-start.6
  227.0 1.9 copy-start.3
  228.8 1.0 copy-start.5
  229.9 1.0 copy-start.7
  233.5 36.6 %copy-start.1 = (s32[2,1024]{1,0:T(2,128)S(1)}, s32[2,1024]{1,0:T(2,128)}, u32[]{:S(2)}) copy-start(s32[2,1024]{1,0:T(2,128)} %get-tuple-element.13.target_ref) | copy-start | bytes 24580
  233.5 36.6 %copy-start.2 = (f32[1,1024]{1,0:T(1,128)S(1)}, f32[1,1024]{1,0:T(1,128)}, u32[]{:S(2)}) copy-start(f32[1,1024]{1,0:T(1,128)} %get-tuple-element.14.scaled_ref) | copy-start | bytes 12292
  233.5 27.6 %collective-permute-start.4 = (bf16[512,768]{1,0:T(8,128)(2,1)S(1)}, bf16[512,768]{1,0:T(8,128)(2,1)S(1)}, u32[]{:S(2)}, u32[]{:S(2)}) collective-permute-start(bf16[512,768]{1,0:T(8,128)(2,1)S(1)} %get-tuple-element.22), channel_id=1, source_target_pairs={{0,256},{4,260},{8,264},{12,268},{16,272},{20,276},{24,280},{28,28... | collective-permute-start | bytes 2359304 | tf_op jit(solution)/shard_map/ppermute | solution.py:407
Sparse Core Ops, SparseCore 0:
  36.2 48.1 all-gather.4
  86.5 47.4 all-gather.6
  171.6 55.2 all-gather.8
